TPU v7x, 256 devices: a whole 4x4x8 slice. The times are simulated.
256 devices in a mesh: loop: 64 (over z, x, y_lo), grp: 4 (over y_hi, core).
Axes of the slice: x: 4, y: 4 (y_hi: 2, y_lo: 2; y = y_hi * 2 + y_lo), z: 8, core: 2. Of those that a mesh axis runs over, the one named last changes fastest.
Arguments:
- slab: bfloat16 [2048, 524288], P(None, ('loop', 'grp')), may hold values from -64 to 64
- sketch: bfloat16 [524288, 256], P(('loop', 'grp')), may hold values from -0.0078125 to 0.0078125
Outputs:
- basis: float32 [2048, 512], P(('loop', 'grp'))
All inputs are finite; a program needn't handle non-finite values.
Results may differ from a plain program's by a relative error of at most 0.0003.
Values may be sent and summed in bfloat16 or wider, within the bound.
No kernel may reach another device: no remote copies, remote signals or barrier semaphores. Data moves between devices by JAX's collectives and lax.ppermute only.
A program may use at most 64 MiB of HBM per device.

v0:
```python
import functools
import math

import jax
import jax.numpy as jnp
from jax import lax
from jax.experimental import pallas as pl
from jax.experimental.pallas import tpu as pltpu
from jax.sharding import Mesh, PartitionSpec as P

ROWS = 2048
B = 128
HI = lax.Precision.HIGHEST
PLANE = ("x", "yl", "yh")
DEVICE = ("z", "x", "yl", "yh", "c")


def wide(row):
    return jnp.broadcast_to(row, (8, B))


def nt(a, b):
    return lax.dot_general(a, b, (((1,), (1,)), ((), ())), precision=HI, preferred_element_type=jnp.float32)


def eliminate(w_ref, c_ref, s):
    r0 = 8 * s
    top = w_ref[r0 : r0 + 8, :B]
    for j in range(8):
        c_ref[8 * j : 8 * j + 8, :] = wide(top[:, r0 + j : r0 + j + 1])
    schur = {(i, j): wide(c_ref[8 * j + i : 8 * j + i + 1, :]) for j in range(8) for i in range(j, 8)}
    rows = [[wide(w_ref[r0 + i : r0 + i + 1, t * B : (t + 1) * B]) for t in range(2)] for i in range(8)]
    ratio, inverse = {}, []
    for j in range(8):
        inv = 1.0 / schur[j, j]
        inverse.append(inv)
        for i in range(j + 1, 8):
            ratio[i, j] = schur[i, j] * inv
        for i in range(j + 1, 8):
            for k in range(j + 1, i + 1):
                schur[i, k] = schur[i, k] - ratio[i, j] * schur[k, j]
        for i in range(j + 1, 8):
            for t in range(2):
                rows[i][t] = rows[i][t] - ratio[i, j] * rows[j][t]
    for i in range(8):
        w_ref[r0 + i : r0 + i + 1, B:] = (rows[i][1] * lax.rsqrt(schur[i, i]))[:1]
    if s == B // 8 - 1:
        return
    g = [None] * 8
    for i in reversed(range(8)):
        g[i] = [rows[i][t] * inverse[i] for t in range(2)]
        for k in range(i + 1, 8):
            for t in range(2):
                g[i][t] = g[i][t] - ratio[k, i] * g[k][t]
    for v in range(s + 1, B // 8):
        at = slice(8 * v, 8 * v + 8)
        left, right = w_ref[at, :B], w_ref[at, B:]
        new_left, new_right = left, right
        for j in range(8):
            col = wide(left[:, r0 + j : r0 + j + 1])
            new_left = new_left - col * g[j][0]
            new_right = new_right - col * g[j][1]
        w_ref[at, :B] = new_left
        w_ref[at, B:] = new_right


def kernel(scale, gram_ref, rows_ref, out_ref, a_ref, w_ref, c_ref):
    n = gram_ref.shape[0]
    a_ref[:n] = gram_ref[...]
    a_ref[n:] = rows_ref[...]
    eye = (lax.broadcasted_iota(jnp.int32, (B, B), 0) == lax.broadcasted_iota(jnp.int32, (B, B), 1)).astype(jnp.float32)
    for k in range(n // B):
        lo, hi = k * B, (k + 1) * B
        w_ref[:, :B] = a_ref[lo:hi, lo:hi]
        w_ref[:, B:] = eye
        for s in range(B // 8):
            eliminate(w_ref, c_ref, s)
        inv = w_ref[:, B:]
        panel = nt(a_ref[hi:, lo:hi], inv)
        out_ref[:, lo:hi] = panel[n - hi :] * scale
        if hi < n:
            a_ref[hi:, hi:] = a_ref[hi:, hi:] - nt(panel, panel[: n - hi])


def solve_rows(gram, rows, scale):
    n = gram.shape[0]
    return pl.pallas_call(
        functools.partial(kernel, scale),
        out_shape=jax.ShapeDtypeStruct(rows.shape, jnp.float32),
        in_specs=[pl.BlockSpec(memory_space=pltpu.VMEM)] * 2,
        out_specs=pl.BlockSpec(memory_space=pltpu.VMEM),
        scratch_shapes=[
            pltpu.VMEM((n + 8, n), jnp.float32),
            pltpu.VMEM((B, 2 * B), jnp.float32),
            pltpu.VMEM((64, B), jnp.float32),
        ],
        compiler_params=pltpu.CompilerParams(vmem_limit_bytes=16 * 1024 * 1024),
    )(gram, rows)


def shifted(block):
    loop = ("z", "x", "yl")
    size = lax.axis_size(loop)
    return lax.ppermute(block, loop, [(i, (i + 1) % size) for i in range(size)])


def core_swap(block):
    return lax.ppermute(block, "c", [(0, 1), (1, 0)])


def spread(block, axes):
    return lax.all_to_all(block, axes, 0, 0, tiled=True)


def gathered(block, axes):
    size = lax.axis_size(axes)
    return spread(jnp.broadcast_to(block[None], (size,) + block.shape), axes)


def scattered_sum(partial):
    depth, width = lax.axis_size("z"), lax.axis_size(PLANE)
    rows, cols = partial.shape
    unit = rows // (depth * width * 2)
    pieces = partial.reshape(depth, width, 2, unit, cols)
    core = lax.axis_index("c")
    away = lax.dynamic_index_in_dim(pieces, 1 - core, 2, keepdims=False)
    kept = lax.dynamic_index_in_dim(pieces, core, 2, keepdims=False)
    chip = (kept + core_swap(away)).transpose(1, 0, 2, 3)
    plane = spread(chip, PLANE).sum(axis=0)
    return spread(plane, "z").sum(axis=0)


def full_gram(own_rows):
    wide = PLANE + ("c",)
    count = lax.axis_size(wide)
    rows = gathered(own_rows, wide).reshape(-1, own_rows.shape[1])
    cols = rows.shape[1]
    unit = cols // count
    mine = lax.dynamic_slice_in_dim(rows, lax.axis_index(wide) * unit, unit, 1)
    part = lax.dot_general(
        mine,
        rows,
        (((0,), (0,)), ((), ())),
        precision=HI,
        preferred_element_type=jnp.float32,
    )
    part = gathered(part, "z").sum(axis=0)
    return gathered(part, wide).reshape(cols, cols)


def body(slab, sketch):
    moved = shifted(sketch)
    own_part = jnp.dot(slab, sketch, preferred_element_type=jnp.float32)
    far_part = jnp.dot(slab, moved, preferred_element_type=jnp.float32)
    own_rows = scattered_sum(jnp.concatenate((own_part, far_part), axis=1))
    gram = full_gram(own_rows)
    return solve_rows(gram, own_rows, math.sqrt(ROWS))


def solution(mesh):
    fine = Mesh(mesh.devices.reshape(8, 4, 2, 2, 2), DEVICE)
    return jax.shard_map(
        body,
        mesh=fine,
        in_specs=(P(None, DEVICE), P(DEVICE, None)),
        out_specs=P(DEVICE, None),
        check_vma=False,
    )
```

profile of v0, /device:TPU:1, one launch (start us, length us, event | category | flops | bytes accessed | tf_op | source)
XLA Modules:
  0.0 174.1 jit_solution(6295505519846619395)
XLA Ops:
  0.0 2.1 %collective-permute-start = (bf16[2048,256]{1,0:T(8,128)(2,1)}, bf16[2048,256]{1,0:T(8,128)(2,1)S(1)}, u32[]{:S(2)}, u32[]{:S(2)}) collective-permute-start(bf16[2048,256]{1,0:T(8,128)(2,1)} %param.3), channel_id=1, source_target_pairs={{0,4},{4,8},{8,12},{12,16},{16,20},{20,24},{24,28},{28,32},{32,36}... | collective-permute-start | bytes 3145736 | tf_op jit(solution)/shard_map/ppermute | solution.py:104
  2.1 0.0 copy-start
  2.1 6.1 %fusion.4 = f32[2048,256]{0,1:T(8,128)S(1)} fusion(bf16[2048,2048]{1,0:T(8,128)(2,1)} %param.2, bf16[2048,256]{1,0:T(8,128)(2,1)} %param.3), kind=kOutput, calls=%fused_computation.7 | convolution fusion | flops 2147483648 | bytes 11534336 | tf_op jit(solution)/shard_map/dot_general | solution.py:153
  8.3 24.4 %collective-permute-done = bf16[2048,256]{1,0:T(8,128)(2,1)S(1)} collective-permute-done((bf16[2048,256]{1,0:T(8,128)(2,1)}, bf16[2048,256]{1,0:T(8,128)(2,1)S(1)}, u32[]{:S(2)}, u32[]{:S(2)}) %collective-permute-start) | collective-permute-done | bytes 1048608 | tf_op jit(solution)/shard_map/ppermute | solution.py:104
  32.7 0.0 copy-done
  32.7 2.4 %fusion.5 = f32[2048,256]{0,1:T(8,128)S(1)} fusion(bf16[2048,2048]{1,0:T(8,128)(2,1)S(1)} %copy-done, bf16[2048,256]{1,0:T(8,128)(2,1)S(1)} %collective-permute-done), kind=kOutput, calls=%fused_computation.8 | convolution fusion | flops 2147483648 | bytes 11534336 | tf_op jit(solution)/shard_map/dot_general | solution.py:154
  35.1 2.2 %pad_maximum_fusion = f32[2048,512]{0,1:T(8,128)} fusion(f32[2048,256]{0,1:T(8,128)S(1)} %fusion.5, f32[2048,256]{0,1:T(8,128)S(1)} %fusion.4), kind=kLoop, calls=%fused_computation | loop fusion | flops 1048576 | bytes 8388608 | tf_op jit(solution)/shard_map/concatenate | solution.py:155
  37.3 5.3 %copy.7 = f32[2048,512]{1,0:T(8,128)} copy(f32[2048,512]{0,1:T(8,128)} %pad_maximum_fusion) | data formatting | bytes 8388608 | tf_op jit(solution)/shard_map/concatenate | solution.py:155
  42.7 3.1 %dynamic-slice_bitcast_fusion = f32[8,16,8,512]{3,2,1,0:T(8,128)} fusion(f32[8,16,2,8,512]{4,3,2,1,0:T(8,128)} %bitcast.17, s32[]{:T(128)S(6)} %select_n.11), kind=kLoop, calls=%fused_computation.3 | loop fusion | bytes 4194308 | tf_op jit(solution)/shard_map/jit(dynamic_index_in_dim)/squeeze | solution.py:126
  45.8 1.2 collective-permute-start.1
  47.0 4.0 %collective-permute-done.1 = f32[8,16,8,512]{3,2,1,0:T(8,128)S(1)} collective-permute-done((f32[8,16,8,512]{3,2,1,0:T(8,128)}, f32[8,16,8,512]{3,2,1,0:T(8,128)S(1)}, u32[]{:S(2)}, u32[]{:S(2)}) %collective-permute-start.1) | collective-permute-done | bytes 2097184 | tf_op jit(solution)/shard_map/ppermute | solution.py:108
  51.0 2.1 %fusion = f32[16,8,8,512]{3,2,0,1:T(8,128)S(1)} fusion(f32[8,16,8,512]{3,2,1,0:T(8,128)S(1)} %collective-permute-done.1, f32[8,16,2,8,512]{4,3,2,1,0:T(8,128)} %bitcast.18, s32[]{:T(128)S(6)} %select_n.10), kind=kLoop, calls=%fused_computation.2 | loop fusion | flops 524288 | bytes 6291460 | tf_op jit(solution)/shard_map/transpose | solution.py:128
  53.1 0.2 copy.8
  53.3 31.4 %all_to_all.25 = f32[16,8,8,512]{3,2,1,0:T(8,128)S(1)} all-to-all(f32[16,8,8,512]{3,2,1,0:T(8,128)S(1)} %copy.8), channel_id=1, replica_groups=mesh['z'=8,'x'=4,'yl'=2,'yh'=2,'c'=2] {'x','yl','yh'}, dimensions={0} | all-to-all | bytes 4194304 | tf_op jit(solution)/shard_map/all_to_all | solution.py:112
  84.7 0.2 reduce_sum.27
  84.9 13.1 %all_to_all.26 = f32[8,8,512]{2,1,0:T(8,128)S(1)} all-to-all(f32[8,8,512]{2,1,0:T(8,128)S(1)} %reduce_sum.27), channel_id=1, replica_groups=mesh['z'=8,'x'=4,'yl'=2,'yh'=2,'c'=2] {'z'}, dimensions={0} | all-to-all | bytes 262144 | tf_op jit(solution)/shard_map/all_to_all | solution.py:112
  98.0 0.8 broadcast_in_dim.6
  98.9 7.0 %all-to-all-start.2 = ((f32[32,8,512]{2,1,0:T(8,128)}), f32[32,8,512]{2,1,0:T(8,128)S(1)}, u32[]{:S(2)}, u32[]{:S(2)}) async-start(f32[32,8,512]{2,1,0:T(8,128)} %broadcast_in_dim.6), calls=%async_computation.2 | async-start | bytes 1048576 | tf_op jit(solution)/shard_map/all_to_all | solution.py:112
  105.9 11.3 %all-to-all-done.2 = f32[32,8,512]{2,1,0:T(8,128)S(1)} async-done(((f32[32,8,512]{2,1,0:T(8,128)}), f32[32,8,512]{2,1,0:T(8,128)S(1)}, u32[]{:S(2)}, u32[]{:S(2)}) %all-to-all-start.2) | async-done | bytes 524320 | tf_op jit(solution)/shard_map/all_to_all | solution.py:112
  117.1 0.4 fusion.1
  117.6 14.8 %all_to_all.27 = f32[8,16,512]{2,1,0:T(8,128)S(1)} all-to-all(f32[8,16,512]{2,1,0:T(8,128)S(1)} %broadcast_in_dim.7), channel_id=1, replica_groups=mesh['z'=8,'x'=4,'yl'=2,'yh'=2,'c'=2] {'z'}, dimensions={0} | all-to-all | bytes 524288 | tf_op jit(solution)/shard_map/all_to_all | solution.py:112
  132.4 0.1 broadcast_in_dim.8
  132.5 20.7 %all_to_all.28 = f32[32,16,512]{2,1,0:T(8,128)S(1)} all-to-all(f32[32,16,512]{2,1,0:T(8,128)S(1)} %broadcast_in_dim.8), channel_id=1, replica_groups=mesh['z'=8,'x'=4,'yl'=2,'yh'=2,'c'=2] {'x','yl','yh','c'}, dimensions={0} | all-to-all | bytes 2097152 | tf_op jit(solution)/shard_map/all_to_all | solution.py:112
  153.2 20.9 %shard_map.28 = f32[8,512]{1,0:T(8,128)} custom-call(f32[512,512]{1,0:T(8,128)S(1)} %bitcast.16, f32[8,512]{1,0:T(8,128)S(1)} %reduce_sum.28.rows_ref), custom_call_target="tpu_custom_call" | custom-call | tf_op jit(solution)/shard_map/pallas_call | solution.py:87
  (3 shorter events, 0.1 us)
Async XLA Ops:
  0.0 32.7 %collective-permute-start = (bf16[2048,256]{1,0:T(8,128)(2,1)}, bf16[2048,256]{1,0:T(8,128)(2,1)S(1)}, u32[]{:S(2)}, u32[]{:S(2)}) collective-permute-start(bf16[2048,256]{1,0:T(8,128)(2,1)} %param.3), channel_id=1, source_target_pairs={{0,4},{4,8},{8,12},{12,16},{16,20},{20,24},{24,28},{28,32},{32,36}... | collective-permute-start | bytes 3145736 | tf_op jit(solution)/shard_map/ppermute | solution.py:104
  2.1 30.6 %copy-start = (bf16[2048,2048]{1,0:T(8,128)(2,1)S(1)}, bf16[2048,2048]{1,0:T(8,128)(2,1)}, u32[]{:S(2)}) copy-start(bf16[2048,2048]{1,0:T(8,128)(2,1)} %param.2) | copy-start | bytes 25165828
  45.8 5.2 %collective-permute-start.1 = (f32[8,16,8,512]{3,2,1,0:T(8,128)}, f32[8,16,8,512]{3,2,1,0:T(8,128)S(1)}, u32[]{:S(2)}, u32[]{:S(2)}) collective-permute-start(f32[8,16,8,512]{3,2,1,0:T(8,128)} %dynamic-slice_bitcast_fusion), channel_id=1, source_target_pairs={{0,1},{1,0},{2,3},{3,2},{4,5},{5,4},{6,7},{7,6},{8,9},{9,8},{10,11... | collective-permute-start | bytes 6291464 | tf_op jit(solution)/shard_map/ppermute | solution.py:108
  98.9 18.3 %all-to-all-start.2 = ((f32[32,8,512]{2,1,0:T(8,128)}), f32[32,8,512]{2,1,0:T(8,128)S(1)}, u32[]{:S(2)}, u32[]{:S(2)}) async-start(f32[32,8,512]{2,1,0:T(8,128)} %broadcast_in_dim.6), calls=%async_computation.2 | async-start | bytes 1048576 | tf_op jit(solution)/shard_map/all_to_all | solution.py:112
where the time goes:
time: 175 us; the launch traced here: 174 us
  blocking collectives  80 us (46%)
  waiting for transfers between devices  39.7 us (23%)
  Pallas kernels  20.9 us (12%)
  starting transfers between devices  10.3 us (6%)
  local copies, waits for them, and re-layouts  9.64 us (6%)
  matrix products  8.93 us (5%)
  other arithmetic  4.5 us (3%)
    all_to_all x4, blocking collectives, spread(): return lax.all_to_all(block, axes, 0, 0, tiled=True)  80 us
    ppermute x1, waiting for transfers between devices, shifted(): return lax.ppermute(block, loop, [(i, (i + 1) % size) for i in range(size)])  24.4 us
    pallas_call x1, Pallas kernels, solve_rows(): pl.pallas_call(functools.partial(kernel, scale), out_shape=jax.ShapeDtype...  20.9 us
    all_to_all x1, waiting for transfers between devices, spread(): return lax.all_to_all(block, axes, 0, 0, tiled=True)  11.3 us
    all_to_all x1, starting transfers between devices, spread(): return lax.all_to_all(block, axes, 0, 0, tiled=True)  6.99 us
    dot_general x1, matrix products, body(): own_part = jnp.dot(slab, sketch, preferred_element_type=jnp.float32)  6.13 us
    concatenate x1, local copies, waits for them, and re-layouts, body(): own_rows = scattered_sum(jnp.concatenate((own_part, far_part), axis=1))  5.35 us
    ppermute x1, waiting for transfers between devices, core_swap(): return lax.ppermute(block, 'c', [(0, 1), (1, 0)])  4 us
  transfers between devices with their start and end apart: 3, of which 3 were waited for; matrix products, arithmetic and copies ran while one was open for 4% of the time, Pallas kernels for 0%

commit v1 on v0

--- a/solution.py
+++ b/solution.py
@@ -117,17 +117,36 @@
     return spread(jnp.broadcast_to(block[None], (size,) + block.shape), axes)
 
 
-def scattered_sum(partial):
+def product_kernel(slab_ref, sketch_ref, after_ref, kept_ref, away_ref):
+    width, unit, cols = kept_ref.shape[0], kept_ref.shape[2], kept_ref.shape[3]
+    total = jnp.dot(slab_ref[...], sketch_ref[...], preferred_element_type=jnp.float32)
+    pairs = total.reshape(width, 2, unit, cols)
+    first = lax.axis_index("c") == 0
+    kept_ref[:, 0] = jnp.where(first, pairs[:, 0], pairs[:, 1])
+    away_ref[:, 0] = jnp.where(first, pairs[:, 1], pairs[:, 0])
+
+
+def product(slab, sketch, after):
     depth, width = lax.axis_size("z"), lax.axis_size(PLANE)
-    rows, cols = partial.shape
+    rows, inner = slab.shape
+    cols = sketch.shape[1]
     unit = rows // (depth * width * 2)
-    pieces = partial.reshape(depth, width, 2, unit, cols)
-    core = lax.axis_index("c")
-    away = lax.dynamic_index_in_dim(pieces, 1 - core, 2, keepdims=False)
-    kept = lax.dynamic_index_in_dim(pieces, core, 2, keepdims=False)
-    chip = (kept + core_swap(away)).transpose(1, 0, 2, 3)
-    plane = spread(chip, PLANE).sum(axis=0)
-    return spread(plane, "z").sum(axis=0)
+    half = pl.BlockSpec((width, 1, unit, cols), lambda z: (0, z, 0, 0))
+    shape = jax.ShapeDtypeStruct((width, depth, unit, cols), jnp.float32)
+    return pl.pallas_call(
+        product_kernel,
+        grid=(depth,),
+        in_specs=[pl.BlockSpec((rows // depth, inner), lambda z: (z, 0)), pl.BlockSpec((inner, cols), lambda z: (0, 0)), pl.BlockSpec(memory_space=pl.ANY)],
+        out_specs=[half, half],
+        out_shape=[shape, shape],
+        cost_estimate=pl.CostEstimate(flops=2 * rows * inner * cols, bytes_accessed=2 * rows * inner, transcendentals=0),
+        compiler_params=pltpu.CompilerParams(vmem_limit_bytes=16 * 1024 * 1024),
+    )(slab, sketch, after)
+
+
+def plane_sum(slab, sketch, after):
+    kept, away = product(slab, sketch, after)
+    return spread(kept + core_swap(away), PLANE).sum(axis=0)
 
 
 def full_gram(own_rows):
@@ -150,9 +169,10 @@
 
 def body(slab, sketch):
     moved = shifted(sketch)
-    own_part = jnp.dot(slab, sketch, preferred_element_type=jnp.float32)
-    far_part = jnp.dot(slab, moved, preferred_element_type=jnp.float32)
-    own_rows = scattered_sum(jnp.concatenate((own_part, far_part), axis=1))
+    own = plane_sum(slab, sketch, sketch)
+    far = plane_sum(slab, moved, own)
+    plane = jnp.concatenate((own, far), axis=2)
+    own_rows = spread(plane, "z").sum(axis=0)
     gram = full_gram(own_rows)
     return solve_rows(gram, own_rows, math.sqrt(ROWS))
 

time: 175 us -> 179 us (1.023)
  blocking collectives: 80 us -> 112 us
  waiting for transfers between devices: 39.7 us -> 15.8 us
  Pallas kernels: 20.9 us -> 29.7 us
  matrix products: 8.93 us -> 0.43 us
  other arithmetic: 4.5 us -> 0.44 us
  local copies, waits for them, and re-layouts: 9.64 us -> 7.75 us
    all_to_all x4 -> x5, blocking collectives: 80 us -> 112 us  [spread(): return lax.all_to_all(block, axes, 0, 0, tiled=True)]
    ppermute x1, waiting for transfers between devices: 24.4 us -> 0.01 us  [shifted(): return lax.ppermute(block, loop, [(i, (i + 1) % size) for i in range(size)])]
    pallas_call x0 -> x2, Pallas kernels: none -> 8.74 us  [product(): pl.pallas_call(product_kernel, grid=(depth,), in_specs=[pl.BlockSpec((row...]
    dot_general x2 -> x0, matrix products: 8.5 us -> none  [the longest x1 6.13 us: body(): own_part = jnp.dot(slab, sketch, preferred_element_type=jnp.float32)]
    unnamed x2 -> x4, local copies, waits for them, and re-layouts: 0.01 us -> 6.76 us
    concatenate x1 -> x0, local copies, waits for them, and re-layouts: 5.35 us -> none  [body(): own_rows = scattered_sum(jnp.concatenate((own_part, far_part), axis=1))]
    ppermute x1 -> x2, starting transfers between devices: 1.23 us -> 4.62 us  [core_swap(): return lax.ppermute(block, 'c', [(0, 1), (1, 0)])]
    squeeze x1 -> x0, local copies, waits for them, and re-layouts: 3.09 us -> none  [scattered_sum(): away = lax.dynamic_index_in_dim(pieces, 1 - core, 2, keepdims=False)]
  transfers between devices with their start and end apart: 3 -> 4, of which waited for: 3 -> 3; matrix products, arithmetic and copies ran while one was open for 4% -> 0% of each run, Pallas kernels for 0% -> 0%
where the time goes in v1:
time: 179 us; the launch traced here: 178 us
  blocking collectives  112 us (63%)
  Pallas kernels  29.7 us (17%)
  waiting for transfers between devices  15.8 us (9%)
  starting transfers between devices  11.6 us (6%)
  local copies, waits for them, and re-layouts  7.75 us (4%)
    all_to_all x5, blocking collectives, spread(): return lax.all_to_all(block, axes, 0, 0, tiled=True)  112 us
    pallas_call x1, Pallas kernels, solve_rows(): pl.pallas_call(functools.partial(kernel, scale), out_shape=jax.ShapeDtype...  20.9 us
    all_to_all x1, waiting for transfers between devices, spread(): return lax.all_to_all(block, axes, 0, 0, tiled=True)  11.3 us
    pallas_call x2, Pallas kernels, product(): pl.pallas_call(product_kernel, grid=(depth,), in_specs=[pl.BlockSpec((row...  8.74 us
    all_to_all x1, starting transfers between devices, spread(): return lax.all_to_all(block, axes, 0, 0, tiled=True)  6.98 us
    unnamed x4, local copies, waits for them, and re-layouts  6.76 us
    ppermute x2, starting transfers between devices, core_swap(): return lax.ppermute(block, 'c', [(0, 1), (1, 0)])  4.62 us
    ppermute x2, waiting for transfers between devices, core_swap(): return lax.ppermute(block, 'c', [(0, 1), (1, 0)])  4.57 us
  transfers between devices with their start and end apart: 4, of which 3 were waited for; matrix products, arithmetic and copies ran while one was open for 0% of the time, Pallas kernels for 0%

profile of v1, /device:TPU:1, one launch (start us, length us, event | category | flops | bytes accessed | tf_op | source)
XLA Modules:
  0.0 178.1 jit_solution(8870464993942683540)
XLA Ops:
  0.0 3.4 %copy-done = bf16[2048,2048]{1,0:T(8,128)(2,1)S(1)} copy-done((bf16[2048,2048]{1,0:T(8,128)(2,1)S(1)}, bf16[2048,2048]{1,0:T(8,128)(2,1)}, u32[]{:S(2)}) %copy-start) | copy-done | bytes 8388632
  3.4 5.0 %shard_map.28 = (f32[16,8,8,256]{3,2,1,0:T(8,128)S(1)}, f32[16,8,8,256]{3,2,1,0:T(8,128)S(1)}) custom-call(bf16[2048,2048]{1,0:T(8,128)(2,1)S(1)} %copy-done, bf16[2048,256]{1,0:T(8,128)(2,1)} %after_ref.1, bf16[2048,256]{1,0:T(8,128)(2,1)} %after_ref.1), custom_call_target="tpu_custom_call" | custom-call | flops 2147483648 | bytes 8388608 | tf_op jit(solution)/shard_map/pallas_call | solution.py:136
  8.4 3.3 %collective-permute-start = (f32[16,8,8,256]{3,2,1,0:T(8,128)S(1)}, f32[16,8,8,256]{3,2,1,0:T(8,128)S(1)}, u32[]{:S(2)}, u32[]{:S(2)}) collective-permute-start(f32[16,8,8,256]{3,2,1,0:T(8,128)S(1)} %get-tuple-element.10), channel_id=1, source_target_pairs={{0,1},{1,0},{2,3},{3,2},{4,5},{5,4},{6,7},{7,6},{8,9},{9,8},{10,11... | collective-permute-start | bytes 3145736 | tf_op jit(solution)/shard_map/ppermute | solution.py:108
  11.7 2.3 %collective-permute-done = f32[16,8,8,256]{3,2,1,0:T(8,128)S(1)} collective-permute-done((f32[16,8,8,256]{3,2,1,0:T(8,128)S(1)}, f32[16,8,8,256]{3,2,1,0:T(8,128)S(1)}, u32[]{:S(2)}, u32[]{:S(2)}) %collective-permute-start) | collective-permute-done | bytes 1048608 | tf_op jit(solution)/shard_map/ppermute | solution.py:108
  14.0 0.1 add.18
  14.1 41.2 %all_to_all.30 = f32[16,8,8,256]{3,2,1,0:T(8,128)S(1)} all-to-all(f32[16,8,8,256]{3,2,1,0:T(8,128)S(1)} %add.18), channel_id=1, replica_groups=mesh['z'=8,'x'=4,'yl'=2,'yh'=2,'c'=2] {'x','yl','yh'}, dimensions={0} | all-to-all | bytes 2097152 | tf_op jit(solution)/shard_map/all_to_all | solution.py:112
  55.4 0.1 reduce_sum.36.after_ref
  55.4 0.0 copy-start.1
  55.5 3.4 %copy-done.1 = bf16[2048,2048]{1,0:T(8,128)(2,1)S(1)} copy-done((bf16[2048,2048]{1,0:T(8,128)(2,1)S(1)}, bf16[2048,2048]{1,0:T(8,128)(2,1)}, u32[]{:S(2)}) %copy-start.1) | copy-done | bytes 8388632
  58.8 3.7 %shard_map.29 = (f32[16,8,8,256]{3,2,1,0:T(8,128)S(1)}, f32[16,8,8,256]{3,2,1,0:T(8,128)S(1)}) custom-call(bf16[2048,2048]{1,0:T(8,128)(2,1)S(1)} %copy-done.1, bf16[2048,256]{1,0:T(8,128)(2,1)S(1)} %collective-permute-done.1.sketch_ref, f32[8,8,256]{2,1,0:T(8,128)S(1)} %reduce_sum.36.after_ref), custom_call_target="tpu_custom_call" | custom-call | flops 2147483648 | bytes 8388608 | tf_op jit(solution)/shard_map/pallas_call | solution.py:136
  62.6 1.3 collective-permute-start.2
  63.9 2.3 %collective-permute-done.2 = f32[16,8,8,256]{3,2,1,0:T(8,128)S(1)} collective-permute-done((f32[16,8,8,256]{3,2,1,0:T(8,128)S(1)}, f32[16,8,8,256]{3,2,1,0:T(8,128)S(1)}, u32[]{:S(2)}, u32[]{:S(2)}) %collective-permute-start.2) | collective-permute-done | bytes 1048608 | tf_op jit(solution)/shard_map/ppermute | solution.py:108
  66.2 0.1 add.19
  66.3 19.7 %all_to_all.31 = f32[16,8,8,256]{3,2,1,0:T(8,128)S(1)} all-to-all(f32[16,8,8,256]{3,2,1,0:T(8,128)S(1)} %add.19), channel_id=1, replica_groups=mesh['z'=8,'x'=4,'yl'=2,'yh'=2,'c'=2] {'x','yl','yh'}, dimensions={0} | all-to-all | bytes 2097152 | tf_op jit(solution)/shard_map/all_to_all | solution.py:112
  86.0 0.1 reduce_sum.37
  86.1 15.9 %all_to_all.32 = f32[8,8,512]{2,1,0:T(8,128)S(1)} all-to-all(f32[8,8,512]{2,1,0:T(8,128)S(1)} %pad_maximum_fusion), channel_id=1, replica_groups=mesh['z'=8,'x'=4,'yl'=2,'yh'=2,'c'=2] {'z'}, dimensions={0} | all-to-all | bytes 262144 | tf_op jit(solution)/shard_map/all_to_all | solution.py:112
  102.0 0.8 broadcast_in_dim.6
  102.9 7.0 %all-to-all-start.3 = ((f32[32,8,512]{2,1,0:T(8,128)}), f32[32,8,512]{2,1,0:T(8,128)S(1)}, u32[]{:S(2)}, u32[]{:S(2)}) async-start(f32[32,8,512]{2,1,0:T(8,128)} %broadcast_in_dim.6), calls=%async_computation.3 | async-start | bytes 1048576 | tf_op jit(solution)/shard_map/all_to_all | solution.py:112
  109.9 11.3 %all-to-all-done.3 = f32[32,8,512]{2,1,0:T(8,128)S(1)} async-done(((f32[32,8,512]{2,1,0:T(8,128)}), f32[32,8,512]{2,1,0:T(8,128)S(1)}, u32[]{:S(2)}, u32[]{:S(2)}) %all-to-all-start.3) | async-done | bytes 524320 | tf_op jit(solution)/shard_map/all_to_all | solution.py:112
  121.1 0.4 fusion
  121.6 14.8 %all_to_all.33 = f32[8,16,512]{2,1,0:T(8,128)S(1)} all-to-all(f32[8,16,512]{2,1,0:T(8,128)S(1)} %broadcast_in_dim.7), channel_id=1, replica_groups=mesh['z'=8,'x'=4,'yl'=2,'yh'=2,'c'=2] {'z'}, dimensions={0} | all-to-all | bytes 524288 | tf_op jit(solution)/shard_map/all_to_all | solution.py:112
  136.4 0.1 broadcast_in_dim.8
  136.5 20.7 %all_to_all.34 = f32[32,16,512]{2,1,0:T(8,128)S(1)} all-to-all(f32[32,16,512]{2,1,0:T(8,128)S(1)} %broadcast_in_dim.8), channel_id=1, replica_groups=mesh['z'=8,'x'=4,'yl'=2,'yh'=2,'c'=2] {'x','yl','yh','c'}, dimensions={0} | all-to-all | bytes 2097152 | tf_op jit(solution)/shard_map/all_to_all | solution.py:112
  157.2 20.9 %shard_map.30 = f32[8,512]{1,0:T(8,128)} custom-call(f32[512,512]{1,0:T(8,128)S(1)} %bitcast.3, f32[8,512]{1,0:T(8,128)S(1)} %reduce_sum.38.rows_ref), custom_call_target="tpu_custom_call" | custom-call | tf_op jit(solution)/shard_map/pallas_call | solution.py:87
  (7 shorter events, 0.1 us)
Async XLA Ops:
  0.0 3.4 %copy-start = (bf16[2048,2048]{1,0:T(8,128)(2,1)S(1)}, bf16[2048,2048]{1,0:T(8,128)(2,1)}, u32[]{:S(2)}) copy-start(bf16[2048,2048]{1,0:T(8,128)(2,1)} %slab_ref.3) | copy-start | bytes 25165828
  8.4 5.6 %collective-permute-start = (f32[16,8,8,256]{3,2,1,0:T(8,128)S(1)}, f32[16,8,8,256]{3,2,1,0:T(8,128)S(1)}, u32[]{:S(2)}, u32[]{:S(2)}) collective-permute-start(f32[16,8,8,256]{3,2,1,0:T(8,128)S(1)} %get-tuple-element.10), channel_id=1, source_target_pairs={{0,1},{1,0},{2,3},{3,2},{4,5},{5,4},{6,7},{7,6},{8,9},{9,8},{10,11... | collective-permute-start | bytes 3145736 | tf_op jit(solution)/shard_map/ppermute | solution.py:108
  11.7 43.7 %collective-permute-start.1 = (bf16[2048,256]{1,0:T(8,128)(2,1)}, bf16[2048,256]{1,0:T(8,128)(2,1)S(1)}, u32[]{:S(2)}, u32[]{:S(2)}) collective-permute-start(bf16[2048,256]{1,0:T(8,128)(2,1)} %after_ref.1), channel_id=1, source_target_pairs={{0,4},{4,8},{8,12},{12,16},{16,20},{20,24},{24,28},{28,32},{32,36}... | collective-permute-start | bytes 3145736 | tf_op jit(solution)/shard_map/ppermute | solution.py:104
  55.4 3.4 %copy-start.1 = (bf16[2048,2048]{1,0:T(8,128)(2,1)S(1)}, bf16[2048,2048]{1,0:T(8,128)(2,1)}, u32[]{:S(2)}) copy-start(bf16[2048,2048]{1,0:T(8,128)(2,1)} %slab_ref.3) | copy-start | bytes 25165828
  62.6 3.6 %collective-permute-start.2 = (f32[16,8,8,256]{3,2,1,0:T(8,128)S(1)}, f32[16,8,8,256]{3,2,1,0:T(8,128)S(1)}, u32[]{:S(2)}, u32[]{:S(2)}) collective-permute-start(f32[16,8,8,256]{3,2,1,0:T(8,128)S(1)} %get-tuple-element.12), channel_id=1, source_target_pairs={{0,1},{1,0},{2,3},{3,2},{4,5},{5,4},{6,7},{7,6},{8,9},{9,8},{10,11... | collective-permute-start | bytes 3145736 | tf_op jit(solution)/shard_map/ppermute | solution.py:108
  102.9 18.3 %all-to-all-start.3 = ((f32[32,8,512]{2,1,0:T(8,128)}), f32[32,8,512]{2,1,0:T(8,128)S(1)}, u32[]{:S(2)}, u32[]{:S(2)}) async-start(f32[32,8,512]{2,1,0:T(8,128)} %broadcast_in_dim.6), calls=%async_computation.3 | async-start | bytes 1048576 | tf_op jit(solution)/shard_map/all_to_all | solution.py:112

commit v2 on v0

--- a/solution.py
+++ b/solution.py
@@ -117,17 +117,81 @@
     return spread(jnp.broadcast_to(block[None], (size,) + block.shape), axes)
 
 
-def scattered_sum(partial):
+def own_kernel(slab_ref, sketch_ref, kept_first, away_first, kept_rest, away_rest):
+    width, unit, cols = kept_first.shape
+    total = jnp.dot(slab_ref[...], sketch_ref[...], preferred_element_type=jnp.float32)
+    pairs = total.reshape(width, 2, unit, 2 * cols)
+    low = lax.axis_index("c") == 0
+    kept = jnp.where(low, pairs[:, 0], pairs[:, 1])
+    away = jnp.where(low, pairs[:, 1], pairs[:, 0])
+    kept_first[...], kept_rest[...] = kept[:, :, :cols], kept[:, :, cols:]
+    away_first[...], away_rest[...] = away[:, :, :cols], away[:, :, cols:]
+
+
+def far_kernel(slab_ref, sketch_ref, kept_own, away_own, after_ref, kept_ref, away_ref):
+    width, count, unit, cols = kept_ref.shape
+    total = jnp.dot(slab_ref[...], sketch_ref[...], preferred_element_type=jnp.float32)
+    pairs = total.reshape(width, 2, unit, (count - 1) * cols)
+    low = lax.axis_index("c") == 0
+    kept = jnp.where(low, pairs[:, 0], pairs[:, 1])
+    away = jnp.where(low, pairs[:, 1], pairs[:, 0])
+    kept_ref[:, 0], away_ref[:, 0] = kept_own[...], away_own[...]
+    for i in range(1, count):
+        at = slice((i - 1) * cols, i * cols)
+        kept_ref[:, i], away_ref[:, i] = kept[:, :, at], away[:, :, at]
+
+
+def products(slab, sketch):
     depth, width = lax.axis_size("z"), lax.axis_size(PLANE)
-    rows, cols = partial.shape
+    rows, inner = slab.shape
+    cols = sketch.shape[1]
     unit = rows // (depth * width * 2)
-    pieces = partial.reshape(depth, width, 2, unit, cols)
-    core = lax.axis_index("c")
-    away = lax.dynamic_index_in_dim(pieces, 1 - core, 2, keepdims=False)
-    kept = lax.dynamic_index_in_dim(pieces, core, 2, keepdims=False)
-    chip = (kept + core_swap(away)).transpose(1, 0, 2, 3)
-    plane = spread(chip, PLANE).sum(axis=0)
-    return spread(plane, "z").sum(axis=0)
+    matrices = [
+        pl.BlockSpec((rows // depth, inner), lambda z: (z, 0)),
+        pl.BlockSpec((inner, cols), lambda z: (0, 0)),
+    ]
+    params = pltpu.CompilerParams(vmem_limit_bytes=56 * 1024 * 1024)
+    first = pl.BlockSpec((None, width, unit, B), lambda z: (z, 0, 0, 0))
+    rest = pl.BlockSpec((width, None, unit, B), lambda z: (0, z, 0, 0))
+    wide_rest = pl.BlockSpec((width, None, 3, unit, B), lambda z: (0, z, 0, 0, 0))
+
+    def shape(*dims):
+        return jax.ShapeDtypeStruct(dims, jnp.float32)
+
+    def own():
+        return pl.pallas_call(
+            own_kernel,
+            grid=(depth,),
+            in_specs=matrices,
+            out_specs=[first, first, rest, rest],
+            out_shape=[shape(depth, width, unit, B)] * 2 + [shape(width, depth, unit, B)] * 2,
+            compiler_params=params,
+        )(slab, sketch)
+
+    def far(moved, kept_rest, away_rest, after):
+        return pl.pallas_call(
+            far_kernel,
+            grid=(depth,),
+            in_specs=matrices + [rest, rest, pl.BlockSpec(memory_space=pl.ANY)],
+            out_specs=[wide_rest, wide_rest],
+            out_shape=[shape(width, depth, 3, unit, B)] * 2,
+            compiler_params=params,
+        )(slab, moved, kept_rest, away_rest, after)
+
+    return own, far
+
+
+def summed_rows(slab, sketch, moved):
+    own, far = products(slab, sketch)
+    kept, away, kept_rest, away_rest = own()
+    first = spread(kept + core_swap(away), "z").sum(axis=0)
+    kept, away = far(moved, kept_rest, away_rest, first)
+    chip = kept + core_swap(away)
+    width, depth, count, unit, cols = chip.shape
+    chip = chip.reshape(width, depth * count, unit, cols)
+    plane = spread(jnp.concatenate((chip, first[:, None]), axis=1), PLANE).sum(axis=0)
+    rest = spread(plane[:-1].reshape(depth, count, unit, cols), "z").sum(axis=0)
+    return jnp.concatenate((plane[-1], rest[0], rest[1], rest[2]), axis=1)
 
 
 def full_gram(own_rows):
@@ -150,9 +214,7 @@
 
 def body(slab, sketch):
     moved = shifted(sketch)
-    own_part = jnp.dot(slab, sketch, preferred_element_type=jnp.float32)
-    far_part = jnp.dot(slab, moved, preferred_element_type=jnp.float32)
-    own_rows = scattered_sum(jnp.concatenate((own_part, far_part), axis=1))
+    own_rows = summed_rows(slab, sketch, moved)
     gram = full_gram(own_rows)
     return solve_rows(gram, own_rows, math.sqrt(ROWS))
 

time: 175 us -> 187 us (1.069)
  Pallas kernels: 20.9 us -> 39.2 us
  blocking collectives: 80 us -> 96.6 us
  waiting for transfers between devices: 39.7 us -> 27.8 us
  matrix products: 8.93 us -> 0.43 us
  local copies, waits for them, and re-layouts: 9.64 us -> 2.6 us
  starting transfers between devices: 10.3 us -> 15.7 us
    ppermute x1, waiting for transfers between devices: 24.4 us -> 3.73 us  [shifted(): return lax.ppermute(block, loop, [(i, (i + 1) % size) for i in range(size)])]
    pallas_call x0 -> x2, Pallas kernels: none -> 18.3 us  [the longest x1 9.33 us: far(): pl.pallas_call(far_kernel, grid=(depth,), in_specs=matrices + [rest, rest...]
    all_to_all x4, blocking collectives: 80 us -> 96.6 us  [spread(): return lax.all_to_all(block, axes, 0, 0, tiled=True)]
    dot_general x2 -> x0, matrix products: 8.5 us -> none  [the longest x1 6.13 us: body(): own_part = jnp.dot(slab, sketch, preferred_element_type=jnp.float32)]
    all_to_all x1 -> x2, waiting for transfers between devices: 11.3 us -> 19.1 us  [spread(): return lax.all_to_all(block, axes, 0, 0, tiled=True)]
    concatenate x1 -> x0, local copies, waits for them, and re-layouts: 5.35 us -> none  [body(): own_rows = scattered_sum(jnp.concatenate((own_part, far_part), axis=1))]
    all_to_all x1 -> x2, starting transfers between devices: 6.99 us -> 11.5 us  [spread(): return lax.all_to_all(block, axes, 0, 0, tiled=True)]
    squeeze x1 -> x2, local copies, waits for them, and re-layouts: 3.09 us -> 0.01 us  [summed_rows(): return jnp.concatenate((plane[-1], rest[0], rest[1], rest[2]), axis=1)]
  transfers between devices with their start and end apart: 3 -> 5, of which waited for: 3 -> 5; matrix products, arithmetic and copies ran while one was open for 4% -> 1% of each run, Pallas kernels for 0% -> 0%
where the time goes in v2:
time: 187 us; the launch traced here: 186 us
  blocking collectives  96.6 us (52%)
  Pallas kernels  39.2 us (21%)
  waiting for transfers between devices  27.8 us (15%)
  starting transfers between devices  15.7 us (8%)
  other arithmetic  3.68 us (2%)
  local copies, waits for them, and re-layouts  2.6 us (1%)
    all_to_all x4, blocking collectives, spread(): return lax.all_to_all(block, axes, 0, 0, tiled=True)  96.6 us
    pallas_call x1, Pallas kernels, solve_rows(): pl.pallas_call(functools.partial(kernel, scale), out_shape=jax.ShapeDtype...  20.9 us
    all_to_all x2, waiting for transfers between devices, spread(): return lax.all_to_all(block, axes, 0, 0, tiled=True)  19.1 us
    all_to_all x2, starting transfers between devices, spread(): return lax.all_to_all(block, axes, 0, 0, tiled=True)  11.5 us
    pallas_call x1, Pallas kernels, far(): pl.pallas_call(far_kernel, grid=(depth,), in_specs=matrices + [rest, rest...  9.33 us
    pallas_call x1, Pallas kernels, own(): pl.pallas_call(own_kernel, grid=(depth,), in_specs=matrices, out_specs=[f...  8.96 us
    ppermute x2, waiting for transfers between devices, core_swap(): return lax.ppermute(block, 'c', [(0, 1), (1, 0)])  4.99 us
    ppermute x2, starting transfers between devices, core_swap(): return lax.ppermute(block, 'c', [(0, 1), (1, 0)])  4.17 us
  transfers between devices with their start and end apart: 5, of which 5 were waited for; matrix products, arithmetic and copies ran while one was open for 1% of the time, Pallas kernels for 0%

profile of v2, /device:TPU:1, one launch (start us, length us, event | category | flops | bytes accessed | tf_op | source)
XLA Modules:
  0.0 186.1 jit_solution(9626615060478465682)
XLA Ops:
  0.0 9.0 %shard_map.28 = (f32[8,16,8,128]{3,2,1,0:T(8,128)}, f32[8,16,8,128]{3,2,1,0:T(8,128)}, f32[16,8,8,128]{3,2,1,0:T(8,128)}, f32[16,8,8,128]{3,2,1,0:T(8,128)}) custom-call(bf16[2048,2048]{1,0:T(8,128)(2,1)} %slab_ref.3, bf16[2048,256]{1,0:T(8,128)(2,1)} %sketch_ref.1), custom_call_target="tpu_custom_call" | custom-call | tf_op jit(solution)/shard_map/pallas_call | solution.py:162
  9.0 3.2 %collective-permute-start.1 = (f32[8,16,8,128]{3,2,1,0:T(8,128)}, f32[8,16,8,128]{3,2,1,0:T(8,128)S(1)}, u32[]{:S(2)}, u32[]{:S(2)}) collective-permute-start(f32[8,16,8,128]{3,2,1,0:T(8,128)} %get-tuple-element.14), channel_id=1, source_target_pairs={{0,1},{1,0},{2,3},{3,2},{4,5},{5,4},{6,7},{7,6},{8,9},{9,8},{10,11... | collective-permute-start | bytes 1572872 | tf_op jit(solution)/shard_map/ppermute | solution.py:108
  12.2 1.7 collective-permute-done.1
  14.0 1.1 add.18
  15.1 23.2 %all_to_all.30 = f32[8,16,8,128]{3,2,1,0:T(8,128)S(1)} all-to-all(f32[8,16,8,128]{3,2,1,0:T(8,128)S(1)} %add.18), channel_id=1, replica_groups=mesh['z'=8,'x'=4,'yl'=2,'yh'=2,'c'=2] {'z'}, dimensions={0} | all-to-all | bytes 1048576 | tf_op jit(solution)/shard_map/all_to_all | solution.py:112
  38.3 0.7 reduce_sum.36.after_ref
  39.0 3.7 %collective-permute-done.sketch_ref = bf16[2048,256]{1,0:T(8,128)(2,1)S(1)} collective-permute-done((bf16[2048,256]{1,0:T(8,128)(2,1)S(1)}, bf16[2048,256]{1,0:T(8,128)(2,1)S(1)}, u32[]{:S(2)}, u32[]{:S(2)}) %collective-permute-start) | collective-permute-done | bytes 1048608 | tf_op jit(solution)/shard_map/ppermute | solution.py:104
  42.7 1.0 copy-done.1
  43.7 9.3 %shard_map.29 = (f32[16,8,3,8,128]{4,3,2,1,0:T(8,128)}, f32[16,8,3,8,128]{4,3,2,1,0:T(8,128)}) custom-call(bf16[2048,2048]{1,0:T(8,128)(2,1)} %slab_ref.3, bf16[2048,256]{1,0:T(8,128)(2,1)} %copy-done.1, f32[16,8,8,128]{3,2,1,0:T(8,128)} %get-tuple-element.11.kept_own, f32[16,8,8,128]{3,2,1,0:T(8,128)} %get-tuple-element.12.away_own, ...), custom_call_target="tpu_custom_call" | custom-call | tf_op jit(solution)/shard_map/pallas_call | solution.py:172
  53.0 0.9 collective-permute-start.2
  53.9 3.2 %collective-permute-done.2 = f32[16,8,3,8,128]{4,3,2,1,0:T(8,128)S(1)} collective-permute-done((f32[16,8,3,8,128]{4,3,2,1,0:T(8,128)}, f32[16,8,3,8,128]{4,3,2,1,0:T(8,128)S(1)}, u32[]{:S(2)}, u32[]{:S(2)}) %collective-permute-start.2) | collective-permute-done | bytes 1572896 | tf_op jit(solution)/shard_map/ppermute | solution.py:108
  57.2 1.7 add.19
  58.9 0.1 pad_maximum_fusion
  59.0 37.9 %all_to_all.31 = f32[16,25,8,128]{3,2,1,0:T(8,128)S(1)} all-to-all(f32[16,25,8,128]{3,2,1,0:T(8,128)S(1)} %pad_maximum_fusion), channel_id=1, replica_groups=mesh['z'=8,'x'=4,'yl'=2,'yh'=2,'c'=2] {'x','yl','yh'}, dimensions={0} | all-to-all | bytes 3276800 | tf_op jit(solution)/shard_map/all_to_all | solution.py:112
  97.0 0.6 slice.21
  97.6 5.0 %all-to-all-start.2 = ((f32[8,3,8,128]{3,2,1,0:T(8,128)}), f32[8,3,8,128]{3,2,1,0:T(8,128)S(1)}, u32[]{:S(2)}, u32[]{:S(2)}) async-start(f32[8,3,8,128]{3,2,1,0:T(8,128)} %bitcast.4), calls=%async_computation.2 | async-start | bytes 196608 | tf_op jit(solution)/shard_map/all_to_all | solution.py:112
  102.7 7.7 %all-to-all-done.2 = f32[8,3,8,128]{3,2,1,0:T(8,128)S(1)} async-done(((f32[8,3,8,128]{3,2,1,0:T(8,128)}), f32[8,3,8,128]{3,2,1,0:T(8,128)S(1)}, u32[]{:S(2)}, u32[]{:S(2)}) %all-to-all-start.2) | async-done | bytes 98336 | tf_op jit(solution)/shard_map/all_to_all | solution.py:112
  110.4 0.8 broadcast_in_dim.9
  111.2 6.5 %all-to-all-start.3 = ((f32[32,8,512]{2,1,0:T(8,128)}), f32[32,8,512]{2,1,0:T(8,128)S(1)}, u32[]{:S(2)}, u32[]{:S(2)}) async-start(f32[32,8,512]{2,1,0:T(8,128)} %broadcast_in_dim.9), calls=%async_computation.3 | async-start | bytes 1048576 | tf_op jit(solution)/shard_map/all_to_all | solution.py:112
  117.7 11.4 %all-to-all-done.3 = f32[32,8,512]{2,1,0:T(8,128)S(1)} async-done(((f32[32,8,512]{2,1,0:T(8,128)}), f32[32,8,512]{2,1,0:T(8,128)S(1)}, u32[]{:S(2)}, u32[]{:S(2)}) %all-to-all-start.3) | async-done | bytes 524320 | tf_op jit(solution)/shard_map/all_to_all | solution.py:112
  129.1 0.4 fusion
  129.6 14.8 %all_to_all.32 = f32[8,16,512]{2,1,0:T(8,128)S(1)} all-to-all(f32[8,16,512]{2,1,0:T(8,128)S(1)} %broadcast_in_dim.10), channel_id=1, replica_groups=mesh['z'=8,'x'=4,'yl'=2,'yh'=2,'c'=2] {'z'}, dimensions={0} | all-to-all | bytes 524288 | tf_op jit(solution)/shard_map/all_to_all | solution.py:112
  144.5 20.7 %all_to_all.33 = f32[32,16,512]{2,1,0:T(8,128)S(1)} all-to-all(f32[32,16,512]{2,1,0:T(8,128)S(1)} %broadcast_in_dim.11), channel_id=1, replica_groups=mesh['z'=8,'x'=4,'yl'=2,'yh'=2,'c'=2] {'x','yl','yh','c'}, dimensions={0} | all-to-all | bytes 2097152 | tf_op jit(solution)/shard_map/all_to_all | solution.py:112
  165.1 20.9 %shard_map.30 = f32[8,512]{1,0:T(8,128)} custom-call(f32[512,512]{1,0:T(8,128)S(1)} %bitcast.16, f32[8,512]{1,0:T(8,128)S(1)} %pad_maximum_fusion.1.rows_ref), custom_call_target="tpu_custom_call" | custom-call | tf_op jit(solution)/shard_map/pallas_call | solution.py:87
  (14 shorter events, 0.3 us)
Async XLA Ops:
  0.0 12.2 %copy-start = (bf16[2048,256]{1,0:T(8,128)(2,1)S(1)}, bf16[2048,256]{1,0:T(8,128)(2,1)}, u32[]{:S(2)}) copy-start(bf16[2048,256]{1,0:T(8,128)(2,1)} %sketch_ref.1) | copy-start | bytes 3145732
  9.0 5.0 %collective-permute-start.1 = (f32[8,16,8,128]{3,2,1,0:T(8,128)}, f32[8,16,8,128]{3,2,1,0:T(8,128)S(1)}, u32[]{:S(2)}, u32[]{:S(2)}) collective-permute-start(f32[8,16,8,128]{3,2,1,0:T(8,128)} %get-tuple-element.14), channel_id=1, source_target_pairs={{0,1},{1,0},{2,3},{3,2},{4,5},{5,4},{6,7},{7,6},{8,9},{9,8},{10,11... | collective-permute-start | bytes 1572872 | tf_op jit(solution)/shard_map/ppermute | solution.py:108
  12.2 30.5 %collective-permute-start = (bf16[2048,256]{1,0:T(8,128)(2,1)S(1)}, bf16[2048,256]{1,0:T(8,128)(2,1)S(1)}, u32[]{:S(2)}, u32[]{:S(2)}) collective-permute-start(bf16[2048,256]{1,0:T(8,128)(2,1)S(1)} %copy-done), channel_id=1, source_target_pairs={{0,4},{4,8},{8,12},{12,16},{16,20},{20,24},{24,28},{28,32},{32,36}... | collective-permute-start | bytes 3145736 | tf_op jit(solution)/shard_map/ppermute | solution.py:104
  42.7 1.0 copy-start.1
  53.0 4.2 %collective-permute-start.2 = (f32[16,8,3,8,128]{4,3,2,1,0:T(8,128)}, f32[16,8,3,8,128]{4,3,2,1,0:T(8,128)S(1)}, u32[]{:S(2)}, u32[]{:S(2)}) collective-permute-start(f32[16,8,3,8,128]{4,3,2,1,0:T(8,128)} %get-tuple-element.16), channel_id=1, source_target_pairs={{0,1},{1,0},{2,3},{3,2},{4,5},{5,4},{6,7},{7,6},{8,9},{9,8},{10,11... | collective-permute-start | bytes 4718600 | tf_op jit(solution)/shard_map/ppermute | solution.py:108
  57.2 1.7 copy-start.2
  97.6 12.7 %all-to-all-start.2 = ((f32[8,3,8,128]{3,2,1,0:T(8,128)}), f32[8,3,8,128]{3,2,1,0:T(8,128)S(1)}, u32[]{:S(2)}, u32[]{:S(2)}) async-start(f32[8,3,8,128]{3,2,1,0:T(8,128)} %bitcast.4), calls=%async_computation.2 | async-start | bytes 196608 | tf_op jit(solution)/shard_map/all_to_all | solution.py:112
  111.2 17.9 %all-to-all-start.3 = ((f32[32,8,512]{2,1,0:T(8,128)}), f32[32,8,512]{2,1,0:T(8,128)S(1)}, u32[]{:S(2)}, u32[]{:S(2)}) async-start(f32[32,8,512]{2,1,0:T(8,128)} %broadcast_in_dim.9), calls=%async_computation.3 | async-start | bytes 1048576 | tf_op jit(solution)/shard_map/all_to_all | solution.py:112

commit v3 on v1

--- a/solution.py
+++ b/solution.py
@@ -65,25 +65,29 @@
 
 
 def kernel(scale, gram_ref, rows_ref, out_ref, a_ref, w_ref, c_ref):
-    n = gram_ref.shape[0]
-    a_ref[:n] = gram_ref[...]
+    n = rows_ref.shape[1]
+    count, unit, _ = gram_ref.shape
+    for q in range(count):
+        top, low = q * unit, n - (q + 1) * unit
+        cut = (top // B + 1) * B
+        a_ref[top : top + unit, :cut] = gram_ref[q, :, :cut]
+        a_ref[low : low + unit, : (low // B + 1) * B] = gram_ref[q, :, cut:]
     a_ref[n:] = rows_ref[...]
     eye = (lax.broadcasted_iota(jnp.int32, (B, B), 0) == lax.broadcasted_iota(jnp.int32, (B, B), 1)).astype(jnp.float32)
-    for k in range(n // B):
-        lo, hi = k * B, (k + 1) * B
+    for lo in range(0, n, B):
+        hi = lo + B
         w_ref[:, :B] = a_ref[lo:hi, lo:hi]
         w_ref[:, B:] = eye
         for s in range(B // 8):
             eliminate(w_ref, c_ref, s)
-        inv = w_ref[:, B:]
-        panel = nt(a_ref[hi:, lo:hi], inv)
+        panel = nt(a_ref[hi:, lo:hi], w_ref[:, B:])
         out_ref[:, lo:hi] = panel[n - hi :] * scale
-        if hi < n:
-            a_ref[hi:, hi:] = a_ref[hi:, hi:] - nt(panel, panel[: n - hi])
+        for at in range(hi, n, B):
+            a_ref[at:, at : at + B] = a_ref[at:, at : at + B] - nt(panel[at - hi :], panel[at - hi : at - hi + B])
 
 
 def solve_rows(gram, rows, scale):
-    n = gram.shape[0]
+    n = rows.shape[1]
     return pl.pallas_call(
         functools.partial(kernel, scale),
         out_shape=jax.ShapeDtypeStruct(rows.shape, jnp.float32),
@@ -117,64 +121,65 @@
     return spread(jnp.broadcast_to(block[None], (size,) + block.shape), axes)
 
 
-def product_kernel(slab_ref, sketch_ref, after_ref, kept_ref, away_ref):
-    width, unit, cols = kept_ref.shape[0], kept_ref.shape[2], kept_ref.shape[3]
+def product_kernel(slab_ref, sketch_ref, kept_ref, away_ref):
+    width, unit, cols = kept_ref.shape
     total = jnp.dot(slab_ref[...], sketch_ref[...], preferred_element_type=jnp.float32)
     pairs = total.reshape(width, 2, unit, cols)
     first = lax.axis_index("c") == 0
-    kept_ref[:, 0] = jnp.where(first, pairs[:, 0], pairs[:, 1])
-    away_ref[:, 0] = jnp.where(first, pairs[:, 1], pairs[:, 0])
+    kept_ref[...] = jnp.where(first, pairs[:, 0], pairs[:, 1])
+    away_ref[...] = jnp.where(first, pairs[:, 1], pairs[:, 0])
 
 
-def product(slab, sketch, after):
+def product(slab, sketch):
     depth, width = lax.axis_size("z"), lax.axis_size(PLANE)
     rows, inner = slab.shape
     cols = sketch.shape[1]
     unit = rows // (depth * width * 2)
-    half = pl.BlockSpec((width, 1, unit, cols), lambda z: (0, z, 0, 0))
+    half = pl.BlockSpec((width, None, unit, cols), lambda z: (0, z, 0, 0))
     shape = jax.ShapeDtypeStruct((width, depth, unit, cols), jnp.float32)
     return pl.pallas_call(
         product_kernel,
         grid=(depth,),
-        in_specs=[pl.BlockSpec((rows // depth, inner), lambda z: (z, 0)), pl.BlockSpec((inner, cols), lambda z: (0, 0)), pl.BlockSpec(memory_space=pl.ANY)],
+        in_specs=[pl.BlockSpec((rows // depth, inner), lambda z: (z, 0)), pl.BlockSpec((inner, cols), lambda z: (0, 0))],
         out_specs=[half, half],
         out_shape=[shape, shape],
         cost_estimate=pl.CostEstimate(flops=2 * rows * inner * cols, bytes_accessed=2 * rows * inner, transcendentals=0),
         compiler_params=pltpu.CompilerParams(vmem_limit_bytes=16 * 1024 * 1024),
-    )(slab, sketch, after)
+    )(slab, sketch)
 
 
-def plane_sum(slab, sketch, after):
-    kept, away = product(slab, sketch, after)
-    return spread(kept + core_swap(away), PLANE).sum(axis=0)
+def chip_sum(slab, sketch):
+    kept, away = product(slab, sketch)
+    return kept + core_swap(away)
 
 
-def full_gram(own_rows):
-    wide = PLANE + ("c",)
-    count = lax.axis_size(wide)
-    rows = gathered(own_rows, wide).reshape(-1, own_rows.shape[1])
+def lower_gram(own_rows):
+    wide_axes = PLANE + ("c",)
+    count = lax.axis_size(wide_axes)
+    rows = gathered(own_rows, wide_axes).reshape(-1, own_rows.shape[1])
     cols = rows.shape[1]
-    unit = cols // count
-    mine = lax.dynamic_slice_in_dim(rows, lax.axis_index(wide) * unit, unit, 1)
+    unit = cols // (2 * count)
+    place = lax.axis_index(wide_axes)
+    top = lax.dynamic_slice_in_dim(rows, place * unit, unit, 1)
+    low = lax.dynamic_slice_in_dim(rows, cols - (place + 1) * unit, unit, 1)
     part = lax.dot_general(
-        mine,
+        jnp.concatenate((top, low), axis=1),
         rows,
         (((0,), (0,)), ((), ())),
         precision=HI,
         preferred_element_type=jnp.float32,
     )
-    part = gathered(part, "z").sum(axis=0)
-    return gathered(part, wide).reshape(cols, cols)
+    short = jnp.concatenate((part[:unit, :B], part[unit:]), axis=1)
+    long = jnp.concatenate((part[:unit, : 2 * B], part[unit:, : 3 * B]), axis=1)
+    packed = jnp.where(place * unit < B, short, long)
+    return gathered(gathered(packed, "z").sum(axis=0), wide_axes)
 
 
 def body(slab, sketch):
     moved = shifted(sketch)
-    own = plane_sum(slab, sketch, sketch)
-    far = plane_sum(slab, moved, own)
-    plane = jnp.concatenate((own, far), axis=2)
-    own_rows = spread(plane, "z").sum(axis=0)
-    gram = full_gram(own_rows)
-    return solve_rows(gram, own_rows, math.sqrt(ROWS))
+    chip = jnp.concatenate((chip_sum(slab, sketch), chip_sum(slab, moved)), axis=3)
+    own_rows = spread(spread(chip, PLANE).sum(axis=0), "z").sum(axis=0)
+    return solve_rows(lower_gram(own_rows), own_rows, math.sqrt(ROWS))
 
 
 def solution(mesh):

time: 179 us -> 156 us (0.87)
  blocking collectives: 112 us -> 73.9 us
  waiting for transfers between devices: 15.8 us -> 34.4 us
  local copies, waits for them, and re-layouts: 7.75 us -> 5.78 us
    all_to_all x5 -> x4, blocking collectives: 112 us -> 73.9 us  [spread(): return lax.all_to_all(block, axes, 0, 0, tiled=True)]
    ppermute x1, waiting for transfers between devices: 0.01 us -> 21 us  [shifted(): return lax.ppermute(block, loop, [(i, (i + 1) % size) for i in range(size)])]
    ppermute x2, waiting for transfers between devices: 4.57 us -> 2.13 us  [core_swap(): return lax.ppermute(block, 'c', [(0, 1), (1, 0)])]
    unnamed x4, local copies, waits for them, and re-layouts: 6.76 us -> 4.61 us
    ppermute x1, starting transfers between devices: 0.01 us -> 2.13 us  [shifted(): return lax.ppermute(block, loop, [(i, (i + 1) % size) for i in range(size)])]
    ppermute x2, starting transfers between devices: 4.62 us -> 2.52 us  [core_swap(): return lax.ppermute(block, 'c', [(0, 1), (1, 0)])]
  transfers between devices with their start and end apart: 4 -> 4, of which waited for: 3 -> 3; matrix products, arithmetic and copies ran while one was open for 0% -> 0% of each run, Pallas kernels for 0% -> 5%
where the time goes in v3:
time: 156 us; the launch traced here: 155 us
  blocking collectives  73.9 us (47%)
  waiting for transfers between devices  34.4 us (22%)
  Pallas kernels  28.2 us (18%)
  starting transfers between devices  11.6 us (7%)
  local copies, waits for them, and re-layouts  5.78 us (4%)
    all_to_all x4, blocking collectives, spread(): return lax.all_to_all(block, axes, 0, 0, tiled=True)  73.9 us
    ppermute x1, waiting for transfers between devices, shifted(): return lax.ppermute(block, loop, [(i, (i + 1) % size) for i in range(size)])  21 us
    pallas_call x1, Pallas kernels, solve_rows(): pl.pallas_call(functools.partial(kernel, scale), out_shape=jax.ShapeDtype...  20.8 us
    all_to_all x1, waiting for transfers between devices, spread(): return lax.all_to_all(block, axes, 0, 0, tiled=True)  11.3 us
    pallas_call x2, Pallas kernels, product(): pl.pallas_call(product_kernel, grid=(depth,), in_specs=[pl.BlockSpec((row...  7.48 us
    all_to_all x1, starting transfers between devices, spread(): return lax.all_to_all(block, axes, 0, 0, tiled=True)  6.99 us
    unnamed x4, local copies, waits for them, and re-layouts  4.61 us
  transfers between devices with their start and end apart: 4, of which 3 were waited for; matrix products, arithmetic and copies ran while one was open for 0% of the time, Pallas kernels for 5%

profile of v3, /device:TPU:1, one launch (start us, length us, event | category | flops | bytes accessed | tf_op | source)
XLA Modules:
  0.0 155.2 jit_solution(17737423252194770696)
XLA Ops:
  0.0 2.1 %collective-permute-start.1 = (bf16[2048,256]{1,0:T(8,128)(2,1)}, bf16[2048,256]{1,0:T(8,128)(2,1)S(1)}, u32[]{:S(2)}, u32[]{:S(2)}) collective-permute-start(bf16[2048,256]{1,0:T(8,128)(2,1)} %sketch_ref.1), channel_id=1, source_target_pairs={{0,4},{4,8},{8,12},{12,16},{16,20},{20,24},{24,28},{28,32},{32,36}... | collective-permute-start | bytes 3145736 | tf_op jit(solution)/shard_map/ppermute | solution.py:108
  2.1 3.4 %copy-done = bf16[2048,2048]{1,0:T(8,128)(2,1)S(1)} copy-done((bf16[2048,2048]{1,0:T(8,128)(2,1)S(1)}, bf16[2048,2048]{1,0:T(8,128)(2,1)}, u32[]{:S(2)}) %copy-start) | copy-done | bytes 8388632
  5.5 1.2 copy-done.1
  6.7 3.7 %shard_map.28 = (f32[16,8,8,256]{3,2,1,0:T(8,128)S(1)}, f32[16,8,8,256]{3,2,1,0:T(8,128)S(1)}) custom-call(bf16[2048,2048]{1,0:T(8,128)(2,1)S(1)} %copy-done, bf16[2048,256]{1,0:T(8,128)(2,1)S(1)} %copy-done.1), custom_call_target="tpu_custom_call" | custom-call | flops 2147483648 | bytes 8388608 | tf_op jit(solution)/shard_map/pallas_call | solution.py:140
  10.5 1.2 collective-permute-start
  11.7 21.0 %collective-permute-done.1.sketch_ref = bf16[2048,256]{1,0:T(8,128)(2,1)S(1)} collective-permute-done((bf16[2048,256]{1,0:T(8,128)(2,1)}, bf16[2048,256]{1,0:T(8,128)(2,1)S(1)}, u32[]{:S(2)}, u32[]{:S(2)}) %collective-permute-start.1) | collective-permute-done | bytes 1048608 | tf_op jit(solution)/shard_map/ppermute | solution.py:108
  32.7 3.7 %shard_map.29 = (f32[16,8,8,256]{3,2,1,0:T(8,128)S(1)}, f32[16,8,8,256]{3,2,1,0:T(8,128)S(1)}) custom-call(bf16[2048,2048]{1,0:T(8,128)(2,1)S(1)} %copy-done, bf16[2048,256]{1,0:T(8,128)(2,1)S(1)} %collective-permute-done.1.sketch_ref), custom_call_target="tpu_custom_call" | custom-call | flops 2147483648 | bytes 8388608 | tf_op jit(solution)/shard_map/pallas_call | solution.py:140
  36.5 1.3 collective-permute-start.2
  37.8 0.2 add.28
  37.9 2.1 %collective-permute-done.2 = f32[16,8,8,256]{3,2,1,0:T(8,128)S(1)} collective-permute-done((f32[16,8,8,256]{3,2,1,0:T(8,128)S(1)}, f32[16,8,8,256]{3,2,1,0:T(8,128)S(1)}, u32[]{:S(2)}, u32[]{:S(2)}) %collective-permute-start.2) | collective-permute-done | bytes 1048608 | tf_op jit(solution)/shard_map/ppermute | solution.py:112
  40.1 0.1 add.29
  40.2 0.3 pad_maximum_fusion
  40.5 31.4 %all_to_all.25 = f32[16,8,8,512]{3,2,1,0:T(8,128)S(1)} all-to-all(f32[16,8,8,512]{3,2,1,0:T(8,128)S(1)} %pad_maximum_fusion), channel_id=1, replica_groups=mesh['z'=8,'x'=4,'yl'=2,'yh'=2,'c'=2] {'x','yl','yh'}, dimensions={0} | all-to-all | bytes 4194304 | tf_op jit(solution)/shard_map/all_to_all | solution.py:116
  71.9 0.2 reduce_sum.27
  72.1 13.1 %all_to_all.26 = f32[8,8,512]{2,1,0:T(8,128)S(1)} all-to-all(f32[8,8,512]{2,1,0:T(8,128)S(1)} %reduce_sum.27), channel_id=1, replica_groups=mesh['z'=8,'x'=4,'yl'=2,'yh'=2,'c'=2] {'z'}, dimensions={0} | all-to-all | bytes 262144 | tf_op jit(solution)/shard_map/all_to_all | solution.py:116
  85.2 0.8 broadcast_in_dim.6
  86.1 7.0 %all-to-all-start.2 = ((f32[32,8,512]{2,1,0:T(8,128)}), f32[32,8,512]{2,1,0:T(8,128)S(1)}, u32[]{:S(2)}, u32[]{:S(2)}) async-start(f32[32,8,512]{2,1,0:T(8,128)} %broadcast_in_dim.6), calls=%async_computation.2 | async-start | bytes 1048576 | tf_op jit(solution)/shard_map/all_to_all | solution.py:116
  93.1 11.3 %all-to-all-done.2 = f32[32,8,512]{2,1,0:T(8,128)S(1)} async-done(((f32[32,8,512]{2,1,0:T(8,128)}), f32[32,8,512]{2,1,0:T(8,128)S(1)}, u32[]{:S(2)}, u32[]{:S(2)}) %all-to-all-start.2) | async-done | bytes 524320 | tf_op jit(solution)/shard_map/all_to_all | solution.py:116
  104.3 0.1 constant_dynamic-slice_fusion.1
  104.6 0.1 copy.6
  104.6 0.4 fusion
  105.1 11.7 %all_to_all.27 = f32[8,8,640]{2,1,0:T(8,128)S(1)} all-to-all(f32[8,8,640]{2,1,0:T(8,128)S(1)} %broadcast_in_dim.7), channel_id=1, replica_groups=mesh['z'=8,'x'=4,'yl'=2,'yh'=2,'c'=2] {'z'}, dimensions={0} | all-to-all | bytes 327680 | tf_op jit(solution)/shard_map/all_to_all | solution.py:116
  116.9 17.6 %all_to_all.28.gram_ref = f32[32,8,640]{2,1,0:T(8,128)S(1)} all-to-all(f32[32,8,640]{2,1,0:T(8,128)S(1)} %broadcast_in_dim.8), channel_id=1, replica_groups=mesh['z'=8,'x'=4,'yl'=2,'yh'=2,'c'=2] {'x','yl','yh','c'}, dimensions={0} | all-to-all | bytes 1310720 | tf_op jit(solution)/shard_map/all_to_all | solution.py:116
  134.5 20.8 %shard_map.30 = f32[8,512]{1,0:T(8,128)} custom-call(f32[32,8,640]{2,1,0:T(8,128)S(1)} %all_to_all.28.gram_ref, f32[8,512]{1,0:T(8,128)S(1)} %reduce_sum.28.rows_ref), custom_call_target="tpu_custom_call" | custom-call | tf_op jit(solution)/shard_map/pallas_call | solution.py:91
  (13 shorter events, 0.2 us)
Async XLA Ops:
  0.0 32.7 %collective-permute-start.1 = (bf16[2048,256]{1,0:T(8,128)(2,1)}, bf16[2048,256]{1,0:T(8,128)(2,1)S(1)}, u32[]{:S(2)}, u32[]{:S(2)}) collective-permute-start(bf16[2048,256]{1,0:T(8,128)(2,1)} %sketch_ref.1), channel_id=1, source_target_pairs={{0,4},{4,8},{8,12},{12,16},{16,20},{20,24},{24,28},{28,32},{32,36}... | collective-permute-start | bytes 3145736 | tf_op jit(solution)/shard_map/ppermute | solution.py:108
  2.1 3.4 %copy-start = (bf16[2048,2048]{1,0:T(8,128)(2,1)S(1)}, bf16[2048,2048]{1,0:T(8,128)(2,1)}, u32[]{:S(2)}) copy-start(bf16[2048,2048]{1,0:T(8,128)(2,1)} %slab_ref.3) | copy-start | bytes 25165828
  5.5 1.2 copy-start.1
  10.5 27.3 %collective-permute-start = (f32[16,8,8,256]{3,2,1,0:T(8,128)S(1)}, f32[16,8,8,256]{3,2,1,0:T(8,128)S(1)}, u32[]{:S(2)}, u32[]{:S(2)}) collective-permute-start(f32[16,8,8,256]{3,2,1,0:T(8,128)S(1)} %get-tuple-element.10), channel_id=1, source_target_pairs={{0,1},{1,0},{2,3},{3,2},{4,5},{5,4},{6,7},{7,6},{8,9},{9,8},{10,11... | collective-permute-start | bytes 3145736 | tf_op jit(solution)/shard_map/ppermute | solution.py:112
  36.5 3.6 %collective-permute-start.2 = (f32[16,8,8,256]{3,2,1,0:T(8,128)S(1)}, f32[16,8,8,256]{3,2,1,0:T(8,128)S(1)}, u32[]{:S(2)}, u32[]{:S(2)}) collective-permute-start(f32[16,8,8,256]{3,2,1,0:T(8,128)S(1)} %get-tuple-element.12), channel_id=1, source_target_pairs={{0,1},{1,0},{2,3},{3,2},{4,5},{5,4},{6,7},{7,6},{8,9},{9,8},{10,11... | collective-permute-start | bytes 3145736 | tf_op jit(solution)/shard_map/ppermute | solution.py:112
  86.1 18.3 %all-to-all-start.2 = ((f32[32,8,512]{2,1,0:T(8,128)}), f32[32,8,512]{2,1,0:T(8,128)S(1)}, u32[]{:S(2)}, u32[]{:S(2)}) async-start(f32[32,8,512]{2,1,0:T(8,128)} %broadcast_in_dim.6), calls=%async_computation.2 | async-start | bytes 1048576 | tf_op jit(solution)/shard_map/all_to_all | solution.py:116

commit v4 on v3

--- a/solution.py
+++ b/solution.py
@@ -23,13 +23,25 @@
     return lax.dot_general(a, b, (((1,), (1,)), ((), ())), precision=HI, preferred_element_type=jnp.float32)
 
 
-def eliminate(w_ref, c_ref, s):
+def eliminate(w_ref, c_ref, s, tasks):
     r0 = 8 * s
-    top = w_ref[r0 : r0 + 8, :B]
+    last = s == B // 8 - 1
+    lane = lax.broadcasted_iota(jnp.int32, (8, B), 1) - r0
+    here = (lane >= 0) & (lane < 8)
+    unit = jnp.where(lane == lax.broadcasted_iota(jnp.int32, (8, B), 0), 1.0, 0.0)
+    top = w_ref[r0 : r0 + 8, :]
     for j in range(8):
         c_ref[8 * j : 8 * j + 8, :] = wide(top[:, r0 + j : r0 + j + 1])
+    c_ref[64:72, :] = jnp.where(here, unit, top)
     schur = {(i, j): wide(c_ref[8 * j + i : 8 * j + i + 1, :]) for j in range(8) for i in range(j, 8)}
-    rows = [[wide(w_ref[r0 + i : r0 + i + 1, t * B : (t + 1) * B]) for t in range(2)] for i in range(8)]
+    rows = [wide(c_ref[64 + i : 65 + i, :]) for i in range(8)]
+    if not last:
+        if tasks and tasks[0][0] == s + 1:
+            tasks.pop(0)[1]()
+        after = slice(r0 + 8, r0 + 16)
+        near = w_ref[after, :]
+        cols = [wide(near[:, r0 + j : r0 + j + 1]) for j in range(8)]
+        near = jnp.where(here, 0.0, near)
     ratio, inverse = {}, []
     for j in range(8):
         inv = 1.0 / schur[j, j]
@@ -40,28 +52,34 @@
             for k in range(j + 1, i + 1):
                 schur[i, k] = schur[i, k] - ratio[i, j] * schur[k, j]
         for i in range(j + 1, 8):
-            for t in range(2):
-                rows[i][t] = rows[i][t] - ratio[i, j] * rows[j][t]
+            rows[i] = rows[i] - ratio[i, j] * rows[j]
+        if not last:
+            for k in range(j + 1, 8):
+                cols[k] = cols[k] - ratio[k, j] * cols[j]
+            near = near - cols[j] * inv * rows[j]
+    if not last:
+        w_ref[after, :] = near
     for i in range(8):
-        w_ref[r0 + i : r0 + i + 1, B:] = (rows[i][1] * lax.rsqrt(schur[i, i]))[:1]
-    if s == B // 8 - 1:
+        w_ref[r0 + i : r0 + i + 1, :] = (rows[i] * lax.rsqrt(schur[i, i]))[:1]
+    while tasks and tasks[0][0] < B:
+        tasks.pop(0)[1]()
+    if s >= B // 8 - 2:
         return
     g = [None] * 8
     for i in reversed(range(8)):
-        g[i] = [rows[i][t] * inverse[i] for t in range(2)]
+        g[i] = rows[i] * inverse[i]
         for k in range(i + 1, 8):
-            for t in range(2):
-                g[i][t] = g[i][t] - ratio[k, i] * g[k][t]
-    for v in range(s + 1, B // 8):
+            g[i] = g[i] - ratio[k, i] * g[k]
+
+    def update(v):
         at = slice(8 * v, 8 * v + 8)
-        left, right = w_ref[at, :B], w_ref[at, B:]
-        new_left, new_right = left, right
+        old = w_ref[at, :]
+        new = jnp.where(here, 0.0, old)
         for j in range(8):
-            col = wide(left[:, r0 + j : r0 + j + 1])
-            new_left = new_left - col * g[j][0]
-            new_right = new_right - col * g[j][1]
-        w_ref[at, :B] = new_left
-        w_ref[at, B:] = new_right
+            new = new - wide(old[:, r0 + j : r0 + j + 1]) * g[j]
+        w_ref[at, :] = new
+
+    tasks[:0] = [(v, functools.partial(update, v)) for v in range(s + 2, B // 8)]
 
 
 def kernel(scale, gram_ref, rows_ref, out_ref, a_ref, w_ref, c_ref):
@@ -73,17 +91,33 @@
         a_ref[top : top + unit, :cut] = gram_ref[q, :, :cut]
         a_ref[low : low + unit, : (low // B + 1) * B] = gram_ref[q, :, cut:]
     a_ref[n:] = rows_ref[...]
-    eye = (lax.broadcasted_iota(jnp.int32, (B, B), 0) == lax.broadcasted_iota(jnp.int32, (B, B), 1)).astype(jnp.float32)
+    lower = lax.broadcasted_iota(jnp.int32, (B, B), 0) >= lax.broadcasted_iota(jnp.int32, (B, B), 1)
+    tasks = []
     for lo in range(0, n, B):
         hi = lo + B
-        w_ref[:, :B] = a_ref[lo:hi, lo:hi]
-        w_ref[:, B:] = eye
+        w = w_ref.at[lo // B % 2]
+        w[...] = a_ref[lo:hi, lo:hi]
         for s in range(B // 8):
-            eliminate(w_ref, c_ref, s)
-        panel = nt(a_ref[hi:, lo:hi], w_ref[:, B:])
-        out_ref[:, lo:hi] = panel[n - hi :] * scale
-        for at in range(hi, n, B):
-            a_ref[at:, at : at + B] = a_ref[at:, at : at + B] - nt(panel[at - hi :], panel[at - hi : at - hi + B])
+            eliminate(w, c_ref.at[s % 2], s, tasks)
+        for _, task in tasks:
+            task()
+        tasks = []
+        inv = jnp.where(lower, w[...], 0.0)
+        if hi == n:
+            out_ref[:, lo:hi] = nt(a_ref[hi:, lo:hi], inv) * scale
+            return
+        near = nt(a_ref[hi : hi + B, lo:hi], inv)
+        a_ref[hi : hi + B, hi : hi + B] = a_ref[hi : hi + B, hi : hi + B] - nt(near, near)
+
+        def rest(lo, hi, inv, near):
+            far = nt(a_ref[hi + B :, lo:hi], inv)
+            out_ref[:, lo:hi] = far[-8:] * scale
+            a_ref[hi + B :, hi : hi + B] = a_ref[hi + B :, hi : hi + B] - nt(far, near)
+            for at in range(hi + B, n, B):
+                low = far[at - hi - B :]
+                a_ref[at:, at : at + B] = a_ref[at:, at : at + B] - nt(low, low[:B])
+
+        tasks.append((B, functools.partial(rest, lo, hi, inv, near)))
 
 
 def solve_rows(gram, rows, scale):
@@ -95,8 +129,8 @@
         out_specs=pl.BlockSpec(memory_space=pltpu.VMEM),
         scratch_shapes=[
             pltpu.VMEM((n + 8, n), jnp.float32),
-            pltpu.VMEM((B, 2 * B), jnp.float32),
-            pltpu.VMEM((64, B), jnp.float32),
+            pltpu.VMEM((2, B, B), jnp.float32),
+            pltpu.VMEM((2, 72, B), jnp.float32),
         ],
         compiler_params=pltpu.CompilerParams(vmem_limit_bytes=16 * 1024 * 1024),
     )(gram, rows)

time: 156 us -> 150 us (0.962)
  Pallas kernels: 28.2 us -> 22.7 us
    pallas_call x1, Pallas kernels: 20.8 us -> 15.2 us  [solve_rows(): pl.pallas_call(functools.partial(kernel, scale), out_shape=jax.ShapeDtype...]
where the time goes in v4:
time: 150 us
  blocking collectives  73.9 us (49%)
  waiting for transfers between devices  34.4 us (23%)
  Pallas kernels  22.7 us (15%)
  starting transfers between devices  11.6 us (8%)
  local copies, waits for them, and re-layouts  5.78 us (4%)
    all_to_all x4, blocking collectives, spread(): return lax.all_to_all(block, axes, 0, 0, tiled=True)  73.9 us
    ppermute x1, waiting for transfers between devices, shifted(): return lax.ppermute(block, loop, [(i, (i + 1) % size) for i in range(size)])  21 us
    pallas_call x1, Pallas kernels, solve_rows(): pl.pallas_call(functools.partial(kernel, scale), out_shape=jax.ShapeDtype...  15.2 us
    all_to_all x1, waiting for transfers between devices, spread(): return lax.all_to_all(block, axes, 0, 0, tiled=True)  11.3 us
    pallas_call x2, Pallas kernels, product(): pl.pallas_call(product_kernel, grid=(depth,), in_specs=[pl.BlockSpec((row...  7.48 us
    all_to_all x1, starting transfers between devices, spread(): return lax.all_to_all(block, axes, 0, 0, tiled=True)  6.99 us
    unnamed x4, local copies, waits for them, and re-layouts  4.61 us
  transfers between devices with their start and end apart: 4, of which 3 were waited for; matrix products, arithmetic and copies ran while one was open for 0% of the time, Pallas kernels for 5%

profile of v4, /device:TPU:1, one launch (start us, length us, event | category | flops | bytes accessed | tf_op | source)
XLA Modules:
  0.0 149.7 jit_solution(17742555343014683668)
XLA Ops:
  0.0 2.1 %collective-permute-start.1 = (bf16[2048,256]{1,0:T(8,128)(2,1)}, bf16[2048,256]{1,0:T(8,128)(2,1)S(1)}, u32[]{:S(2)}, u32[]{:S(2)}) collective-permute-start(bf16[2048,256]{1,0:T(8,128)(2,1)} %sketch_ref.1), channel_id=1, source_target_pairs={{0,4},{4,8},{8,12},{12,16},{16,20},{20,24},{24,28},{28,32},{32,36}... | collective-permute-start | bytes 3145736 | tf_op jit(solution)/shard_map/ppermute | solution.py:142
  2.1 3.4 %copy-done = bf16[2048,2048]{1,0:T(8,128)(2,1)S(1)} copy-done((bf16[2048,2048]{1,0:T(8,128)(2,1)S(1)}, bf16[2048,2048]{1,0:T(8,128)(2,1)}, u32[]{:S(2)}) %copy-start) | copy-done | bytes 8388632
  5.5 1.2 copy-done.1
  6.7 3.7 %shard_map.28 = (f32[16,8,8,256]{3,2,1,0:T(8,128)S(1)}, f32[16,8,8,256]{3,2,1,0:T(8,128)S(1)}) custom-call(bf16[2048,2048]{1,0:T(8,128)(2,1)S(1)} %copy-done, bf16[2048,256]{1,0:T(8,128)(2,1)S(1)} %copy-done.1), custom_call_target="tpu_custom_call" | custom-call | flops 2147483648 | bytes 8388608 | tf_op jit(solution)/shard_map/pallas_call | solution.py:174
  10.5 1.2 collective-permute-start
  11.7 21.0 %collective-permute-done.1.sketch_ref = bf16[2048,256]{1,0:T(8,128)(2,1)S(1)} collective-permute-done((bf16[2048,256]{1,0:T(8,128)(2,1)}, bf16[2048,256]{1,0:T(8,128)(2,1)S(1)}, u32[]{:S(2)}, u32[]{:S(2)}) %collective-permute-start.1) | collective-permute-done | bytes 1048608 | tf_op jit(solution)/shard_map/ppermute | solution.py:142
  32.7 3.7 %shard_map.29 = (f32[16,8,8,256]{3,2,1,0:T(8,128)S(1)}, f32[16,8,8,256]{3,2,1,0:T(8,128)S(1)}) custom-call(bf16[2048,2048]{1,0:T(8,128)(2,1)S(1)} %copy-done, bf16[2048,256]{1,0:T(8,128)(2,1)S(1)} %collective-permute-done.1.sketch_ref), custom_call_target="tpu_custom_call" | custom-call | flops 2147483648 | bytes 8388608 | tf_op jit(solution)/shard_map/pallas_call | solution.py:174
  36.5 1.3 collective-permute-start.2
  37.8 0.2 add.28
  37.9 2.1 %collective-permute-done.2 = f32[16,8,8,256]{3,2,1,0:T(8,128)S(1)} collective-permute-done((f32[16,8,8,256]{3,2,1,0:T(8,128)S(1)}, f32[16,8,8,256]{3,2,1,0:T(8,128)S(1)}, u32[]{:S(2)}, u32[]{:S(2)}) %collective-permute-start.2) | collective-permute-done | bytes 1048608 | tf_op jit(solution)/shard_map/ppermute | solution.py:146
  40.1 0.1 add.29
  40.2 0.3 pad_maximum_fusion
  40.5 31.4 %all_to_all.25 = f32[16,8,8,512]{3,2,1,0:T(8,128)S(1)} all-to-all(f32[16,8,8,512]{3,2,1,0:T(8,128)S(1)} %pad_maximum_fusion), channel_id=1, replica_groups=mesh['z'=8,'x'=4,'yl'=2,'yh'=2,'c'=2] {'x','yl','yh'}, dimensions={0} | all-to-all | bytes 4194304 | tf_op jit(solution)/shard_map/all_to_all | solution.py:150
  71.9 0.2 reduce_sum.27
  72.1 13.1 %all_to_all.26 = f32[8,8,512]{2,1,0:T(8,128)S(1)} all-to-all(f32[8,8,512]{2,1,0:T(8,128)S(1)} %reduce_sum.27), channel_id=1, replica_groups=mesh['z'=8,'x'=4,'yl'=2,'yh'=2,'c'=2] {'z'}, dimensions={0} | all-to-all | bytes 262144 | tf_op jit(solution)/shard_map/all_to_all | solution.py:150
  85.2 0.8 broadcast_in_dim.6
  86.1 7.0 %all-to-all-start.2 = ((f32[32,8,512]{2,1,0:T(8,128)}), f32[32,8,512]{2,1,0:T(8,128)S(1)}, u32[]{:S(2)}, u32[]{:S(2)}) async-start(f32[32,8,512]{2,1,0:T(8,128)} %broadcast_in_dim.6), calls=%async_computation.2 | async-start | bytes 1048576 | tf_op jit(solution)/shard_map/all_to_all | solution.py:150
  93.1 11.3 %all-to-all-done.2 = f32[32,8,512]{2,1,0:T(8,128)S(1)} async-done(((f32[32,8,512]{2,1,0:T(8,128)}), f32[32,8,512]{2,1,0:T(8,128)S(1)}, u32[]{:S(2)}, u32[]{:S(2)}) %all-to-all-start.2) | async-done | bytes 524320 | tf_op jit(solution)/shard_map/all_to_all | solution.py:150
  104.3 0.1 constant_dynamic-slice_fusion.1
  104.6 0.1 copy.6
  104.6 0.4 fusion
  105.1 11.7 %all_to_all.27 = f32[8,8,640]{2,1,0:T(8,128)S(1)} all-to-all(f32[8,8,640]{2,1,0:T(8,128)S(1)} %broadcast_in_dim.7), channel_id=1, replica_groups=mesh['z'=8,'x'=4,'yl'=2,'yh'=2,'c'=2] {'z'}, dimensions={0} | all-to-all | bytes 327680 | tf_op jit(solution)/shard_map/all_to_all | solution.py:150
  116.9 17.6 %all_to_all.28.gram_ref = f32[32,8,640]{2,1,0:T(8,128)S(1)} all-to-all(f32[32,8,640]{2,1,0:T(8,128)S(1)} %broadcast_in_dim.8), channel_id=1, replica_groups=mesh['z'=8,'x'=4,'yl'=2,'yh'=2,'c'=2] {'x','yl','yh','c'}, dimensions={0} | all-to-all | bytes 1310720 | tf_op jit(solution)/shard_map/all_to_all | solution.py:150
  134.5 15.2 %shard_map.30 = f32[8,512]{1,0:T(8,128)} custom-call(f32[32,8,640]{2,1,0:T(8,128)S(1)} %all_to_all.28.gram_ref, f32[8,512]{1,0:T(8,128)S(1)} %reduce_sum.28.rows_ref), custom_call_target="tpu_custom_call" | custom-call | tf_op jit(solution)/shard_map/pallas_call | solution.py:125
  (13 shorter events, 0.2 us)
Async XLA Ops:
  0.0 32.7 %collective-permute-start.1 = (bf16[2048,256]{1,0:T(8,128)(2,1)}, bf16[2048,256]{1,0:T(8,128)(2,1)S(1)}, u32[]{:S(2)}, u32[]{:S(2)}) collective-permute-start(bf16[2048,256]{1,0:T(8,128)(2,1)} %sketch_ref.1), channel_id=1, source_target_pairs={{0,4},{4,8},{8,12},{12,16},{16,20},{20,24},{24,28},{28,32},{32,36}... | collective-permute-start | bytes 3145736 | tf_op jit(solution)/shard_map/ppermute | solution.py:142
  2.1 3.4 %copy-start = (bf16[2048,2048]{1,0:T(8,128)(2,1)S(1)}, bf16[2048,2048]{1,0:T(8,128)(2,1)}, u32[]{:S(2)}) copy-start(bf16[2048,2048]{1,0:T(8,128)(2,1)} %slab_ref.3) | copy-start | bytes 25165828
  5.5 1.2 copy-start.1
  10.5 27.3 %collective-permute-start = (f32[16,8,8,256]{3,2,1,0:T(8,128)S(1)}, f32[16,8,8,256]{3,2,1,0:T(8,128)S(1)}, u32[]{:S(2)}, u32[]{:S(2)}) collective-permute-start(f32[16,8,8,256]{3,2,1,0:T(8,128)S(1)} %get-tuple-element.10), channel_id=1, source_target_pairs={{0,1},{1,0},{2,3},{3,2},{4,5},{5,4},{6,7},{7,6},{8,9},{9,8},{10,11... | collective-permute-start | bytes 3145736 | tf_op jit(solution)/shard_map/ppermute | solution.py:146
  36.5 3.6 %collective-permute-start.2 = (f32[16,8,8,256]{3,2,1,0:T(8,128)S(1)}, f32[16,8,8,256]{3,2,1,0:T(8,128)S(1)}, u32[]{:S(2)}, u32[]{:S(2)}) collective-permute-start(f32[16,8,8,256]{3,2,1,0:T(8,128)S(1)} %get-tuple-element.12), channel_id=1, source_target_pairs={{0,1},{1,0},{2,3},{3,2},{4,5},{5,4},{6,7},{7,6},{8,9},{9,8},{10,11... | collective-permute-start | bytes 3145736 | tf_op jit(solution)/shard_map/ppermute | solution.py:146
  86.1 18.3 %all-to-all-start.2 = ((f32[32,8,512]{2,1,0:T(8,128)}), f32[32,8,512]{2,1,0:T(8,128)S(1)}, u32[]{:S(2)}, u32[]{:S(2)}) async-start(f32[32,8,512]{2,1,0:T(8,128)} %broadcast_in_dim.6), calls=%async_computation.2 | async-start | bytes 1048576 | tf_op jit(solution)/shard_map/all_to_all | solution.py:150

commit v5 on v4

--- a/solution.py
+++ b/solution.py
@@ -155,42 +155,109 @@
     return spread(jnp.broadcast_to(block[None], (size,) + block.shape), axes)
 
 
-def product_kernel(slab_ref, sketch_ref, kept_ref, away_ref):
-    width, unit, cols = kept_ref.shape
+def halves(slab_ref, sketch_ref, unit):
     total = jnp.dot(slab_ref[...], sketch_ref[...], preferred_element_type=jnp.float32)
-    pairs = total.reshape(width, 2, unit, cols)
+    pairs = total.reshape(-1, 2, unit, total.shape[1])
     first = lax.axis_index("c") == 0
-    kept_ref[...] = jnp.where(first, pairs[:, 0], pairs[:, 1])
-    away_ref[...] = jnp.where(first, pairs[:, 1], pairs[:, 0])
+    return jnp.where(first, pairs[:, 0], pairs[:, 1]), jnp.where(first, pairs[:, 1], pairs[:, 0])
+
+
+def product_kernel(slab_ref, sketch_ref, *out_refs):
+    width, unit, _ = out_refs[0].shape
+    for i, value in enumerate(halves(slab_ref, sketch_ref, unit)):
+        for j in range(4):
+            side, t = divmod(j, 2)
+            out_refs[4 * i + j][...] = value[side * width : (side + 1) * width, :, t * B : (t + 1) * B]
 
 
 def product(slab, sketch):
-    depth, width = lax.axis_size("z"), lax.axis_size(PLANE)
     rows, inner = slab.shape
     cols = sketch.shape[1]
-    unit = rows // (depth * width * 2)
-    half = pl.BlockSpec((width, None, unit, cols), lambda z: (0, z, 0, 0))
-    shape = jax.ShapeDtypeStruct((width, depth, unit, cols), jnp.float32)
+    depth, width = lax.axis_size("z"), lax.axis_size(PLANE) // 2
+    unit = rows // (depth * width * 4)
     return pl.pallas_call(
         product_kernel,
         grid=(depth,),
         in_specs=[pl.BlockSpec((rows // depth, inner), lambda z: (z, 0)), pl.BlockSpec((inner, cols), lambda z: (0, 0))],
-        out_specs=[half, half],
-        out_shape=[shape, shape],
+        out_specs=[pl.BlockSpec((width, None, unit, B), lambda z: (0, z, 0, 0))] * 8,
+        out_shape=[jax.ShapeDtypeStruct((width, depth, unit, B), jnp.float32)] * 8,
         cost_estimate=pl.CostEstimate(flops=2 * rows * inner * cols, bytes_accessed=2 * rows * inner, transcendentals=0),
         compiler_params=pltpu.CompilerParams(vmem_limit_bytes=16 * 1024 * 1024),
     )(slab, sketch)
 
 
-def chip_sum(slab, sketch):
-    kept, away = product(slab, sketch)
-    return kept + core_swap(away)
-
-
-def lower_gram(own_rows):
+def own_sum(slab, sketch):
+    parts = product(slab, sketch)
+    chip = [kept + core_swap(away) for kept, away in zip(parts[:4], parts[4:])]
+    low = lax.axis_index("yh") == 0
+    kept = jnp.stack([jnp.where(low, chip[t], chip[2 + t]) for t in range(2)])
+    away = jnp.stack([jnp.where(low, chip[2 + t], chip[t]) for t in range(2)])
+    return kept, lax.ppermute(away, ("yl", "yh"), [(i, 3 - i) for i in range(4)])
+
+
+def combine_kernel(own_kept, own_got, *refs):
+    out_ref = refs[8]
+    width = out_ref.shape[0] // 2
+    for j in range(4):
+        side, t = divmod(j, 2)
+        out_ref[side * width : (side + 1) * width, :, t] = refs[j][...] + refs[4 + j][...]
+    for t in range(2):
+        out_ref[t * width : (t + 1) * width, :, 2] = own_kept[t] + own_got[t]
+
+
+def combined(own, kept, got):
+    width, depth, unit, _ = kept[0].shape
+    return pl.pallas_call(
+        combine_kernel,
+        in_specs=[pl.BlockSpec(memory_space=pltpu.VMEM)] * 10,
+        out_specs=pl.BlockSpec(memory_space=pltpu.VMEM),
+        out_shape=jax.ShapeDtypeStruct((2 * width, depth, 3, unit, B), jnp.float32),
+        compiler_params=pltpu.CompilerParams(vmem_limit_bytes=16 * 1024 * 1024),
+    )(*own, *kept, *got)
+
+
+def scattered_sum(slab, sketch, moved):
+    own = own_sum(slab, sketch)
+    parts = product(slab, moved)
+    plane = spread(combined(own, parts[:4], [core_swap(away) for away in parts[4:]]), PLANE)
+    count, depth, _, unit, _ = plane.shape
+    far = plane[:, :, :2].sum(axis=0)
+    own = plane[:, :, 2].reshape(count // 2, 2, depth, unit, B).sum(axis=0)
+    both = jnp.concatenate((far, own.transpose(1, 0, 2, 3)), axis=1)
+    return spread(both, "z").sum(axis=0)
+
+
+def assemble_kernel(parts_ref, rows_ref, own_ref):
+    count, tiles, unit, _ = parts_ref.shape
+    width = count // 2
+    for q in range(width):
+        for c in range(2):
+            at = slice((2 * q + c) * unit, (2 * q + c + 1) * unit)
+            for t in range(2):
+                source = 2 * (t * (width // 2) + q % (width // 2)) + c
+                rows_ref[at, t * B : (t + 1) * B] = parts_ref[source, 2 + q // (width // 2)]
+                rows_ref[at, (2 + t) * B : (3 + t) * B] = parts_ref[2 * q + c, t]
+    place = lax.axis_index(PLANE) * 2 + lax.axis_index("c")
+    own_ref[...] = rows_ref[pl.ds(pl.multiple_of(place * unit, unit), unit), :]
+
+
+def assembled(parts):
+    count, tiles, unit, _ = parts.shape
+    return pl.pallas_call(
+        assemble_kernel,
+        in_specs=[pl.BlockSpec(memory_space=pltpu.VMEM)],
+        out_specs=[pl.BlockSpec(memory_space=pltpu.VMEM)] * 2,
+        out_shape=[
+            jax.ShapeDtypeStruct((count * unit, tiles * B), jnp.float32),
+            jax.ShapeDtypeStruct((unit, tiles * B), jnp.float32),
+        ],
+        compiler_params=pltpu.CompilerParams(vmem_limit_bytes=16 * 1024 * 1024),
+    )(parts)
+
+
+def lower_gram(rows):
     wide_axes = PLANE + ("c",)
     count = lax.axis_size(wide_axes)
-    rows = gathered(own_rows, wide_axes).reshape(-1, own_rows.shape[1])
     cols = rows.shape[1]
     unit = cols // (2 * count)
     place = lax.axis_index(wide_axes)
@@ -211,9 +278,8 @@
 
 def body(slab, sketch):
     moved = shifted(sketch)
-    chip = jnp.concatenate((chip_sum(slab, sketch), chip_sum(slab, moved)), axis=3)
-    own_rows = spread(spread(chip, PLANE).sum(axis=0), "z").sum(axis=0)
-    return solve_rows(lower_gram(own_rows), own_rows, math.sqrt(ROWS))
+    rows, own_rows = assembled(gathered(scattered_sum(slab, sketch, moved), PLANE + ("c",)))
+    return solve_rows(lower_gram(rows), own_rows, math.sqrt(ROWS))
 
 
 def solution(mesh):

time: 150 us -> 148 us (0.987)
  waiting for transfers between devices: 34.4 us -> 28.3 us
  blocking collectives: 73.9 us -> 68.3 us
  starting transfers between devices: 11.6 us -> 15.6 us
  local copies, waits for them, and re-layouts: 5.78 us -> 9.23 us
  other arithmetic: 0.77 us -> 2.32 us
    ppermute x1, waiting for transfers between devices: 21 us -> 14.4 us  [shifted(): return lax.ppermute(block, loop, [(i, (i + 1) % size) for i in range(size)])]
    all_to_all x4, blocking collectives: 73.9 us -> 68.3 us  [spread(): return lax.all_to_all(block, axes, 0, 0, tiled=True)]
    unnamed x4 -> x6, local copies, waits for them, and re-layouts: 4.61 us -> 7.99 us
    ppermute x0 -> x1, starting transfers between devices: none -> 2.75 us  [own_sum(): lax.ppermute(away, ('yl', 'yh'), [(i, 3 - i) for i in range(4)])]
    another operation x0 -> x4, other arithmetic: none -> 2.19 us  [the longest x3 2.15 us: own_sum(): away = jnp.stack([jnp.where(low, chip[2 + t], chip[t]) for t in range(2)])]
    ppermute x2 -> x8, starting transfers between devices: 2.52 us -> 3.74 us  [core_swap(): return lax.ppermute(block, 'c', [(0, 1), (1, 0)])]
  transfers between devices with their start and end apart: 4 -> 11, of which waited for: 3 -> 8; matrix products, arithmetic and copies ran while one was open for 0% -> 1% of each run, Pallas kernels for 5% -> 5%
where the time goes in v5:
time: 148 us; the launch traced here: 147 us
  blocking collectives  68.3 us (46%)
  waiting for transfers between devices  28.3 us (19%)
  Pallas kernels  23 us (16%)
  starting transfers between devices  15.6 us (11%)
  local copies, waits for them, and re-layouts  9.23 us (6%)
  other arithmetic  2.32 us (2%)
    all_to_all x4, blocking collectives, spread(): return lax.all_to_all(block, axes, 0, 0, tiled=True)  68.3 us
    pallas_call x1, Pallas kernels, solve_rows(): pl.pallas_call(functools.partial(kernel, scale), out_shape=jax.ShapeDtype...  15.2 us
    ppermute x1, waiting for transfers between devices, shifted(): return lax.ppermute(block, loop, [(i, (i + 1) % size) for i in range(size)])  14.4 us
    all_to_all x1, waiting for transfers between devices, spread(): return lax.all_to_all(block, axes, 0, 0, tiled=True)  11.3 us
    unnamed x6, local copies, waits for them, and re-layouts  7.99 us
    pallas_call x2, Pallas kernels, product(): pl.pallas_call(product_kernel, grid=(depth,), in_specs=[pl.BlockSpec((row...  7.61 us
    all_to_all x1, starting transfers between devices, spread(): return lax.all_to_all(block, axes, 0, 0, tiled=True)  6.99 us
    ppermute x8, starting transfers between devices, core_swap(): return lax.ppermute(block, 'c', [(0, 1), (1, 0)])  3.74 us
  transfers between devices with their start and end apart: 11, of which 8 were waited for; matrix products, arithmetic and copies ran while one was open for 1% of the time, Pallas kernels for 5%

profile of v5, /device:TPU:1, one launch (start us, length us, event | category | flops | bytes accessed | tf_op | source)
XLA Modules:
  0.0 147.3 jit_solution(5547010996037356917)
XLA Ops:
  0.0 2.1 %collective-permute-start.5 = (bf16[2048,256]{1,0:T(8,128)(2,1)}, bf16[2048,256]{1,0:T(8,128)(2,1)S(1)}, u32[]{:S(2)}, u32[]{:S(2)}) collective-permute-start(bf16[2048,256]{1,0:T(8,128)(2,1)} %sketch_ref.1), channel_id=1, source_target_pairs={{0,4},{4,8},{8,12},{12,16},{16,20},{20,24},{24,28},{28,32},{32,36}... | collective-permute-start | bytes 3145736 | tf_op jit(solution)/shard_map/ppermute | solution.py:142
  2.1 3.4 %copy-done = bf16[2048,2048]{1,0:T(8,128)(2,1)S(1)} copy-done((bf16[2048,2048]{1,0:T(8,128)(2,1)S(1)}, bf16[2048,2048]{1,0:T(8,128)(2,1)}, u32[]{:S(2)}) %copy-start) | copy-done | bytes 8388632
  5.5 1.2 copy-done.2
  6.7 3.8 %shard_map.28 = (f32[8,8,8,128]{3,2,1,0:T(8,128)S(1)}, f32[8,8,8,128]{3,2,1,0:T(8,128)S(1)}, f32[8,8,8,128]{3,2,1,0:T(8,128)S(1)}, f32[8,8,8,128]{3,2,1,0:T(8,12...) custom-call(bf16[2048,2048]{1,0:T(8,128)(2,1)S(1)} %copy-done, ...), custom_call_target="tpu_custom_call" | custom-call | flops 2147483648 | bytes 8388608 | tf_op jit(solution)/shard_map/pallas_call | solution.py:178
  10.5 1.2 collective-permute-start
  11.9 0.4 collective-permute-start.2
  12.4 0.7 collective-permute-done
  13.4 1.1 select_bitcast_fusion.1
  14.5 1.0 select_bitcast_fusion
  15.6 2.8 %collective-permute-start.4 = (f32[2,8,8,8,128]{4,3,2,1,0:T(8,128)S(1)}, f32[2,8,8,8,128]{4,3,2,1,0:T(8,128)S(1)}, u32[]{:S(2)}, u32[]{:S(2)}) collective-permute-start(f32[2,8,8,8,128]{4,3,2,1,0:T(8,128)S(1)} %pad_maximum_fusion.1), channel_id=1, source_target_pairs={{0,6},{2,4},{4,2},{6,0},{1,7},{3,5},{5,3},{7,1},{8,14},{10,12},{12... | collective-permute-start | bytes 1572872 | tf_op jit(solution)/shard_map/ppermute | solution.py:195
  18.4 14.4 %collective-permute-done.5.sketch_ref = bf16[2048,256]{1,0:T(8,128)(2,1)S(1)} collective-permute-done((bf16[2048,256]{1,0:T(8,128)(2,1)}, bf16[2048,256]{1,0:T(8,128)(2,1)S(1)}, u32[]{:S(2)}, u32[]{:S(2)}) %collective-permute-start.5) | collective-permute-done | bytes 1048608 | tf_op jit(solution)/shard_map/ppermute | solution.py:142
  32.7 3.4 %copy-done.1 = bf16[2048,2048]{1,0:T(8,128)(2,1)S(1)} copy-done((bf16[2048,2048]{1,0:T(8,128)(2,1)S(1)}, bf16[2048,2048]{1,0:T(8,128)(2,1)}, u32[]{:S(2)}) %copy-start.1) | copy-done | bytes 8388632
  36.1 3.8 %shard_map.29 = (f32[8,8,8,128]{3,2,1,0:T(8,128)S(1)}, f32[8,8,8,128]{3,2,1,0:T(8,128)S(1)}, f32[8,8,8,128]{3,2,1,0:T(8,128)S(1)}, f32[8,8,8,128]{3,2,1,0:T(8,12...) custom-call(bf16[2048,2048]{1,0:T(8,128)(2,1)S(1)} %copy-done.1, ...), custom_call_target="tpu_custom_call" | custom-call | flops 2147483648 | bytes 8388608 | tf_op jit(solution)/shard_map/pallas_call | solution.py:178
  39.9 1.3 collective-permute-start.6
  41.3 0.4 collective-permute-start.8
  41.9 0.5 collective-permute-done.6.refs_4_
  43.7 25.8 %all_to_all.25 = f32[16,8,3,8,128]{4,3,2,1,0:T(8,128)S(1)} all-to-all(f32[16,8,3,8,128]{4,3,2,1,0:T(8,128)S(1)} %shard_map.30), channel_id=1, replica_groups=mesh['z'=8,'x'=4,'yl'=2,'yh'=2,'c'=2] {'x','yl','yh'}, dimensions={0} | all-to-all | bytes 3145728 | tf_op jit(solution)/shard_map/all_to_all | solution.py:150
  69.7 13.1 %all_to_all.26 = f32[8,4,8,128]{3,2,1,0:T(8,128)S(1)} all-to-all(f32[8,4,8,128]{3,2,1,0:T(8,128)S(1)} %pad_maximum_fusion.2), channel_id=1, replica_groups=mesh['z'=8,'x'=4,'yl'=2,'yh'=2,'c'=2] {'z'}, dimensions={0} | all-to-all | bytes 262144 | tf_op jit(solution)/shard_map/all_to_all | solution.py:150
  82.8 0.9 broadcast_in_dim.6
  83.7 7.0 %all-to-all-start.2 = ((f32[32,4,8,128]{3,2,1,0:T(8,128)}), f32[32,4,8,128]{3,2,1,0:T(8,128)S(1)}, u32[]{:S(2)}, u32[]{:S(2)}) async-start(f32[32,4,8,128]{3,2,1,0:T(8,128)} %broadcast_in_dim.6), calls=%async_computation.2 | async-start | bytes 1048576 | tf_op jit(solution)/shard_map/all_to_all | solution.py:150
  90.7 11.3 %all-to-all-done.2.parts_ref = f32[32,4,8,128]{3,2,1,0:T(8,128)S(1)} async-done(((f32[32,4,8,128]{3,2,1,0:T(8,128)}), f32[32,4,8,128]{3,2,1,0:T(8,128)S(1)}, u32[]{:S(2)}, u32[]{:S(2)}) %all-to-all-start.2) | async-done | bytes 524320 | tf_op jit(solution)/shard_map/all_to_all | solution.py:150
  102.7 11.7 %all_to_all.27 = f32[8,8,640]{2,1,0:T(8,128)S(1)} all-to-all(f32[8,8,640]{2,1,0:T(8,128)S(1)} %broadcast_in_dim.7), channel_id=1, replica_groups=mesh['z'=8,'x'=4,'yl'=2,'yh'=2,'c'=2] {'z'}, dimensions={0} | all-to-all | bytes 327680 | tf_op jit(solution)/shard_map/all_to_all | solution.py:150
  114.5 17.6 %all_to_all.28.gram_ref = f32[32,8,640]{2,1,0:T(8,128)S(1)} all-to-all(f32[32,8,640]{2,1,0:T(8,128)S(1)} %broadcast_in_dim.8), channel_id=1, replica_groups=mesh['z'=8,'x'=4,'yl'=2,'yh'=2,'c'=2] {'x','yl','yh','c'}, dimensions={0} | all-to-all | bytes 1310720 | tf_op jit(solution)/shard_map/all_to_all | solution.py:150
  132.1 15.2 %shard_map.32 = f32[8,512]{1,0:T(8,128)} custom-call(f32[32,8,640]{2,1,0:T(8,128)S(1)} %all_to_all.28.gram_ref, f32[8,512]{1,0:T(8,128)S(1)} %get-tuple-element.40.rows_ref), custom_call_target="tpu_custom_call" | custom-call | tf_op jit(solution)/shard_map/pallas_call | solution.py:125
  (36 shorter events, 3.1 us)
Async XLA Ops:
  0.0 32.7 %collective-permute-start.5 = (bf16[2048,256]{1,0:T(8,128)(2,1)}, bf16[2048,256]{1,0:T(8,128)(2,1)S(1)}, u32[]{:S(2)}, u32[]{:S(2)}) collective-permute-start(bf16[2048,256]{1,0:T(8,128)(2,1)} %sketch_ref.1), channel_id=1, source_target_pairs={{0,4},{4,8},{8,12},{12,16},{16,20},{20,24},{24,28},{28,32},{32,36}... | collective-permute-start | bytes 3145736 | tf_op jit(solution)/shard_map/ppermute | solution.py:142
  2.1 3.4 %copy-start = (bf16[2048,2048]{1,0:T(8,128)(2,1)S(1)}, bf16[2048,2048]{1,0:T(8,128)(2,1)}, u32[]{:S(2)}) copy-start(bf16[2048,2048]{1,0:T(8,128)(2,1)} %slab_ref.3) | copy-start | bytes 25165828
  5.5 1.2 copy-start.2
  10.5 2.5 %collective-permute-start = (f32[8,8,8,128]{3,2,1,0:T(8,128)S(1)}, f32[8,8,8,128]{3,2,1,0:T(8,128)}, u32[]{:S(2)}, u32[]{:S(2)}) collective-permute-start(f32[8,8,8,128]{3,2,1,0:T(8,128)S(1)} %get-tuple-element.24), channel_id=1, source_target_pairs={{0,1},{1,0},{2,3},{3,2},{4,5},{5,4},{6,7},{7,6},{8,9},{9,8},{10,11... | collective-permute-start | bytes 786440 | tf_op jit(solution)/shard_map/ppermute | solution.py:146
  11.8 1.7 %collective-permute-start.1 = (f32[8,8,8,128]{3,2,1,0:T(8,128)S(1)}, f32[8,8,8,128]{3,2,1,0:T(8,128)}, u32[]{:S(2)}, u32[]{:S(2)}) collective-permute-start(f32[8,8,8,128]{3,2,1,0:T(8,128)S(1)} %get-tuple-element.26), channel_id=1, source_target_pairs={{0,1},{1,0},{2,3},{3,2},{4,5},{5,4},{6,7},{7,6},{8,9},{9,8},{10,11... | collective-permute-start | bytes 786440 | tf_op jit(solution)/shard_map/ppermute | solution.py:146
  11.9 2.7 %collective-permute-start.2 = (f32[8,8,8,128]{3,2,1,0:T(8,128)S(1)}, f32[8,8,8,128]{3,2,1,0:T(8,128)S(1)}, u32[]{:S(2)}, u32[]{:S(2)}) collective-permute-start(f32[8,8,8,128]{3,2,1,0:T(8,128)S(1)} %get-tuple-element.28), channel_id=1, source_target_pairs={{0,1},{1,0},{2,3},{3,2},{4,5},{5,4},{6,7},{7,6},{8,9},{9,8},{10,11... | collective-permute-start | bytes 786440 | tf_op jit(solution)/shard_map/ppermute | solution.py:146
  12.3 2.3 %collective-permute-start.3 = (f32[8,8,8,128]{3,2,1,0:T(8,128)S(1)}, f32[8,8,8,128]{3,2,1,0:T(8,128)}, u32[]{:S(2)}, u32[]{:S(2)}) collective-permute-start(f32[8,8,8,128]{3,2,1,0:T(8,128)S(1)} %get-tuple-element.30), channel_id=1, source_target_pairs={{0,1},{1,0},{2,3},{3,2},{4,5},{5,4},{6,7},{7,6},{8,9},{9,8},{10,11... | collective-permute-start | bytes 786440 | tf_op jit(solution)/shard_map/ppermute | solution.py:146
  15.6 26.3 %collective-permute-start.4 = (f32[2,8,8,8,128]{4,3,2,1,0:T(8,128)S(1)}, f32[2,8,8,8,128]{4,3,2,1,0:T(8,128)S(1)}, u32[]{:S(2)}, u32[]{:S(2)}) collective-permute-start(f32[2,8,8,8,128]{4,3,2,1,0:T(8,128)S(1)} %pad_maximum_fusion.1), channel_id=1, source_target_pairs={{0,6},{2,4},{4,2},{6,0},{1,7},{3,5},{5,3},{7,1},{8,14},{10,12},{12... | collective-permute-start | bytes 1572872 | tf_op jit(solution)/shard_map/ppermute | solution.py:195
  32.7 3.4 %copy-start.1 = (bf16[2048,2048]{1,0:T(8,128)(2,1)S(1)}, bf16[2048,2048]{1,0:T(8,128)(2,1)}, u32[]{:S(2)}) copy-start(bf16[2048,2048]{1,0:T(8,128)(2,1)} %slab_ref.3) | copy-start | bytes 25165828
  39.9 2.5 %collective-permute-start.6 = (f32[8,8,8,128]{3,2,1,0:T(8,128)S(1)}, f32[8,8,8,128]{3,2,1,0:T(8,128)S(1)}, u32[]{:S(2)}, u32[]{:S(2)}) collective-permute-start(f32[8,8,8,128]{3,2,1,0:T(8,128)S(1)} %get-tuple-element.35), channel_id=1, source_target_pairs={{0,1},{1,0},{2,3},{3,2},{4,5},{5,4},{6,7},{7,6},{8,9},{9,8},{10,11... | collective-permute-start | bytes 786440 | tf_op jit(solution)/shard_map/ppermute | solution.py:146
  41.2 1.5 %collective-permute-start.7 = (f32[8,8,8,128]{3,2,1,0:T(8,128)S(1)}, f32[8,8,8,128]{3,2,1,0:T(8,128)S(1)}, u32[]{:S(2)}, u32[]{:S(2)}) collective-permute-start(f32[8,8,8,128]{3,2,1,0:T(8,128)S(1)} %get-tuple-element.36), channel_id=1, source_target_pairs={{0,1},{1,0},{2,3},{3,2},{4,5},{5,4},{6,7},{7,6},{8,9},{9,8},{10,11... | collective-permute-start | bytes 786440 | tf_op jit(solution)/shard_map/ppermute | solution.py:146
  41.3 1.8 %collective-permute-start.8 = (f32[8,8,8,128]{3,2,1,0:T(8,128)S(1)}, f32[8,8,8,128]{3,2,1,0:T(8,128)S(1)}, u32[]{:S(2)}, u32[]{:S(2)}) collective-permute-start(f32[8,8,8,128]{3,2,1,0:T(8,128)S(1)} %get-tuple-element.37), channel_id=1, source_target_pairs={{0,1},{1,0},{2,3},{3,2},{4,5},{5,4},{6,7},{7,6},{8,9},{9,8},{10,11... | collective-permute-start | bytes 786440 | tf_op jit(solution)/shard_map/ppermute | solution.py:146
  41.7 1.8 %collective-permute-start.9 = (f32[8,8,8,128]{3,2,1,0:T(8,128)S(1)}, f32[8,8,8,128]{3,2,1,0:T(8,128)S(1)}, u32[]{:S(2)}, u32[]{:S(2)}) collective-permute-start(f32[8,8,8,128]{3,2,1,0:T(8,128)S(1)} %get-tuple-element.38), channel_id=1, source_target_pairs={{0,1},{1,0},{2,3},{3,2},{4,5},{5,4},{6,7},{7,6},{8,9},{9,8},{10,11... | collective-permute-start | bytes 786440 | tf_op jit(solution)/shard_map/ppermute | solution.py:146
  83.7 18.3 %all-to-all-start.2 = ((f32[32,4,8,128]{3,2,1,0:T(8,128)}), f32[32,4,8,128]{3,2,1,0:T(8,128)S(1)}, u32[]{:S(2)}, u32[]{:S(2)}) async-start(f32[32,4,8,128]{3,2,1,0:T(8,128)} %broadcast_in_dim.6), calls=%async_computation.2 | async-start | bytes 1048576 | tf_op jit(solution)/shard_map/all_to_all | solution.py:150

commit v6 on v5

--- a/solution.py
+++ b/solution.py
@@ -155,44 +155,71 @@
     return spread(jnp.broadcast_to(block[None], (size,) + block.shape), axes)
 
 
-def halves(slab_ref, sketch_ref, unit):
-    total = jnp.dot(slab_ref[...], sketch_ref[...], preferred_element_type=jnp.float32)
-    pairs = total.reshape(-1, 2, unit, total.shape[1])
+def store_halves(z, slab_ref, sketch_ref, out_refs):
+    width, depth, unit, _ = out_refs[0].shape
+    step = slab_ref.shape[0] // depth
+    block = slab_ref[pl.ds(pl.multiple_of(z * step, step), step), :]
+    total = jnp.dot(block, sketch_ref[...], preferred_element_type=jnp.float32)
+    pairs = total.reshape(2 * width, 2, unit, total.shape[1])
     first = lax.axis_index("c") == 0
-    return jnp.where(first, pairs[:, 0], pairs[:, 1]), jnp.where(first, pairs[:, 1], pairs[:, 0])
-
-
-def product_kernel(slab_ref, sketch_ref, *out_refs):
-    width, unit, _ = out_refs[0].shape
-    for i, value in enumerate(halves(slab_ref, sketch_ref, unit)):
+    values = jnp.where(first, pairs[:, 0], pairs[:, 1]), jnp.where(first, pairs[:, 1], pairs[:, 0])
+    for i, value in enumerate(values):
         for j in range(4):
             side, t = divmod(j, 2)
-            out_refs[4 * i + j][...] = value[side * width : (side + 1) * width, :, t * B : (t + 1) * B]
-
-
-def product(slab, sketch):
+            out_refs[4 * i + j][:, z] = value[side * width : (side + 1) * width, :, t * B : (t + 1) * B]
+
+
+def own_kernel(slab_ref, sketch_ref, local_ref, *refs):
+    out_refs, sems = refs[:8], refs[8]
+    depth = out_refs[0].shape[1]
+    step = slab_ref.shape[0] // depth
+
+    def fetch(z):
+        rows = pl.ds(pl.multiple_of(z * step, step), step)
+        return pltpu.make_async_copy(slab_ref.at[rows, :], local_ref.at[rows, :], sems.at[z])
+
+    for z in range(depth):
+        fetch(z).start()
+
+    @pl.loop(0, depth)
+    def _(z):
+        fetch(z).wait()
+        store_halves(z, local_ref, sketch_ref, out_refs)
+
+
+def far_kernel(slab_ref, sketch_ref, *out_refs):
+    @pl.loop(0, out_refs[0].shape[1])
+    def _(z):
+        store_halves(z, slab_ref, sketch_ref, out_refs)
+
+
+def product(slab, sketch, fetched):
     rows, inner = slab.shape
     cols = sketch.shape[1]
     depth, width = lax.axis_size("z"), lax.axis_size(PLANE) // 2
     unit = rows // (depth * width * 4)
+    vmem = pl.BlockSpec(memory_space=pltpu.VMEM)
+    parts = [jax.ShapeDtypeStruct((width, depth, unit, B), jnp.float32)] * 8
+    local = [] if fetched else [jax.ShapeDtypeStruct(slab.shape, slab.dtype)]
     return pl.pallas_call(
-        product_kernel,
-        grid=(depth,),
-        in_specs=[pl.BlockSpec((rows // depth, inner), lambda z: (z, 0)), pl.BlockSpec((inner, cols), lambda z: (0, 0))],
-        out_specs=[pl.BlockSpec((width, None, unit, B), lambda z: (0, z, 0, 0))] * 8,
-        out_shape=[jax.ShapeDtypeStruct((width, depth, unit, B), jnp.float32)] * 8,
+        far_kernel if fetched else own_kernel,
+        in_specs=[vmem if fetched else pl.BlockSpec(memory_space=pl.ANY), vmem],
+        out_specs=[vmem] * len(local + parts),
+        out_shape=local + parts,
+        scratch_shapes=[] if fetched else [pltpu.SemaphoreType.DMA((depth,))],
         cost_estimate=pl.CostEstimate(flops=2 * rows * inner * cols, bytes_accessed=2 * rows * inner, transcendentals=0),
-        compiler_params=pltpu.CompilerParams(vmem_limit_bytes=16 * 1024 * 1024),
+        compiler_params=pltpu.CompilerParams(vmem_limit_bytes=24 * 1024 * 1024),
     )(slab, sketch)
 
 
 def own_sum(slab, sketch):
-    parts = product(slab, sketch)
+    local, *parts = product(slab, sketch, False)
     chip = [kept + core_swap(away) for kept, away in zip(parts[:4], parts[4:])]
     low = lax.axis_index("yh") == 0
     kept = jnp.stack([jnp.where(low, chip[t], chip[2 + t]) for t in range(2)])
     away = jnp.stack([jnp.where(low, chip[2 + t], chip[t]) for t in range(2)])
-    return kept, lax.ppermute(away, ("yl", "yh"), [(i, 3 - i) for i in range(4)])
+    got = lax.ppermute(away, ("yl", "yh"), [(i, 3 - i) for i in range(4)])
+    return local, (kept, got)
 
 
 def combine_kernel(own_kept, own_got, *refs):
@@ -217,8 +244,8 @@
 
 
 def scattered_sum(slab, sketch, moved):
-    own = own_sum(slab, sketch)
-    parts = product(slab, moved)
+    local, own = own_sum(slab, sketch)
+    parts = product(local, moved, True)
     plane = spread(combined(own, parts[:4], [core_swap(away) for away in parts[4:]]), PLANE)
     count, depth, _, unit, _ = plane.shape
     far = plane[:, :, :2].sum(axis=0)

time: 148 us -> 148 us (level)
  waiting for transfers between devices: 28.3 us -> 24.9 us
  local copies, waits for them, and re-layouts: 9.23 us -> 12.4 us
    ppermute x1, waiting for transfers between devices: 14.4 us -> 10.5 us  [shifted(): return lax.ppermute(block, loop, [(i, (i + 1) % size) for i in range(size)])]
    unnamed x6 -> x8, local copies, waits for them, and re-layouts: 7.99 us -> 11.2 us
where the time goes in v6:
time: 148 us; the launch traced here: 147 us
  blocking collectives  68.3 us (46%)
  waiting for transfers between devices  24.9 us (17%)
  Pallas kernels  23.1 us (16%)
  starting transfers between devices  15.4 us (10%)
  local copies, waits for them, and re-layouts  12.4 us (8%)
  other arithmetic  2.33 us (2%)
    all_to_all x4, blocking collectives, spread(): return lax.all_to_all(block, axes, 0, 0, tiled=True)  68.3 us
    pallas_call x1, Pallas kernels, solve_rows(): pl.pallas_call(functools.partial(kernel, scale), out_shape=jax.ShapeDtype...  15.2 us
    all_to_all x1, waiting for transfers between devices, spread(): return lax.all_to_all(block, axes, 0, 0, tiled=True)  11.3 us
    unnamed x8, local copies, waits for them, and re-layouts  11.2 us
    ppermute x1, waiting for transfers between devices, shifted(): return lax.ppermute(block, loop, [(i, (i + 1) % size) for i in range(size)])  10.5 us
    pallas_call x2, Pallas kernels, product(): pl.pallas_call(far_kernel if fetched else own_kernel, in_specs=[vmem if f...  7.69 us
    all_to_all x1, starting transfers between devices, spread(): return lax.all_to_all(block, axes, 0, 0, tiled=True)  6.99 us
    ppermute x8, starting transfers between devices, core_swap(): return lax.ppermute(block, 'c', [(0, 1), (1, 0)])  3.55 us
  transfers between devices with their start and end apart: 11, of which 8 were waited for; matrix products, arithmetic and copies ran while one was open for 1% of the time, Pallas kernels for 5%

profile of v6, /device:TPU:1, one launch (start us, length us, event | category | flops | bytes accessed | tf_op | source)
XLA Modules:
  0.0 147.0 jit_solution(12367086002001100735)
XLA Ops:
  0.0 2.1 %collective-permute-start.5 = (bf16[2048,256]{1,0:T(8,128)(2,1)}, bf16[2048,256]{1,0:T(8,128)(2,1)S(1)}, u32[]{:S(2)}, u32[]{:S(2)}) collective-permute-start(bf16[2048,256]{1,0:T(8,128)(2,1)} %sketch_ref.1), channel_id=1, source_target_pairs={{0,4},{4,8},{8,12},{12,16},{16,20},{20,24},{24,28},{28,32},{32,36}... | collective-permute-start | bytes 3145736 | tf_op jit(solution)/shard_map/ppermute | solution.py:142
  2.1 3.4 %copy-done = bf16[2048,2048]{1,0:T(8,128)(2,1)S(1)} copy-done((bf16[2048,2048]{1,0:T(8,128)(2,1)S(1)}, bf16[2048,2048]{1,0:T(8,128)(2,1)}, u32[]{:S(2)}) %copy-start) | copy-done | bytes 8388632
  5.5 1.2 copy-done.3
  6.7 4.2 %shard_map.28 = (bf16[2048,2048]{1,0:T(8,128)(2,1)S(1)}, f32[8,8,8,128]{3,2,1,0:T(8,128)S(1)}, f32[8,8,8,128]{3,2,1,0:T(8,128)S(1)}, f32[8,8,8,128]{3,2,1,0:T(8,...) custom-call(bf16[2048,2048]{1,0:T(8,128)(2,1)S(1)} %copy-done, ...), custom_call_target="tpu_custom_call" | custom-call | flops 2147483648 | bytes 8388608 | tf_op jit(solution)/shard_map/pallas_call | solution.py:204
  10.9 3.2 %copy-done.1 = bf16[2048,2048]{1,0:T(8,128)(2,1)} copy-done((bf16[2048,2048]{1,0:T(8,128)(2,1)}, bf16[2048,2048]{1,0:T(8,128)(2,1)S(1)}, u32[]{:S(2)}) %copy-start.1) | copy-done | bytes 8388632
  14.1 1.1 collective-permute-start
  15.3 0.5 collective-permute-start.2
  15.8 0.8 collective-permute-done
  16.5 0.7 collective-permute-done.1
  17.3 1.1 select_bitcast_fusion.1
  18.4 1.0 select_bitcast_fusion
  19.4 2.8 %collective-permute-start.4 = (f32[2,8,8,8,128]{4,3,2,1,0:T(8,128)S(1)}, f32[2,8,8,8,128]{4,3,2,1,0:T(8,128)S(1)}, u32[]{:S(2)}, u32[]{:S(2)}) collective-permute-start(f32[2,8,8,8,128]{4,3,2,1,0:T(8,128)S(1)} %pad_maximum_fusion.1), channel_id=1, source_target_pairs={{0,6},{2,4},{4,2},{6,0},{1,7},{3,5},{5,3},{7,1},{8,14},{10,12},{12... | collective-permute-start | bytes 1572872 | tf_op jit(solution)/shard_map/ppermute | solution.py:221
  22.2 10.5 %collective-permute-done.5.sketch_ref = bf16[2048,256]{1,0:T(8,128)(2,1)S(1)} collective-permute-done((bf16[2048,256]{1,0:T(8,128)(2,1)}, bf16[2048,256]{1,0:T(8,128)(2,1)S(1)}, u32[]{:S(2)}, u32[]{:S(2)}) %collective-permute-start.5) | collective-permute-done | bytes 1048608 | tf_op jit(solution)/shard_map/ppermute | solution.py:142
  32.7 3.4 %copy-done.2 = bf16[2048,2048]{1,0:T(8,128)(2,1)S(1)} copy-done((bf16[2048,2048]{1,0:T(8,128)(2,1)S(1)}, bf16[2048,2048]{1,0:T(8,128)(2,1)}, u32[]{:S(2)}) %copy-start.2) | copy-done | bytes 8388632
  36.1 3.5 %shard_map.29 = (f32[8,8,8,128]{3,2,1,0:T(8,128)S(1)}, f32[8,8,8,128]{3,2,1,0:T(8,128)S(1)}, f32[8,8,8,128]{3,2,1,0:T(8,128)S(1)}, f32[8,8,8,128]{3,2,1,0:T(8,12...) custom-call(bf16[2048,2048]{1,0:T(8,128)(2,1)S(1)} %copy-done.2, ...), custom_call_target="tpu_custom_call" | custom-call | flops 2147483648 | bytes 8388608 | tf_op jit(solution)/shard_map/pallas_call | solution.py:204
  39.6 1.3 collective-permute-start.6
  43.4 25.8 %all_to_all.25 = f32[16,8,3,8,128]{4,3,2,1,0:T(8,128)S(1)} all-to-all(f32[16,8,3,8,128]{4,3,2,1,0:T(8,128)S(1)} %shard_map.30), channel_id=1, replica_groups=mesh['z'=8,'x'=4,'yl'=2,'yh'=2,'c'=2] {'x','yl','yh'}, dimensions={0} | all-to-all | bytes 3145728 | tf_op jit(solution)/shard_map/all_to_all | solution.py:150
  69.4 13.1 %all_to_all.26 = f32[8,4,8,128]{3,2,1,0:T(8,128)S(1)} all-to-all(f32[8,4,8,128]{3,2,1,0:T(8,128)S(1)} %pad_maximum_fusion.2), channel_id=1, replica_groups=mesh['z'=8,'x'=4,'yl'=2,'yh'=2,'c'=2] {'z'}, dimensions={0} | all-to-all | bytes 262144 | tf_op jit(solution)/shard_map/all_to_all | solution.py:150
  82.5 0.9 broadcast_in_dim.6
  83.4 7.0 %all-to-all-start.2 = ((f32[32,4,8,128]{3,2,1,0:T(8,128)}), f32[32,4,8,128]{3,2,1,0:T(8,128)S(1)}, u32[]{:S(2)}, u32[]{:S(2)}) async-start(f32[32,4,8,128]{3,2,1,0:T(8,128)} %broadcast_in_dim.6), calls=%async_computation.2 | async-start | bytes 1048576 | tf_op jit(solution)/shard_map/all_to_all | solution.py:150
  90.4 11.3 %all-to-all-done.2.parts_ref = f32[32,4,8,128]{3,2,1,0:T(8,128)S(1)} async-done(((f32[32,4,8,128]{3,2,1,0:T(8,128)}), f32[32,4,8,128]{3,2,1,0:T(8,128)S(1)}, u32[]{:S(2)}, u32[]{:S(2)}) %all-to-all-start.2) | async-done | bytes 524320 | tf_op jit(solution)/shard_map/all_to_all | solution.py:150
  102.4 11.7 %all_to_all.27 = f32[8,8,640]{2,1,0:T(8,128)S(1)} all-to-all(f32[8,8,640]{2,1,0:T(8,128)S(1)} %broadcast_in_dim.7), channel_id=1, replica_groups=mesh['z'=8,'x'=4,'yl'=2,'yh'=2,'c'=2] {'z'}, dimensions={0} | all-to-all | bytes 327680 | tf_op jit(solution)/shard_map/all_to_all | solution.py:150
  114.2 17.6 %all_to_all.28.gram_ref = f32[32,8,640]{2,1,0:T(8,128)S(1)} all-to-all(f32[32,8,640]{2,1,0:T(8,128)S(1)} %broadcast_in_dim.8), channel_id=1, replica_groups=mesh['z'=8,'x'=4,'yl'=2,'yh'=2,'c'=2] {'x','yl','yh','c'}, dimensions={0} | all-to-all | bytes 1310720 | tf_op jit(solution)/shard_map/all_to_all | solution.py:150
  131.8 15.2 %shard_map.32 = f32[8,512]{1,0:T(8,128)} custom-call(f32[32,8,640]{2,1,0:T(8,128)S(1)} %all_to_all.28.gram_ref, f32[8,512]{1,0:T(8,128)S(1)} %get-tuple-element.42.rows_ref), custom_call_target="tpu_custom_call" | custom-call | tf_op jit(solution)/shard_map/pallas_call | solution.py:125
  (38 shorter events, 3.4 us)
Async XLA Ops:
  0.0 32.7 %collective-permute-start.5 = (bf16[2048,256]{1,0:T(8,128)(2,1)}, bf16[2048,256]{1,0:T(8,128)(2,1)S(1)}, u32[]{:S(2)}, u32[]{:S(2)}) collective-permute-start(bf16[2048,256]{1,0:T(8,128)(2,1)} %sketch_ref.1), channel_id=1, source_target_pairs={{0,4},{4,8},{8,12},{12,16},{16,20},{20,24},{24,28},{28,32},{32,36}... | collective-permute-start | bytes 3145736 | tf_op jit(solution)/shard_map/ppermute | solution.py:142
  2.1 3.4 %copy-start = (bf16[2048,2048]{1,0:T(8,128)(2,1)S(1)}, bf16[2048,2048]{1,0:T(8,128)(2,1)}, u32[]{:S(2)}) copy-start(bf16[2048,2048]{1,0:T(8,128)(2,1)} %slab_ref.1) | copy-start | bytes 25165828
  5.5 1.2 copy-start.3
  10.9 3.2 %copy-start.1 = (bf16[2048,2048]{1,0:T(8,128)(2,1)}, bf16[2048,2048]{1,0:T(8,128)(2,1)S(1)}, u32[]{:S(2)}) copy-start(bf16[2048,2048]{1,0:T(8,128)(2,1)S(1)} %get-tuple-element.32.slab_ref) | copy-start | bytes 25165828
  14.1 2.4 %collective-permute-start = (f32[8,8,8,128]{3,2,1,0:T(8,128)S(1)}, f32[8,8,8,128]{3,2,1,0:T(8,128)}, u32[]{:S(2)}, u32[]{:S(2)}) collective-permute-start(f32[8,8,8,128]{3,2,1,0:T(8,128)S(1)} %get-tuple-element.25), channel_id=1, source_target_pairs={{0,1},{1,0},{2,3},{3,2},{4,5},{5,4},{6,7},{7,6},{8,9},{9,8},{10,11... | collective-permute-start | bytes 786440 | tf_op jit(solution)/shard_map/ppermute | solution.py:146
  15.3 2.0 %collective-permute-start.1 = (f32[8,8,8,128]{3,2,1,0:T(8,128)S(1)}, f32[8,8,8,128]{3,2,1,0:T(8,128)}, u32[]{:S(2)}, u32[]{:S(2)}) collective-permute-start(f32[8,8,8,128]{3,2,1,0:T(8,128)S(1)} %get-tuple-element.27), channel_id=1, source_target_pairs={{0,1},{1,0},{2,3},{3,2},{4,5},{5,4},{6,7},{7,6},{8,9},{9,8},{10,11... | collective-permute-start | bytes 786440 | tf_op jit(solution)/shard_map/ppermute | solution.py:146
  15.3 3.1 %collective-permute-start.2 = (f32[8,8,8,128]{3,2,1,0:T(8,128)S(1)}, f32[8,8,8,128]{3,2,1,0:T(8,128)S(1)}, u32[]{:S(2)}, u32[]{:S(2)}) collective-permute-start(f32[8,8,8,128]{3,2,1,0:T(8,128)S(1)} %get-tuple-element.29), channel_id=1, source_target_pairs={{0,1},{1,0},{2,3},{3,2},{4,5},{5,4},{6,7},{7,6},{8,9},{9,8},{10,11... | collective-permute-start | bytes 786440 | tf_op jit(solution)/shard_map/ppermute | solution.py:146
  15.8 2.6 %collective-permute-start.3 = (f32[8,8,8,128]{3,2,1,0:T(8,128)S(1)}, f32[8,8,8,128]{3,2,1,0:T(8,128)}, u32[]{:S(2)}, u32[]{:S(2)}) collective-permute-start(f32[8,8,8,128]{3,2,1,0:T(8,128)S(1)} %get-tuple-element.31), channel_id=1, source_target_pairs={{0,1},{1,0},{2,3},{3,2},{4,5},{5,4},{6,7},{7,6},{8,9},{9,8},{10,11... | collective-permute-start | bytes 786440 | tf_op jit(solution)/shard_map/ppermute | solution.py:146
  19.4 22.2 %collective-permute-start.4 = (f32[2,8,8,8,128]{4,3,2,1,0:T(8,128)S(1)}, f32[2,8,8,8,128]{4,3,2,1,0:T(8,128)S(1)}, u32[]{:S(2)}, u32[]{:S(2)}) collective-permute-start(f32[2,8,8,8,128]{4,3,2,1,0:T(8,128)S(1)} %pad_maximum_fusion.1), channel_id=1, source_target_pairs={{0,6},{2,4},{4,2},{6,0},{1,7},{3,5},{5,3},{7,1},{8,14},{10,12},{12... | collective-permute-start | bytes 1572872 | tf_op jit(solution)/shard_map/ppermute | solution.py:221
  32.7 3.4 %copy-start.2 = (bf16[2048,2048]{1,0:T(8,128)(2,1)S(1)}, bf16[2048,2048]{1,0:T(8,128)(2,1)}, u32[]{:S(2)}) copy-start(bf16[2048,2048]{1,0:T(8,128)(2,1)} %copy-done.1) | copy-start | bytes 25165828
  39.6 2.5 %collective-permute-start.6 = (f32[8,8,8,128]{3,2,1,0:T(8,128)S(1)}, f32[8,8,8,128]{3,2,1,0:T(8,128)S(1)}, u32[]{:S(2)}, u32[]{:S(2)}) collective-permute-start(f32[8,8,8,128]{3,2,1,0:T(8,128)S(1)} %get-tuple-element.37), channel_id=1, source_target_pairs={{0,1},{1,0},{2,3},{3,2},{4,5},{5,4},{6,7},{7,6},{8,9},{9,8},{10,11... | collective-permute-start | bytes 786440 | tf_op jit(solution)/shard_map/ppermute | solution.py:146
  40.9 1.5 %collective-permute-start.7 = (f32[8,8,8,128]{3,2,1,0:T(8,128)S(1)}, f32[8,8,8,128]{3,2,1,0:T(8,128)S(1)}, u32[]{:S(2)}, u32[]{:S(2)}) collective-permute-start(f32[8,8,8,128]{3,2,1,0:T(8,128)S(1)} %get-tuple-element.38), channel_id=1, source_target_pairs={{0,1},{1,0},{2,3},{3,2},{4,5},{5,4},{6,7},{7,6},{8,9},{9,8},{10,11... | collective-permute-start | bytes 786440 | tf_op jit(solution)/shard_map/ppermute | solution.py:146
  41.0 1.8 %collective-permute-start.8 = (f32[8,8,8,128]{3,2,1,0:T(8,128)S(1)}, f32[8,8,8,128]{3,2,1,0:T(8,128)S(1)}, u32[]{:S(2)}, u32[]{:S(2)}) collective-permute-start(f32[8,8,8,128]{3,2,1,0:T(8,128)S(1)} %get-tuple-element.39), channel_id=1, source_target_pairs={{0,1},{1,0},{2,3},{3,2},{4,5},{5,4},{6,7},{7,6},{8,9},{9,8},{10,11... | collective-permute-start | bytes 786440 | tf_op jit(solution)/shard_map/ppermute | solution.py:146
  41.4 1.8 %collective-permute-start.9 = (f32[8,8,8,128]{3,2,1,0:T(8,128)S(1)}, f32[8,8,8,128]{3,2,1,0:T(8,128)S(1)}, u32[]{:S(2)}, u32[]{:S(2)}) collective-permute-start(f32[8,8,8,128]{3,2,1,0:T(8,128)S(1)} %get-tuple-element.40), channel_id=1, source_target_pairs={{0,1},{1,0},{2,3},{3,2},{4,5},{5,4},{6,7},{7,6},{8,9},{9,8},{10,11... | collective-permute-start | bytes 786440 | tf_op jit(solution)/shard_map/ppermute | solution.py:146
  83.4 18.3 %all-to-all-start.2 = ((f32[32,4,8,128]{3,2,1,0:T(8,128)}), f32[32,4,8,128]{3,2,1,0:T(8,128)S(1)}, u32[]{:S(2)}, u32[]{:S(2)}) async-start(f32[32,4,8,128]{3,2,1,0:T(8,128)} %broadcast_in_dim.6), calls=%async_computation.2 | async-start | bytes 1048576 | tf_op jit(solution)/shard_map/all_to_all | solution.py:150

commit v7 on v6

--- a/solution.py
+++ b/solution.py
@@ -212,12 +212,27 @@
     )(slab, sketch)
 
 
+def pair_kernel(*refs):
+    kept_ref, away_ref = refs[8:]
+    low = lax.axis_index("yh") == 0
+    for q in range(kept_ref.shape[1]):
+        for t in range(2):
+            first = refs[t][q] + refs[4 + t][q]
+            second = refs[2 + t][q] + refs[6 + t][q]
+            kept_ref[t, q] = jnp.where(low, first, second)
+            away_ref[t, q] = jnp.where(low, second, first)
+
+
 def own_sum(slab, sketch):
     local, *parts = product(slab, sketch, False)
-    chip = [kept + core_swap(away) for kept, away in zip(parts[:4], parts[4:])]
-    low = lax.axis_index("yh") == 0
-    kept = jnp.stack([jnp.where(low, chip[t], chip[2 + t]) for t in range(2)])
-    away = jnp.stack([jnp.where(low, chip[2 + t], chip[t]) for t in range(2)])
+    vmem = pl.BlockSpec(memory_space=pltpu.VMEM)
+    kept, away = pl.pallas_call(
+        pair_kernel,
+        in_specs=[vmem] * 8,
+        out_specs=[vmem] * 2,
+        out_shape=[jax.ShapeDtypeStruct((2,) + parts[0].shape, jnp.float32)] * 2,
+        compiler_params=pltpu.CompilerParams(vmem_limit_bytes=16 * 1024 * 1024),
+    )(*parts[:4], *[core_swap(part) for part in parts[4:]])
     got = lax.ppermute(away, ("yl", "yh"), [(i, 3 - i) for i in range(4)])
     return local, (kept, got)
 

time: 148 us -> 144 us (0.973)
  local copies, waits for them, and re-layouts: 12.4 us -> 5.84 us
  waiting for transfers between devices: 24.9 us -> 30 us
  other arithmetic: 2.33 us -> 0.14 us
    unnamed x8 -> x4, local copies, waits for them, and re-layouts: 11.2 us -> 4.61 us
    ppermute x1, waiting for transfers between devices: 10.5 us -> 15.4 us  [shifted(): return lax.ppermute(block, loop, [(i, (i + 1) % size) for i in range(size)])]
    another operation x4 -> x0, other arithmetic: 2.19 us -> none  [the longest x3 2.15 us: own_sum(): away = jnp.stack([jnp.where(low, chip[2 + t], chip[t]) for t in range(2)])]
  transfers between devices with their start and end apart: 11 -> 11, of which waited for: 8 -> 10; matrix products, arithmetic and copies ran while one was open for 1% -> 0% of each run, Pallas kernels for 5% -> 5%
where the time goes in v7:
time: 144 us
  blocking collectives  68.3 us (47%)
  waiting for transfers between devices  30 us (21%)
  Pallas kernels  23.2 us (16%)
  starting transfers between devices  15.6 us (11%)
  local copies, waits for them, and re-layouts  5.84 us (4%)
    all_to_all x4, blocking collectives, spread(): return lax.all_to_all(block, axes, 0, 0, tiled=True)  68.3 us
    ppermute x1, waiting for transfers between devices, shifted(): return lax.ppermute(block, loop, [(i, (i + 1) % size) for i in range(size)])  15.4 us
    pallas_call x1, Pallas kernels, solve_rows(): pl.pallas_call(functools.partial(kernel, scale), out_shape=jax.ShapeDtype...  15.2 us
    all_to_all x1, waiting for transfers between devices, spread(): return lax.all_to_all(block, axes, 0, 0, tiled=True)  11.3 us
    pallas_call x2, Pallas kernels, product(): pl.pallas_call(far_kernel if fetched else own_kernel, in_specs=[vmem if f...  7.69 us
    all_to_all x1, starting transfers between devices, spread(): return lax.all_to_all(block, axes, 0, 0, tiled=True)  6.99 us
    unnamed x4, local copies, waits for them, and re-layouts  4.61 us
    ppermute x8, starting transfers between devices, core_swap(): return lax.ppermute(block, 'c', [(0, 1), (1, 0)])  3.74 us
  transfers between devices with their start and end apart: 11, of which 10 were waited for; matrix products, arithmetic and copies ran while one was open for 0% of the time, Pallas kernels for 5%

profile of v7, /device:TPU:1, one launch (start us, length us, event | category | flops | bytes accessed | tf_op | source)
XLA Modules:
  0.0 143.7 jit_solution(916809512505477789)
XLA Ops:
  0.0 2.1 %collective-permute-start.5 = (bf16[2048,256]{1,0:T(8,128)(2,1)}, bf16[2048,256]{1,0:T(8,128)(2,1)S(1)}, u32[]{:S(2)}, u32[]{:S(2)}) collective-permute-start(bf16[2048,256]{1,0:T(8,128)(2,1)} %sketch_ref.1), channel_id=1, source_target_pairs={{0,4},{4,8},{8,12},{12,16},{16,20},{20,24},{24,28},{28,32},{32,36}... | collective-permute-start | bytes 3145736 | tf_op jit(solution)/shard_map/ppermute | solution.py:142
  2.1 3.4 %copy-done = bf16[2048,2048]{1,0:T(8,128)(2,1)S(1)} copy-done((bf16[2048,2048]{1,0:T(8,128)(2,1)S(1)}, bf16[2048,2048]{1,0:T(8,128)(2,1)}, u32[]{:S(2)}) %copy-start) | copy-done | bytes 8388632
  5.5 1.2 copy-done.1
  6.7 4.2 %shard_map.28 = (bf16[2048,2048]{1,0:T(8,128)(2,1)S(1)}, f32[8,8,8,128]{3,2,1,0:T(8,128)S(1)}, f32[8,8,8,128]{3,2,1,0:T(8,128)S(1)}, f32[8,8,8,128]{3,2,1,0:T(8,...) custom-call(bf16[2048,2048]{1,0:T(8,128)(2,1)S(1)} %copy-done, ...), custom_call_target="tpu_custom_call" | custom-call | flops 2147483648 | bytes 8388608 | tf_op jit(solution)/shard_map/pallas_call | solution.py:204
  10.9 1.2 collective-permute-start
  12.2 0.4 collective-permute-start.2
  12.7 0.6 collective-permute-done.refs_4_
  13.7 0.4 collective-permute-done.2.refs_6_
  14.5 2.8 %collective-permute-start.4 = (f32[2,8,8,8,128]{4,3,2,1,0:T(8,128)S(1)}, f32[2,8,8,8,128]{4,3,2,1,0:T(8,128)S(1)}, u32[]{:S(2)}, u32[]{:S(2)}) collective-permute-start(f32[2,8,8,8,128]{4,3,2,1,0:T(8,128)S(1)} %get-tuple-element.35), channel_id=1, source_target_pairs={{0,6},{2,4},{4,2},{6,0},{1,7},{3,5},{5,3},{7,1},{8,14},{10,12},{12... | collective-permute-start | bytes 1572872 | tf_op jit(solution)/shard_map/ppermute | solution.py:236
  17.3 15.4 %collective-permute-done.5.sketch_ref = bf16[2048,256]{1,0:T(8,128)(2,1)S(1)} collective-permute-done((bf16[2048,256]{1,0:T(8,128)(2,1)}, bf16[2048,256]{1,0:T(8,128)(2,1)S(1)}, u32[]{:S(2)}, u32[]{:S(2)}) %collective-permute-start.5) | collective-permute-done | bytes 1048608 | tf_op jit(solution)/shard_map/ppermute | solution.py:142
  32.7 3.5 %shard_map.30 = (f32[8,8,8,128]{3,2,1,0:T(8,128)S(1)}, f32[8,8,8,128]{3,2,1,0:T(8,128)S(1)}, f32[8,8,8,128]{3,2,1,0:T(8,128)S(1)}, f32[8,8,8,128]{3,2,1,0:T(8,12...) custom-call(bf16[2048,2048]{1,0:T(8,128)(2,1)S(1)} %get-tuple-elemen, ...), custom_call_target="tpu_custom_call" | custom-call | flops 2147483648 | bytes 8388608 | tf_op jit(solution)/shard_map/pallas_call | solution.py:204
  36.2 1.3 collective-permute-start.6
  37.7 0.4 collective-permute-start.8
  38.2 0.5 collective-permute-done.6.refs_4_
  39.1 0.4 collective-permute-done.8.refs_6_
  40.0 25.8 %all_to_all.25 = f32[16,8,3,8,128]{4,3,2,1,0:T(8,128)S(1)} all-to-all(f32[16,8,3,8,128]{4,3,2,1,0:T(8,128)S(1)} %shard_map.31), channel_id=1, replica_groups=mesh['z'=8,'x'=4,'yl'=2,'yh'=2,'c'=2] {'x','yl','yh'}, dimensions={0} | all-to-all | bytes 3145728 | tf_op jit(solution)/shard_map/all_to_all | solution.py:150
  66.0 13.1 %all_to_all.26 = f32[8,4,8,128]{3,2,1,0:T(8,128)S(1)} all-to-all(f32[8,4,8,128]{3,2,1,0:T(8,128)S(1)} %pad_maximum_fusion), channel_id=1, replica_groups=mesh['z'=8,'x'=4,'yl'=2,'yh'=2,'c'=2] {'z'}, dimensions={0} | all-to-all | bytes 262144 | tf_op jit(solution)/shard_map/all_to_all | solution.py:150
  79.1 0.9 broadcast_in_dim.6
  80.0 7.0 %all-to-all-start.2 = ((f32[32,4,8,128]{3,2,1,0:T(8,128)}), f32[32,4,8,128]{3,2,1,0:T(8,128)S(1)}, u32[]{:S(2)}, u32[]{:S(2)}) async-start(f32[32,4,8,128]{3,2,1,0:T(8,128)} %broadcast_in_dim.6), calls=%async_computation.2 | async-start | bytes 1048576 | tf_op jit(solution)/shard_map/all_to_all | solution.py:150
  87.0 11.3 %all-to-all-done.2.parts_ref = f32[32,4,8,128]{3,2,1,0:T(8,128)S(1)} async-done(((f32[32,4,8,128]{3,2,1,0:T(8,128)}), f32[32,4,8,128]{3,2,1,0:T(8,128)S(1)}, u32[]{:S(2)}, u32[]{:S(2)}) %all-to-all-start.2) | async-done | bytes 524320 | tf_op jit(solution)/shard_map/all_to_all | solution.py:150
  98.6 0.4 fusion
  99.0 11.7 %all_to_all.27 = f32[8,8,640]{2,1,0:T(8,128)S(1)} all-to-all(f32[8,8,640]{2,1,0:T(8,128)S(1)} %broadcast_in_dim.7), channel_id=1, replica_groups=mesh['z'=8,'x'=4,'yl'=2,'yh'=2,'c'=2] {'z'}, dimensions={0} | all-to-all | bytes 327680 | tf_op jit(solution)/shard_map/all_to_all | solution.py:150
  110.8 17.6 %all_to_all.28.gram_ref = f32[32,8,640]{2,1,0:T(8,128)S(1)} all-to-all(f32[32,8,640]{2,1,0:T(8,128)S(1)} %broadcast_in_dim.8), channel_id=1, replica_groups=mesh['z'=8,'x'=4,'yl'=2,'yh'=2,'c'=2] {'x','yl','yh','c'}, dimensions={0} | all-to-all | bytes 1310720 | tf_op jit(solution)/shard_map/all_to_all | solution.py:150
  128.4 15.2 %shard_map.33 = f32[8,512]{1,0:T(8,128)} custom-call(f32[32,8,640]{2,1,0:T(8,128)S(1)} %all_to_all.28.gram_ref, f32[8,512]{1,0:T(8,128)S(1)} %get-tuple-element.46.rows_ref), custom_call_target="tpu_custom_call" | custom-call | tf_op jit(solution)/shard_map/pallas_call | solution.py:125
  (31 shorter events, 2.7 us)
Async XLA Ops:
  0.0 32.7 %collective-permute-start.5 = (bf16[2048,256]{1,0:T(8,128)(2,1)}, bf16[2048,256]{1,0:T(8,128)(2,1)S(1)}, u32[]{:S(2)}, u32[]{:S(2)}) collective-permute-start(bf16[2048,256]{1,0:T(8,128)(2,1)} %sketch_ref.1), channel_id=1, source_target_pairs={{0,4},{4,8},{8,12},{12,16},{16,20},{20,24},{24,28},{28,32},{32,36}... | collective-permute-start | bytes 3145736 | tf_op jit(solution)/shard_map/ppermute | solution.py:142
  2.1 3.4 %copy-start = (bf16[2048,2048]{1,0:T(8,128)(2,1)S(1)}, bf16[2048,2048]{1,0:T(8,128)(2,1)}, u32[]{:S(2)}) copy-start(bf16[2048,2048]{1,0:T(8,128)(2,1)} %slab_ref.1) | copy-start | bytes 25165828
  5.5 1.2 copy-start.1
  10.9 2.4 %collective-permute-start = (f32[8,8,8,128]{3,2,1,0:T(8,128)S(1)}, f32[8,8,8,128]{3,2,1,0:T(8,128)S(1)}, u32[]{:S(2)}, u32[]{:S(2)}) collective-permute-start(f32[8,8,8,128]{3,2,1,0:T(8,128)S(1)} %get-tuple-element.30), channel_id=1, source_target_pairs={{0,1},{1,0},{2,3},{3,2},{4,5},{5,4},{6,7},{7,6},{8,9},{9,8},{10,11... | collective-permute-start | bytes 786440 | tf_op jit(solution)/shard_map/ppermute | solution.py:146
  12.1 1.5 %collective-permute-start.1 = (f32[8,8,8,128]{3,2,1,0:T(8,128)S(1)}, f32[8,8,8,128]{3,2,1,0:T(8,128)S(1)}, u32[]{:S(2)}, u32[]{:S(2)}) collective-permute-start(f32[8,8,8,128]{3,2,1,0:T(8,128)S(1)} %get-tuple-element.31), channel_id=1, source_target_pairs={{0,1},{1,0},{2,3},{3,2},{4,5},{5,4},{6,7},{7,6},{8,9},{9,8},{10,11... | collective-permute-start | bytes 786440 | tf_op jit(solution)/shard_map/ppermute | solution.py:146
  12.2 1.8 %collective-permute-start.2 = (f32[8,8,8,128]{3,2,1,0:T(8,128)S(1)}, f32[8,8,8,128]{3,2,1,0:T(8,128)S(1)}, u32[]{:S(2)}, u32[]{:S(2)}) collective-permute-start(f32[8,8,8,128]{3,2,1,0:T(8,128)S(1)} %get-tuple-element.32), channel_id=1, source_target_pairs={{0,1},{1,0},{2,3},{3,2},{4,5},{5,4},{6,7},{7,6},{8,9},{9,8},{10,11... | collective-permute-start | bytes 786440 | tf_op jit(solution)/shard_map/ppermute | solution.py:146
  12.6 1.8 %collective-permute-start.3 = (f32[8,8,8,128]{3,2,1,0:T(8,128)S(1)}, f32[8,8,8,128]{3,2,1,0:T(8,128)S(1)}, u32[]{:S(2)}, u32[]{:S(2)}) collective-permute-start(f32[8,8,8,128]{3,2,1,0:T(8,128)S(1)} %get-tuple-element.33), channel_id=1, source_target_pairs={{0,1},{1,0},{2,3},{3,2},{4,5},{5,4},{6,7},{7,6},{8,9},{9,8},{10,11... | collective-permute-start | bytes 786440 | tf_op jit(solution)/shard_map/ppermute | solution.py:146
  14.5 23.6 %collective-permute-start.4 = (f32[2,8,8,8,128]{4,3,2,1,0:T(8,128)S(1)}, f32[2,8,8,8,128]{4,3,2,1,0:T(8,128)S(1)}, u32[]{:S(2)}, u32[]{:S(2)}) collective-permute-start(f32[2,8,8,8,128]{4,3,2,1,0:T(8,128)S(1)} %get-tuple-element.35), channel_id=1, source_target_pairs={{0,6},{2,4},{4,2},{6,0},{1,7},{3,5},{5,3},{7,1},{8,14},{10,12},{12... | collective-permute-start | bytes 1572872 | tf_op jit(solution)/shard_map/ppermute | solution.py:236
  36.2 2.5 %collective-permute-start.6 = (f32[8,8,8,128]{3,2,1,0:T(8,128)S(1)}, f32[8,8,8,128]{3,2,1,0:T(8,128)S(1)}, u32[]{:S(2)}, u32[]{:S(2)}) collective-permute-start(f32[8,8,8,128]{3,2,1,0:T(8,128)S(1)} %get-tuple-element.41), channel_id=1, source_target_pairs={{0,1},{1,0},{2,3},{3,2},{4,5},{5,4},{6,7},{7,6},{8,9},{9,8},{10,11... | collective-permute-start | bytes 786440 | tf_op jit(solution)/shard_map/ppermute | solution.py:146
  37.6 1.5 %collective-permute-start.7 = (f32[8,8,8,128]{3,2,1,0:T(8,128)S(1)}, f32[8,8,8,128]{3,2,1,0:T(8,128)S(1)}, u32[]{:S(2)}, u32[]{:S(2)}) collective-permute-start(f32[8,8,8,128]{3,2,1,0:T(8,128)S(1)} %get-tuple-element.42), channel_id=1, source_target_pairs={{0,1},{1,0},{2,3},{3,2},{4,5},{5,4},{6,7},{7,6},{8,9},{9,8},{10,11... | collective-permute-start | bytes 786440 | tf_op jit(solution)/shard_map/ppermute | solution.py:146
  37.7 1.8 %collective-permute-start.8 = (f32[8,8,8,128]{3,2,1,0:T(8,128)S(1)}, f32[8,8,8,128]{3,2,1,0:T(8,128)S(1)}, u32[]{:S(2)}, u32[]{:S(2)}) collective-permute-start(f32[8,8,8,128]{3,2,1,0:T(8,128)S(1)} %get-tuple-element.43), channel_id=1, source_target_pairs={{0,1},{1,0},{2,3},{3,2},{4,5},{5,4},{6,7},{7,6},{8,9},{9,8},{10,11... | collective-permute-start | bytes 786440 | tf_op jit(solution)/shard_map/ppermute | solution.py:146
  38.1 1.8 %collective-permute-start.9 = (f32[8,8,8,128]{3,2,1,0:T(8,128)S(1)}, f32[8,8,8,128]{3,2,1,0:T(8,128)S(1)}, u32[]{:S(2)}, u32[]{:S(2)}) collective-permute-start(f32[8,8,8,128]{3,2,1,0:T(8,128)S(1)} %get-tuple-element.44), channel_id=1, source_target_pairs={{0,1},{1,0},{2,3},{3,2},{4,5},{5,4},{6,7},{7,6},{8,9},{9,8},{10,11... | collective-permute-start | bytes 786440 | tf_op jit(solution)/shard_map/ppermute | solution.py:146
  80.0 18.3 %all-to-all-start.2 = ((f32[32,4,8,128]{3,2,1,0:T(8,128)}), f32[32,4,8,128]{3,2,1,0:T(8,128)S(1)}, u32[]{:S(2)}, u32[]{:S(2)}) async-start(f32[32,4,8,128]{3,2,1,0:T(8,128)} %broadcast_in_dim.6), calls=%async_computation.2 | async-start | bytes 1048576 | tf_op jit(solution)/shard_map/all_to_all | solution.py:150

commit v8 on v7

--- a/solution.py
+++ b/solution.py
@@ -181,14 +181,14 @@
     for z in range(depth):
         fetch(z).start()
 
-    @pl.loop(0, depth)
+    @pl.loop(0, depth, unroll=True)
     def _(z):
         fetch(z).wait()
         store_halves(z, local_ref, sketch_ref, out_refs)
 
 
 def far_kernel(slab_ref, sketch_ref, *out_refs):
-    @pl.loop(0, out_refs[0].shape[1])
+    @pl.loop(0, out_refs[0].shape[1], unroll=True)
     def _(z):
         store_halves(z, slab_ref, sketch_ref, out_refs)
 
@@ -258,7 +258,7 @@
     )(*own, *kept, *got)
 
 
-def scattered_sum(slab, sketch, moved):
+def scattered_parts(slab, sketch, moved):
     local, own = own_sum(slab, sketch)
     parts = product(local, moved, True)
     plane = spread(combined(own, parts[:4], [core_swap(away) for away in parts[4:]]), PLANE)
@@ -266,7 +266,28 @@
     far = plane[:, :, :2].sum(axis=0)
     own = plane[:, :, 2].reshape(count // 2, 2, depth, unit, B).sum(axis=0)
     both = jnp.concatenate((far, own.transpose(1, 0, 2, 3)), axis=1)
-    return spread(both, "z").sum(axis=0)
+    return spread(both, "z")
+
+
+def copies_kernel(parts_ref, out_ref):
+    total = parts_ref[0]
+    for i in range(1, parts_ref.shape[0]):
+        total = total + parts_ref[i]
+    for i in range(out_ref.shape[0]):
+        out_ref[i] = total
+
+
+def gathered_sum(parts, axes):
+    return spread(
+        pl.pallas_call(
+            copies_kernel,
+            in_specs=[pl.BlockSpec(memory_space=pltpu.VMEM)],
+            out_specs=pl.BlockSpec(memory_space=pltpu.VMEM),
+            out_shape=jax.ShapeDtypeStruct((lax.axis_size(axes),) + parts.shape[1:], parts.dtype),
+            compiler_params=pltpu.CompilerParams(vmem_limit_bytes=16 * 1024 * 1024),
+        )(parts),
+        axes,
+    )
 
 
 def assemble_kernel(parts_ref, rows_ref, own_ref):
@@ -315,12 +336,12 @@
     short = jnp.concatenate((part[:unit, :B], part[unit:]), axis=1)
     long = jnp.concatenate((part[:unit, : 2 * B], part[unit:, : 3 * B]), axis=1)
     packed = jnp.where(place * unit < B, short, long)
-    return gathered(gathered(packed, "z").sum(axis=0), wide_axes)
+    return gathered_sum(gathered(packed, "z"), wide_axes)
 
 
 def body(slab, sketch):
     moved = shifted(sketch)
-    rows, own_rows = assembled(gathered(scattered_sum(slab, sketch, moved), PLANE + ("c",)))
+    rows, own_rows = assembled(gathered_sum(scattered_parts(slab, sketch, moved), PLANE + ("c",)))
     return solve_rows(lower_gram(rows), own_rows, math.sqrt(ROWS))
 
 

time: 144 us -> 143 us (level)
  waiting for transfers between devices: 30 us -> 28.1 us
  Pallas kernels: 23.2 us -> 24.9 us
    ppermute x1, waiting for transfers between devices: 15.4 us -> 13.5 us  [shifted(): return lax.ppermute(block, loop, [(i, (i + 1) % size) for i in range(size)])]
  transfers between devices with their start and end apart: 11 -> 11, of which waited for: 10 -> 10; matrix products, arithmetic and copies ran while one was open for 0% -> 0% of each run, Pallas kernels for 5% -> 6%
where the time goes in v8:
time: 143 us; the launch traced here: 142 us
  blocking collectives  68.3 us (48%)
  waiting for transfers between devices  28.1 us (20%)
  Pallas kernels  24.9 us (17%)
  starting transfers between devices  15.6 us (11%)
  local copies, waits for them, and re-layouts  4.94 us (3%)
    all_to_all x4, blocking collectives, spread(): return lax.all_to_all(block, axes, 0, 0, tiled=True)  68.3 us
    pallas_call x1, Pallas kernels, solve_rows(): pl.pallas_call(functools.partial(kernel, scale), out_shape=jax.ShapeDtype...  15.2 us
    ppermute x1, waiting for transfers between devices, shifted(): return lax.ppermute(block, loop, [(i, (i + 1) % size) for i in range(size)])  13.5 us
    all_to_all x1, waiting for transfers between devices, spread(): return lax.all_to_all(block, axes, 0, 0, tiled=True)  11.3 us
    pallas_call x2, Pallas kernels, product(): pl.pallas_call(far_kernel if fetched else own_kernel, in_specs=[vmem if f...  8.48 us
    all_to_all x1, starting transfers between devices, spread(): return lax.all_to_all(block, axes, 0, 0, tiled=True)  6.99 us
    unnamed x4, local copies, waits for them, and re-layouts  4.61 us
    ppermute x8, starting transfers between devices, core_swap(): return lax.ppermute(block, 'c', [(0, 1), (1, 0)])  3.74 us
  transfers between devices with their start and end apart: 11, of which 10 were waited for; matrix products, arithmetic and copies ran while one was open for 0% of the time, Pallas kernels for 6%

profile of v8, /device:TPU:1, one launch (start us, length us, event | category | flops | bytes accessed | tf_op | source)
XLA Modules:
  0.0 142.5 jit_solution(11985333776624598556)
XLA Ops:
  0.0 2.1 %collective-permute-start.5 = (bf16[2048,256]{1,0:T(8,128)(2,1)}, bf16[2048,256]{1,0:T(8,128)(2,1)S(1)}, u32[]{:S(2)}, u32[]{:S(2)}) collective-permute-start(bf16[2048,256]{1,0:T(8,128)(2,1)} %sketch_ref.1), channel_id=1, source_target_pairs={{0,4},{4,8},{8,12},{12,16},{16,20},{20,24},{24,28},{28,32},{32,36}... | collective-permute-start | bytes 3145736 | tf_op jit(solution)/shard_map/ppermute | solution.py:142
  2.1 3.4 %copy-done = bf16[2048,2048]{1,0:T(8,128)(2,1)S(1)} copy-done((bf16[2048,2048]{1,0:T(8,128)(2,1)S(1)}, bf16[2048,2048]{1,0:T(8,128)(2,1)}, u32[]{:S(2)}) %copy-start) | copy-done | bytes 8388632
  5.5 1.2 copy-done.1
  6.7 6.1 %shard_map.28 = (bf16[2048,2048]{1,0:T(8,128)(2,1)S(1)}, f32[8,8,8,128]{3,2,1,0:T(8,128)S(1)}, f32[8,8,8,128]{3,2,1,0:T(8,128)S(1)}, f32[8,8,8,128]{3,2,1,0:T(8,...) custom-call(bf16[2048,2048]{1,0:T(8,128)(2,1)S(1)} %copy-done, ...), custom_call_target="tpu_custom_call" | custom-call | flops 2147483648 | bytes 8388608 | tf_op jit(solution)/shard_map/pallas_call | solution.py:204
  12.9 1.2 collective-permute-start
  14.2 0.4 collective-permute-start.2
  14.7 0.6 collective-permute-done.refs_4_
  15.6 0.4 collective-permute-done.2.refs_6_
  16.5 2.8 %collective-permute-start.4 = (f32[2,8,8,8,128]{4,3,2,1,0:T(8,128)S(1)}, f32[2,8,8,8,128]{4,3,2,1,0:T(8,128)S(1)}, u32[]{:S(2)}, u32[]{:S(2)}) collective-permute-start(f32[2,8,8,8,128]{4,3,2,1,0:T(8,128)S(1)} %get-tuple-element.35), channel_id=1, source_target_pairs={{0,6},{2,4},{4,2},{6,0},{1,7},{3,5},{5,3},{7,1},{8,14},{10,12},{12... | collective-permute-start | bytes 1572872 | tf_op jit(solution)/shard_map/ppermute | solution.py:236
  19.2 13.5 %collective-permute-done.5.sketch_ref = bf16[2048,256]{1,0:T(8,128)(2,1)S(1)} collective-permute-done((bf16[2048,256]{1,0:T(8,128)(2,1)}, bf16[2048,256]{1,0:T(8,128)(2,1)S(1)}, u32[]{:S(2)}, u32[]{:S(2)}) %collective-permute-start.5) | collective-permute-done | bytes 1048608 | tf_op jit(solution)/shard_map/ppermute | solution.py:142
  32.7 2.3 %shard_map.30 = (f32[8,8,8,128]{3,2,1,0:T(8,128)S(1)}, f32[8,8,8,128]{3,2,1,0:T(8,128)S(1)}, f32[8,8,8,128]{3,2,1,0:T(8,128)S(1)}, f32[8,8,8,128]{3,2,1,0:T(8,12...) custom-call(bf16[2048,2048]{1,0:T(8,128)(2,1)S(1)} %get-tuple-elemen, ...), custom_call_target="tpu_custom_call" | custom-call | flops 2147483648 | bytes 8388608 | tf_op jit(solution)/shard_map/pallas_call | solution.py:204
  35.0 1.3 collective-permute-start.6
  36.5 0.4 collective-permute-start.8
  37.0 0.5 collective-permute-done.6.refs_4_
  37.9 0.4 collective-permute-done.8.refs_6_
  38.8 25.8 %all_to_all.25 = f32[16,8,3,8,128]{4,3,2,1,0:T(8,128)S(1)} all-to-all(f32[16,8,3,8,128]{4,3,2,1,0:T(8,128)S(1)} %shard_map.31), channel_id=1, replica_groups=mesh['z'=8,'x'=4,'yl'=2,'yh'=2,'c'=2] {'x','yl','yh'}, dimensions={0} | all-to-all | bytes 3145728 | tf_op jit(solution)/shard_map/all_to_all | solution.py:150
  64.8 13.1 %all_to_all.26.parts_ref = f32[8,4,8,128]{3,2,1,0:T(8,128)S(1)} all-to-all(f32[8,4,8,128]{3,2,1,0:T(8,128)S(1)} %pad_maximum_fusion), channel_id=1, replica_groups=mesh['z'=8,'x'=4,'yl'=2,'yh'=2,'c'=2] {'z'}, dimensions={0} | all-to-all | bytes 262144 | tf_op jit(solution)/shard_map/all_to_all | solution.py:150
  77.9 0.9 shard_map.32
  78.8 7.0 %all-to-all-start.2 = ((f32[32,4,8,128]{3,2,1,0:T(8,128)}), f32[32,4,8,128]{3,2,1,0:T(8,128)S(1)}, u32[]{:S(2)}, u32[]{:S(2)}) async-start(f32[32,4,8,128]{3,2,1,0:T(8,128)} %shard_map.32), calls=%async_computation.2 | async-start | bytes 1048576 | tf_op jit(solution)/shard_map/all_to_all | solution.py:150
  85.8 11.3 %all-to-all-done.2.parts_ref = f32[32,4,8,128]{3,2,1,0:T(8,128)S(1)} async-done(((f32[32,4,8,128]{3,2,1,0:T(8,128)}), f32[32,4,8,128]{3,2,1,0:T(8,128)S(1)}, u32[]{:S(2)}, u32[]{:S(2)}) %all-to-all-start.2) | async-done | bytes 524320 | tf_op jit(solution)/shard_map/all_to_all | solution.py:150
  97.4 0.4 fusion
  97.8 11.7 %all_to_all.27.parts_ref = f32[8,8,640]{2,1,0:T(8,128)S(1)} all-to-all(f32[8,8,640]{2,1,0:T(8,128)S(1)} %broadcast_in_dim.2), channel_id=1, replica_groups=mesh['z'=8,'x'=4,'yl'=2,'yh'=2,'c'=2] {'z'}, dimensions={0} | all-to-all | bytes 327680 | tf_op jit(solution)/shard_map/all_to_all | solution.py:150
  109.7 17.6 %all_to_all.28.gram_ref = f32[32,8,640]{2,1,0:T(8,128)S(1)} all-to-all(f32[32,8,640]{2,1,0:T(8,128)S(1)} %shard_map.34), channel_id=1, replica_groups=mesh['z'=8,'x'=4,'yl'=2,'yh'=2,'c'=2] {'x','yl','yh','c'}, dimensions={0} | all-to-all | bytes 1310720 | tf_op jit(solution)/shard_map/all_to_all | solution.py:150
  127.2 15.2 %shard_map.35 = f32[8,512]{1,0:T(8,128)} custom-call(f32[32,8,640]{2,1,0:T(8,128)S(1)} %all_to_all.28.gram_ref, f32[8,512]{1,0:T(8,128)S(1)} %get-tuple-element.46.rows_ref), custom_call_target="tpu_custom_call" | custom-call | tf_op jit(solution)/shard_map/pallas_call | solution.py:125
  (29 shorter events, 2.7 us)
Async XLA Ops:
  0.0 32.7 %collective-permute-start.5 = (bf16[2048,256]{1,0:T(8,128)(2,1)}, bf16[2048,256]{1,0:T(8,128)(2,1)S(1)}, u32[]{:S(2)}, u32[]{:S(2)}) collective-permute-start(bf16[2048,256]{1,0:T(8,128)(2,1)} %sketch_ref.1), channel_id=1, source_target_pairs={{0,4},{4,8},{8,12},{12,16},{16,20},{20,24},{24,28},{28,32},{32,36}... | collective-permute-start | bytes 3145736 | tf_op jit(solution)/shard_map/ppermute | solution.py:142
  2.1 3.4 %copy-start = (bf16[2048,2048]{1,0:T(8,128)(2,1)S(1)}, bf16[2048,2048]{1,0:T(8,128)(2,1)}, u32[]{:S(2)}) copy-start(bf16[2048,2048]{1,0:T(8,128)(2,1)} %slab_ref.1) | copy-start | bytes 25165828
  5.5 1.2 copy-start.1
  12.9 2.4 %collective-permute-start = (f32[8,8,8,128]{3,2,1,0:T(8,128)S(1)}, f32[8,8,8,128]{3,2,1,0:T(8,128)S(1)}, u32[]{:S(2)}, u32[]{:S(2)}) collective-permute-start(f32[8,8,8,128]{3,2,1,0:T(8,128)S(1)} %get-tuple-element.30), channel_id=1, source_target_pairs={{0,1},{1,0},{2,3},{3,2},{4,5},{5,4},{6,7},{7,6},{8,9},{9,8},{10,11... | collective-permute-start | bytes 786440 | tf_op jit(solution)/shard_map/ppermute | solution.py:146
  14.1 1.5 %collective-permute-start.1 = (f32[8,8,8,128]{3,2,1,0:T(8,128)S(1)}, f32[8,8,8,128]{3,2,1,0:T(8,128)S(1)}, u32[]{:S(2)}, u32[]{:S(2)}) collective-permute-start(f32[8,8,8,128]{3,2,1,0:T(8,128)S(1)} %get-tuple-element.31), channel_id=1, source_target_pairs={{0,1},{1,0},{2,3},{3,2},{4,5},{5,4},{6,7},{7,6},{8,9},{9,8},{10,11... | collective-permute-start | bytes 786440 | tf_op jit(solution)/shard_map/ppermute | solution.py:146
  14.2 1.8 %collective-permute-start.2 = (f32[8,8,8,128]{3,2,1,0:T(8,128)S(1)}, f32[8,8,8,128]{3,2,1,0:T(8,128)S(1)}, u32[]{:S(2)}, u32[]{:S(2)}) collective-permute-start(f32[8,8,8,128]{3,2,1,0:T(8,128)S(1)} %get-tuple-element.32), channel_id=1, source_target_pairs={{0,1},{1,0},{2,3},{3,2},{4,5},{5,4},{6,7},{7,6},{8,9},{9,8},{10,11... | collective-permute-start | bytes 786440 | tf_op jit(solution)/shard_map/ppermute | solution.py:146
  14.6 1.8 %collective-permute-start.3 = (f32[8,8,8,128]{3,2,1,0:T(8,128)S(1)}, f32[8,8,8,128]{3,2,1,0:T(8,128)S(1)}, u32[]{:S(2)}, u32[]{:S(2)}) collective-permute-start(f32[8,8,8,128]{3,2,1,0:T(8,128)S(1)} %get-tuple-element.33), channel_id=1, source_target_pairs={{0,1},{1,0},{2,3},{3,2},{4,5},{5,4},{6,7},{7,6},{8,9},{9,8},{10,11... | collective-permute-start | bytes 786440 | tf_op jit(solution)/shard_map/ppermute | solution.py:146
  16.5 20.5 %collective-permute-start.4 = (f32[2,8,8,8,128]{4,3,2,1,0:T(8,128)S(1)}, f32[2,8,8,8,128]{4,3,2,1,0:T(8,128)S(1)}, u32[]{:S(2)}, u32[]{:S(2)}) collective-permute-start(f32[2,8,8,8,128]{4,3,2,1,0:T(8,128)S(1)} %get-tuple-element.35), channel_id=1, source_target_pairs={{0,6},{2,4},{4,2},{6,0},{1,7},{3,5},{5,3},{7,1},{8,14},{10,12},{12... | collective-permute-start | bytes 1572872 | tf_op jit(solution)/shard_map/ppermute | solution.py:236
  35.0 2.5 %collective-permute-start.6 = (f32[8,8,8,128]{3,2,1,0:T(8,128)S(1)}, f32[8,8,8,128]{3,2,1,0:T(8,128)S(1)}, u32[]{:S(2)}, u32[]{:S(2)}) collective-permute-start(f32[8,8,8,128]{3,2,1,0:T(8,128)S(1)} %get-tuple-element.41), channel_id=1, source_target_pairs={{0,1},{1,0},{2,3},{3,2},{4,5},{5,4},{6,7},{7,6},{8,9},{9,8},{10,11... | collective-permute-start | bytes 786440 | tf_op jit(solution)/shard_map/ppermute | solution.py:146
  36.4 1.5 %collective-permute-start.7 = (f32[8,8,8,128]{3,2,1,0:T(8,128)S(1)}, f32[8,8,8,128]{3,2,1,0:T(8,128)S(1)}, u32[]{:S(2)}, u32[]{:S(2)}) collective-permute-start(f32[8,8,8,128]{3,2,1,0:T(8,128)S(1)} %get-tuple-element.42), channel_id=1, source_target_pairs={{0,1},{1,0},{2,3},{3,2},{4,5},{5,4},{6,7},{7,6},{8,9},{9,8},{10,11... | collective-permute-start | bytes 786440 | tf_op jit(solution)/shard_map/ppermute | solution.py:146
  36.5 1.8 %collective-permute-start.8 = (f32[8,8,8,128]{3,2,1,0:T(8,128)S(1)}, f32[8,8,8,128]{3,2,1,0:T(8,128)S(1)}, u32[]{:S(2)}, u32[]{:S(2)}) collective-permute-start(f32[8,8,8,128]{3,2,1,0:T(8,128)S(1)} %get-tuple-element.43), channel_id=1, source_target_pairs={{0,1},{1,0},{2,3},{3,2},{4,5},{5,4},{6,7},{7,6},{8,9},{9,8},{10,11... | collective-permute-start | bytes 786440 | tf_op jit(solution)/shard_map/ppermute | solution.py:146
  36.9 1.8 %collective-permute-start.9 = (f32[8,8,8,128]{3,2,1,0:T(8,128)S(1)}, f32[8,8,8,128]{3,2,1,0:T(8,128)S(1)}, u32[]{:S(2)}, u32[]{:S(2)}) collective-permute-start(f32[8,8,8,128]{3,2,1,0:T(8,128)S(1)} %get-tuple-element.44), channel_id=1, source_target_pairs={{0,1},{1,0},{2,3},{3,2},{4,5},{5,4},{6,7},{7,6},{8,9},{9,8},{10,11... | collective-permute-start | bytes 786440 | tf_op jit(solution)/shard_map/ppermute | solution.py:146
  78.8 18.3 %all-to-all-start.2 = ((f32[32,4,8,128]{3,2,1,0:T(8,128)}), f32[32,4,8,128]{3,2,1,0:T(8,128)S(1)}, u32[]{:S(2)}, u32[]{:S(2)}) async-start(f32[32,4,8,128]{3,2,1,0:T(8,128)} %shard_map.32), calls=%async_computation.2 | async-start | bytes 1048576 | tf_op jit(solution)/shard_map/all_to_all | solution.py:150

commit v9 on v8

--- a/solution.py
+++ b/solution.py
@@ -181,7 +181,7 @@
     for z in range(depth):
         fetch(z).start()
 
-    @pl.loop(0, depth, unroll=True)
+    @pl.loop(0, depth)
     def _(z):
         fetch(z).wait()
         store_halves(z, local_ref, sketch_ref, out_refs)

time: 143 us -> 143 us (level)
  Pallas kernels: 24.9 us -> 22.9 us
  waiting for transfers between devices: 28.1 us -> 30 us
    ppermute x1, waiting for transfers between devices: 13.5 us -> 15.4 us  [shifted(): return lax.ppermute(block, loop, [(i, (i + 1) % size) for i in range(size)])]
    pallas_call x2, Pallas kernels: 8.48 us -> 6.5 us  [product(): pl.pallas_call(far_kernel if fetched else own_kernel, in_specs=[vmem if f...]
  transfers between devices with their start and end apart: 11 -> 11, of which waited for: 10 -> 10; matrix products, arithmetic and copies ran while one was open for 0% -> 0% of each run, Pallas kernels for 6% -> 5%
where the time goes in v9:
time: 143 us; the launch traced here: 142 us
  blocking collectives  68.3 us (48%)
  waiting for transfers between devices  30 us (21%)
  Pallas kernels  22.9 us (16%)
  starting transfers between devices  15.6 us (11%)
  local copies, waits for them, and re-layouts  4.94 us (3%)
    all_to_all x4, blocking collectives, spread(): return lax.all_to_all(block, axes, 0, 0, tiled=True)  68.3 us
    ppermute x1, waiting for transfers between devices, shifted(): return lax.ppermute(block, loop, [(i, (i + 1) % size) for i in range(size)])  15.4 us
    pallas_call x1, Pallas kernels, solve_rows(): pl.pallas_call(functools.partial(kernel, scale), out_shape=jax.ShapeDtype...  15.2 us
    all_to_all x1, waiting for transfers between devices, spread(): return lax.all_to_all(block, axes, 0, 0, tiled=True)  11.3 us
    all_to_all x1, starting transfers between devices, spread(): return lax.all_to_all(block, axes, 0, 0, tiled=True)  6.99 us
    pallas_call x2, Pallas kernels, product(): pl.pallas_call(far_kernel if fetched else own_kernel, in_specs=[vmem if f...  6.5 us
    unnamed x4, local copies, waits for them, and re-layouts  4.61 us
    ppermute x8, starting transfers between devices, core_swap(): return lax.ppermute(block, 'c', [(0, 1), (1, 0)])  3.74 us
  transfers between devices with their start and end apart: 11, of which 10 were waited for; matrix products, arithmetic and copies ran while one was open for 0% of the time, Pallas kernels for 5%

profile of v9, /device:TPU:1, one launch (start us, length us, event | category | flops | bytes accessed | tf_op | source)
XLA Modules:
  0.0 142.5 jit_solution(12224209341366883194)
XLA Ops:
  0.0 2.1 %collective-permute-start.5 = (bf16[2048,256]{1,0:T(8,128)(2,1)}, bf16[2048,256]{1,0:T(8,128)(2,1)S(1)}, u32[]{:S(2)}, u32[]{:S(2)}) collective-permute-start(bf16[2048,256]{1,0:T(8,128)(2,1)} %sketch_ref.1), channel_id=1, source_target_pairs={{0,4},{4,8},{8,12},{12,16},{16,20},{20,24},{24,28},{28,32},{32,36}... | collective-permute-start | bytes 3145736 | tf_op jit(solution)/shard_map/ppermute | solution.py:142
  2.1 3.4 %copy-done = bf16[2048,2048]{1,0:T(8,128)(2,1)S(1)} copy-done((bf16[2048,2048]{1,0:T(8,128)(2,1)S(1)}, bf16[2048,2048]{1,0:T(8,128)(2,1)}, u32[]{:S(2)}) %copy-start) | copy-done | bytes 8388632
  5.5 1.2 copy-done.1
  6.7 4.2 %shard_map.28 = (bf16[2048,2048]{1,0:T(8,128)(2,1)S(1)}, f32[8,8,8,128]{3,2,1,0:T(8,128)S(1)}, f32[8,8,8,128]{3,2,1,0:T(8,128)S(1)}, f32[8,8,8,128]{3,2,1,0:T(8,...) custom-call(bf16[2048,2048]{1,0:T(8,128)(2,1)S(1)} %copy-done, ...), custom_call_target="tpu_custom_call" | custom-call | flops 2147483648 | bytes 8388608 | tf_op jit(solution)/shard_map/pallas_call | solution.py:204
  10.9 1.2 collective-permute-start
  12.2 0.4 collective-permute-start.2
  12.7 0.6 collective-permute-done.refs_4_
  13.7 0.4 collective-permute-done.2.refs_6_
  14.5 2.8 %collective-permute-start.4 = (f32[2,8,8,8,128]{4,3,2,1,0:T(8,128)S(1)}, f32[2,8,8,8,128]{4,3,2,1,0:T(8,128)S(1)}, u32[]{:S(2)}, u32[]{:S(2)}) collective-permute-start(f32[2,8,8,8,128]{4,3,2,1,0:T(8,128)S(1)} %get-tuple-element.35), channel_id=1, source_target_pairs={{0,6},{2,4},{4,2},{6,0},{1,7},{3,5},{5,3},{7,1},{8,14},{10,12},{12... | collective-permute-start | bytes 1572872 | tf_op jit(solution)/shard_map/ppermute | solution.py:236
  17.3 15.4 %collective-permute-done.5.sketch_ref = bf16[2048,256]{1,0:T(8,128)(2,1)S(1)} collective-permute-done((bf16[2048,256]{1,0:T(8,128)(2,1)}, bf16[2048,256]{1,0:T(8,128)(2,1)S(1)}, u32[]{:S(2)}, u32[]{:S(2)}) %collective-permute-start.5) | collective-permute-done | bytes 1048608 | tf_op jit(solution)/shard_map/ppermute | solution.py:142
  32.7 2.3 %shard_map.30 = (f32[8,8,8,128]{3,2,1,0:T(8,128)S(1)}, f32[8,8,8,128]{3,2,1,0:T(8,128)S(1)}, f32[8,8,8,128]{3,2,1,0:T(8,128)S(1)}, f32[8,8,8,128]{3,2,1,0:T(8,12...) custom-call(bf16[2048,2048]{1,0:T(8,128)(2,1)S(1)} %get-tuple-elemen, ...), custom_call_target="tpu_custom_call" | custom-call | flops 2147483648 | bytes 8388608 | tf_op jit(solution)/shard_map/pallas_call | solution.py:204
  35.0 1.3 collective-permute-start.6
  36.5 0.4 collective-permute-start.8
  37.0 0.5 collective-permute-done.6.refs_4_
  37.9 0.4 collective-permute-done.8.refs_6_
  38.8 25.8 %all_to_all.25 = f32[16,8,3,8,128]{4,3,2,1,0:T(8,128)S(1)} all-to-all(f32[16,8,3,8,128]{4,3,2,1,0:T(8,128)S(1)} %shard_map.31), channel_id=1, replica_groups=mesh['z'=8,'x'=4,'yl'=2,'yh'=2,'c'=2] {'x','yl','yh'}, dimensions={0} | all-to-all | bytes 3145728 | tf_op jit(solution)/shard_map/all_to_all | solution.py:150
  64.8 13.1 %all_to_all.26.parts_ref = f32[8,4,8,128]{3,2,1,0:T(8,128)S(1)} all-to-all(f32[8,4,8,128]{3,2,1,0:T(8,128)S(1)} %pad_maximum_fusion), channel_id=1, replica_groups=mesh['z'=8,'x'=4,'yl'=2,'yh'=2,'c'=2] {'z'}, dimensions={0} | all-to-all | bytes 262144 | tf_op jit(solution)/shard_map/all_to_all | solution.py:150
  77.9 0.9 shard_map.32
  78.8 7.0 %all-to-all-start.2 = ((f32[32,4,8,128]{3,2,1,0:T(8,128)}), f32[32,4,8,128]{3,2,1,0:T(8,128)S(1)}, u32[]{:S(2)}, u32[]{:S(2)}) async-start(f32[32,4,8,128]{3,2,1,0:T(8,128)} %shard_map.32), calls=%async_computation.2 | async-start | bytes 1048576 | tf_op jit(solution)/shard_map/all_to_all | solution.py:150
  85.8 11.3 %all-to-all-done.2.parts_ref = f32[32,4,8,128]{3,2,1,0:T(8,128)S(1)} async-done(((f32[32,4,8,128]{3,2,1,0:T(8,128)}), f32[32,4,8,128]{3,2,1,0:T(8,128)S(1)}, u32[]{:S(2)}, u32[]{:S(2)}) %all-to-all-start.2) | async-done | bytes 524320 | tf_op jit(solution)/shard_map/all_to_all | solution.py:150
  97.4 0.4 fusion
  97.8 11.7 %all_to_all.27.parts_ref = f32[8,8,640]{2,1,0:T(8,128)S(1)} all-to-all(f32[8,8,640]{2,1,0:T(8,128)S(1)} %broadcast_in_dim.2), channel_id=1, replica_groups=mesh['z'=8,'x'=4,'yl'=2,'yh'=2,'c'=2] {'z'}, dimensions={0} | all-to-all | bytes 327680 | tf_op jit(solution)/shard_map/all_to_all | solution.py:150
  109.6 17.6 %all_to_all.28.gram_ref = f32[32,8,640]{2,1,0:T(8,128)S(1)} all-to-all(f32[32,8,640]{2,1,0:T(8,128)S(1)} %shard_map.34), channel_id=1, replica_groups=mesh['z'=8,'x'=4,'yl'=2,'yh'=2,'c'=2] {'x','yl','yh','c'}, dimensions={0} | all-to-all | bytes 1310720 | tf_op jit(solution)/shard_map/all_to_all | solution.py:150
  127.2 15.2 %shard_map.35 = f32[8,512]{1,0:T(8,128)} custom-call(f32[32,8,640]{2,1,0:T(8,128)S(1)} %all_to_all.28.gram_ref, f32[8,512]{1,0:T(8,128)S(1)} %get-tuple-element.46.rows_ref), custom_call_target="tpu_custom_call" | custom-call | tf_op jit(solution)/shard_map/pallas_call | solution.py:125
  (29 shorter events, 2.7 us)
Async XLA Ops:
  0.0 32.7 %collective-permute-start.5 = (bf16[2048,256]{1,0:T(8,128)(2,1)}, bf16[2048,256]{1,0:T(8,128)(2,1)S(1)}, u32[]{:S(2)}, u32[]{:S(2)}) collective-permute-start(bf16[2048,256]{1,0:T(8,128)(2,1)} %sketch_ref.1), channel_id=1, source_target_pairs={{0,4},{4,8},{8,12},{12,16},{16,20},{20,24},{24,28},{28,32},{32,36}... | collective-permute-start | bytes 3145736 | tf_op jit(solution)/shard_map/ppermute | solution.py:142
  2.1 3.4 %copy-start = (bf16[2048,2048]{1,0:T(8,128)(2,1)S(1)}, bf16[2048,2048]{1,0:T(8,128)(2,1)}, u32[]{:S(2)}) copy-start(bf16[2048,2048]{1,0:T(8,128)(2,1)} %slab_ref.1) | copy-start | bytes 25165828
  5.5 1.2 copy-start.1
  10.9 2.4 %collective-permute-start = (f32[8,8,8,128]{3,2,1,0:T(8,128)S(1)}, f32[8,8,8,128]{3,2,1,0:T(8,128)S(1)}, u32[]{:S(2)}, u32[]{:S(2)}) collective-permute-start(f32[8,8,8,128]{3,2,1,0:T(8,128)S(1)} %get-tuple-element.30), channel_id=1, source_target_pairs={{0,1},{1,0},{2,3},{3,2},{4,5},{5,4},{6,7},{7,6},{8,9},{9,8},{10,11... | collective-permute-start | bytes 786440 | tf_op jit(solution)/shard_map/ppermute | solution.py:146
  12.1 1.5 %collective-permute-start.1 = (f32[8,8,8,128]{3,2,1,0:T(8,128)S(1)}, f32[8,8,8,128]{3,2,1,0:T(8,128)S(1)}, u32[]{:S(2)}, u32[]{:S(2)}) collective-permute-start(f32[8,8,8,128]{3,2,1,0:T(8,128)S(1)} %get-tuple-element.31), channel_id=1, source_target_pairs={{0,1},{1,0},{2,3},{3,2},{4,5},{5,4},{6,7},{7,6},{8,9},{9,8},{10,11... | collective-permute-start | bytes 786440 | tf_op jit(solution)/shard_map/ppermute | solution.py:146
  12.2 1.8 %collective-permute-start.2 = (f32[8,8,8,128]{3,2,1,0:T(8,128)S(1)}, f32[8,8,8,128]{3,2,1,0:T(8,128)S(1)}, u32[]{:S(2)}, u32[]{:S(2)}) collective-permute-start(f32[8,8,8,128]{3,2,1,0:T(8,128)S(1)} %get-tuple-element.32), channel_id=1, source_target_pairs={{0,1},{1,0},{2,3},{3,2},{4,5},{5,4},{6,7},{7,6},{8,9},{9,8},{10,11... | collective-permute-start | bytes 786440 | tf_op jit(solution)/shard_map/ppermute | solution.py:146
  12.6 1.8 %collective-permute-start.3 = (f32[8,8,8,128]{3,2,1,0:T(8,128)S(1)}, f32[8,8,8,128]{3,2,1,0:T(8,128)S(1)}, u32[]{:S(2)}, u32[]{:S(2)}) collective-permute-start(f32[8,8,8,128]{3,2,1,0:T(8,128)S(1)} %get-tuple-element.33), channel_id=1, source_target_pairs={{0,1},{1,0},{2,3},{3,2},{4,5},{5,4},{6,7},{7,6},{8,9},{9,8},{10,11... | collective-permute-start | bytes 786440 | tf_op jit(solution)/shard_map/ppermute | solution.py:146
  14.5 22.5 %collective-permute-start.4 = (f32[2,8,8,8,128]{4,3,2,1,0:T(8,128)S(1)}, f32[2,8,8,8,128]{4,3,2,1,0:T(8,128)S(1)}, u32[]{:S(2)}, u32[]{:S(2)}) collective-permute-start(f32[2,8,8,8,128]{4,3,2,1,0:T(8,128)S(1)} %get-tuple-element.35), channel_id=1, source_target_pairs={{0,6},{2,4},{4,2},{6,0},{1,7},{3,5},{5,3},{7,1},{8,14},{10,12},{12... | collective-permute-start | bytes 1572872 | tf_op jit(solution)/shard_map/ppermute | solution.py:236
  35.0 2.5 %collective-permute-start.6 = (f32[8,8,8,128]{3,2,1,0:T(8,128)S(1)}, f32[8,8,8,128]{3,2,1,0:T(8,128)S(1)}, u32[]{:S(2)}, u32[]{:S(2)}) collective-permute-start(f32[8,8,8,128]{3,2,1,0:T(8,128)S(1)} %get-tuple-element.41), channel_id=1, source_target_pairs={{0,1},{1,0},{2,3},{3,2},{4,5},{5,4},{6,7},{7,6},{8,9},{9,8},{10,11... | collective-permute-start | bytes 786440 | tf_op jit(solution)/shard_map/ppermute | solution.py:146
  36.4 1.5 %collective-permute-start.7 = (f32[8,8,8,128]{3,2,1,0:T(8,128)S(1)}, f32[8,8,8,128]{3,2,1,0:T(8,128)S(1)}, u32[]{:S(2)}, u32[]{:S(2)}) collective-permute-start(f32[8,8,8,128]{3,2,1,0:T(8,128)S(1)} %get-tuple-element.42), channel_id=1, source_target_pairs={{0,1},{1,0},{2,3},{3,2},{4,5},{5,4},{6,7},{7,6},{8,9},{9,8},{10,11... | collective-permute-start | bytes 786440 | tf_op jit(solution)/shard_map/ppermute | solution.py:146
  36.5 1.8 %collective-permute-start.8 = (f32[8,8,8,128]{3,2,1,0:T(8,128)S(1)}, f32[8,8,8,128]{3,2,1,0:T(8,128)S(1)}, u32[]{:S(2)}, u32[]{:S(2)}) collective-permute-start(f32[8,8,8,128]{3,2,1,0:T(8,128)S(1)} %get-tuple-element.43), channel_id=1, source_target_pairs={{0,1},{1,0},{2,3},{3,2},{4,5},{5,4},{6,7},{7,6},{8,9},{9,8},{10,11... | collective-permute-start | bytes 786440 | tf_op jit(solution)/shard_map/ppermute | solution.py:146
  36.9 1.8 %collective-permute-start.9 = (f32[8,8,8,128]{3,2,1,0:T(8,128)S(1)}, f32[8,8,8,128]{3,2,1,0:T(8,128)S(1)}, u32[]{:S(2)}, u32[]{:S(2)}) collective-permute-start(f32[8,8,8,128]{3,2,1,0:T(8,128)S(1)} %get-tuple-element.44), channel_id=1, source_target_pairs={{0,1},{1,0},{2,3},{3,2},{4,5},{5,4},{6,7},{7,6},{8,9},{9,8},{10,11... | collective-permute-start | bytes 786440 | tf_op jit(solution)/shard_map/ppermute | solution.py:146
  78.8 18.3 %all-to-all-start.2 = ((f32[32,4,8,128]{3,2,1,0:T(8,128)}), f32[32,4,8,128]{3,2,1,0:T(8,128)S(1)}, u32[]{:S(2)}, u32[]{:S(2)}) async-start(f32[32,4,8,128]{3,2,1,0:T(8,128)} %shard_map.32), calls=%async_computation.2 | async-start | bytes 1048576 | tf_op jit(solution)/shard_map/all_to_all | solution.py:150
